TPU v7x, 512 devices: a whole 4x4x16 slice. The times are simulated.
512 devices in a mesh: chan: 16 (over z_hi, y, core), tm: 32 (over x, z_lo).
Axes of the slice: x: 4, y: 4, z: 16 (z_hi: 2, z_lo: 8; z = z_hi * 8 + z_lo), core: 2. Of those that a mesh axis runs over, the one named last changes fastest.
Arguments:
- signal: bfloat16 [4096, 131072], P('chan', 'tm'), may hold values from -6 to 6
- spatial: float32 [4096, 64], P('chan'), may hold values from -0.09375 to 0.09375
- temporal: float32 [64, 128], replicated, may hold values from -0.5 to 0.5
- activations: float32 [64, 131072], P(None, 'tm'), may hold values from 0 to 1
- threshold: float32 [64], replicated, may hold values from 0.05 to 0.5
- step_size: float32 [1], replicated, may hold values from 0.06 to 0.12
Outputs:
- refined: float32 [64, 131072], P(None, 'tm')
All inputs are finite; a program needn't handle non-finite values.
Results may differ from a plain program's by a relative error of at most 0.0003.
Values sent between devices are 32-bit elements; how exact they have to be, the bound alone decides.
No kernel may reach another device: no remote copies, remote signals or barrier semaphores. Data moves between devices by JAX's collectives and lax.ppermute only.
A program may use at most 64 MiB of HBM per device.

v0:
```python
import jax
import jax.numpy as jnp
from jax import lax
from jax.sharding import PartitionSpec as P

ITERS = 2


def passed_along(block, axis, distance):
    devices = range(lax.axis_size(axis))
    route = [(i - distance, i) for i in devices if i - distance in devices]
    return lax.ppermute(block, axis, route)


def make_bands(temporal):
    length = temporal.shape[1]
    positions = jnp.arange(length, dtype=jnp.int32)
    offsets = positions[None, :] - positions[:, None]
    lookup_table = temporal[:, offsets % length]
    current_band = jnp.where(offsets[None] >= 0, lookup_table, 0.0)
    carry_band = jnp.where(offsets[None] < 0, lookup_table, 0.0)
    return (current_band, carry_band)


def conv_blocks(field, left_rim, current_band, carry_band):
    atoms, width = field.shape
    length = current_band.shape[1]
    blocks = field.reshape(atoms, width // length, length)
    before = jnp.concatenate([left_rim[:, None, :], blocks[:, :-1]], axis=1)
    result = jnp.einsum("kja,kab->kjb", blocks, current_band, precision=lax.Precision.HIGHEST)
    result = result + jnp.einsum(
        "kja,kab->kjb", before, carry_band, precision=lax.Precision.HIGHEST
    )
    return result.reshape(atoms, width)


def corr_blocks(field, right_rim, current_band, carry_band):
    atoms, width = field.shape
    length = current_band.shape[1]
    blocks = field.reshape(atoms, width // length, length)
    after = jnp.concatenate([blocks[:, 1:], right_rim[:, None, :]], axis=1)
    result = jnp.einsum("kjb,kab->kja", blocks, current_band, precision=lax.Precision.HIGHEST)
    result = result + jnp.einsum("kjb,kab->kja", after, carry_band, precision=lax.Precision.HIGHEST)
    return result.reshape(atoms, width)


def per_device(signal, spatial, temporal, activations, threshold, step_size):
    current_band, carry_band = make_bands(temporal)
    length = temporal.shape[1]
    rate = step_size[0]
    shrink = threshold[:, None]
    gram_matrix, cross_terms = lax.psum(
        (
            jnp.dot(
                spatial.T,
                spatial,
                precision=lax.Precision.HIGHEST,
                preferred_element_type=jnp.float32,
            ),
            jnp.dot(
                spatial.T,
                signal.astype(jnp.float32),
                precision=lax.Precision.HIGHEST,
                preferred_element_type=jnp.float32,
            ),
        ),
        "chan",
    )
    point = activations
    previous = activations
    inertia = 1.0
    for iteration in range(ITERS):
        left_rim = passed_along(point[:, -length:], "tm", 1)
        rebuilt = conv_blocks(point, left_rim, current_band, carry_band)
        projected = (
            jnp.dot(
                gram_matrix,
                rebuilt,
                precision=lax.Precision.HIGHEST,
                preferred_element_type=jnp.float32,
            )
            - cross_terms
        )
        next_rim = passed_along(projected[:, :length], "tm", -1)
        gradient = corr_blocks(projected, next_rim, current_band, carry_band)
        update = jnp.maximum(point - rate * (gradient + shrink), 0.0)
        inertia_next = (1.0 + (1.0 + 4.0 * inertia * inertia) ** 0.5) / 2.0
        point = update + (inertia - 1.0) / inertia_next * (update - previous)
        previous = update
        inertia = inertia_next
    return previous


def solution(mesh):
    in_specs = (P("chan", "tm"), P("chan", None), P(), P(None, "tm"), P(), P())
    out_specs = P(None, "tm")
    return jax.shard_map(
        per_device, mesh=mesh, in_specs=in_specs, out_specs=out_specs, check_vma=False
    )
```

profile of v0, /device:TPU:31, one launch (start us, length us, event | category | flops | bytes accessed | tf_op | source)
XLA Modules:
  0.0 350.8 jit_solution(16710543651708254266)
XLA Ops:
  6.5 0.0 copy-start
  6.5 0.0 copy-start.4
  6.5 0.0 copy-start.5
  6.5 0.0 all-reduce.2.cloned.1.call-start
  6.5 0.9 slice.24
  7.5 3.5 %collective-permute-start = (f32[64,128]{1,0:T(8,128)S(1)}, f32[64,128]{1,0:T(8,128)S(1)}, u32[]{:S(2)}, u32[]{:S(2)}) collective-permute-start(f32[64,128]{1,0:T(8,128)S(1)} %slice.24), channel_id=1, source_target_pairs={{0,1},{1,2},{2,3},{3,4},{4,5},{5,6},{6,7},{7,8},{8,9},{9,10},{10,1... | collective-permute-start | bytes 98312 | tf_op jit(solution)/shard_map/ppermute | solution.py:12
  11.0 0.0 copy-done
  11.0 3.0 fusion.98
  14.0 0.0 all-reduce.2.cloned.1.call-update
  14.0 0.0 copy-done.4
  14.1 0.2 fusion.97
  14.3 0.1 fusion.79
  14.3 0.0 copy-done.5
  14.3 0.1 copy.12
  14.4 54.8 %gather_fusion = f32[16384,64]{1,0:T(8,128)} fusion(f32[64,128]{0,1:T(8,128)S(1)} %copy.12, s32[16384]{0:T(1024)S(1)} %fusion.79), kind=kCustom, calls=%fused_computation | custom fusion | bytes 8454144 | tf_op jit(solution)/shard_map/gather | solution.py:19
  69.3 7.4 %copy.13 = f32[128,128,64]{1,0,2:T(8,128)} copy(f32[128,128,64]{2,1,0:T(8,128)} %bitcast.94) | data formatting | bytes 8388608 | tf_op jit(solution)/shard_map/gather | solution.py:19
  76.6 1.4 copy.17
  78.1 6.4 %fusion.40 = f32[64,32,128]{2,1,0:T(8,128)} fusion(f32[64,32,128]{2,1,0:T(8,128)S(1)} %bitcast.96, f32[128,128,64]{1,0,2:T(8,128)} %copy.13, pred[128,128]{1,0:T(8,128)(4,1)S(1)} %fusion.83), kind=kOutput, calls=%fused_computation.43 | convolution fusion | flops 403701760 | bytes 6307840 | tf_op jit(solution)/shard_map/kja,kab->kjb/dot_general | solution.py:30
  85.1 122.8 %psum.14 = f32[64,64]{1,0:T(8,128)S(1)} all-reduce(f32[64,64]{1,0:T(8,128)S(1)} %fusion.97), channel_id=1, replica_groups=mesh['chan'=16,'tm'=32] {'chan'}, use_global_device_ids=true, to_apply=%region_0.1 | all-reduce | flops 4096 | bytes 32768 | tf_op jit(solution)/shard_map/psum | solution.py:52
  207.9 0.0 collective-permute-done
  207.9 6.4 %fusion.43 = f32[64,32,128]{2,1,0:T(8,128)} fusion(f32[64,32,128]{2,1,0:T(8,128)} %fusion.40, f32[128,128,64]{1,0,2:T(8,128)} %copy.13, pred[128,128]{1,0:T(8,128)(4,1)S(1)} %fusion.82, f32[64,31,128]{2,1,0:T(8,128)S(1)} %bitcast.97, f32[64,1,128]{2,1,0:T(1,128)S(1)} %bitcast.111), kind=kOutput, calls=%fused_computation.44 | convolution fusion | flops 404226048 | bytes 7356416 | tf_op jit(solution)/shard_map/kja,kab->kjb/dot_general | solution.py:31
  214.3 62.5 %all-reduce.2.cloned.1.call-done = f32[64,4096]{1,0:T(8,128)} async-done(((f32[64,4096]{1,0:T(8,128)}), f32[64,4096]{1,0:T(8,128)}) %all-reduce.2.cloned.1.call-update) | async-done | bytes 1048592 | tf_op jit(solution)/shard_map/psum | solution.py:52
  276.8 0.0 copy-start.1
  276.8 3.3 convolution_subtract_fusion.1
  280.1 0.2 copy.19
  280.3 10.9 %collective-permute-start.1 = (f32[64,128]{1,0:T(8,128)S(1)}, f32[64,128]{1,0:T(8,128)S(1)}, u32[]{:S(2)}, u32[]{:S(2)}) collective-permute-start(f32[64,128]{1,0:T(8,128)S(1)} %slice.36), channel_id=1, source_target_pairs={{1,0},{2,1},{3,2},{4,3},{5,4},{6,5},{7,6},{8,7},{9,8},{10,9},{11,1... | collective-permute-start | bytes 98312 | tf_op jit(solution)/shard_map/ppermute | solution.py:12
  291.2 0.0 copy-done.1
  291.2 6.6 %fusion.12 = f32[64,32,128]{2,1,0:T(8,128)S(1)} fusion(f32[64,32,128]{2,1,0:T(8,128)S(1)} %bitcast.102, f32[128,128,64]{1,0,2:T(8,128)S(1)} %copy-done.1, pred[128,128]{1,0:T(8,128)(4,1)S(1)} %fusion.83), kind=kOutput, calls=%fused_computation.15 | convolution fusion | flops 403701760 | bytes 6307840 | tf_op jit(solution)/shard_map/kjb,kab->kja/dot_general | solution.py:42
  297.8 0.1 slice.35
  297.9 0.0 copy-start.2
  297.9 0.0 copy-start.6
  297.9 0.0 collective-permute-done.1
  298.0 6.7 %fusion.46 = f32[64,32,128]{2,1,0:T(8,128)S(1)} fusion(f32[64,32,128]{2,1,0:T(8,128)S(1)} %fusion.12, f32[128,128,64]{1,0,2:T(8,128)S(1)} %copy-done.1, pred[128,128]{1,0:T(8,128)(4,1)S(1)} %fusion.82, f32[64,1,128]{2,1,0:T(1,128)S(1)} %bitcast.113, f32[64,31,128]{2,1,0:T(8,128)S(1)} %slice.35), kind=kOutput, calls=%fused_computation.45 | convolution fusion | flops 404226048 | bytes 7356416 | tf_op jit(solution)/shard_map/kjb,kab->kja/dot_general | solution.py:43
  304.6 0.0 copy-done.2
  304.6 0.0 copy-done.6
  304.6 0.8 multiply_add_fusion
  305.5 0.2 copy.21
  305.7 2.1 collective-permute-start.2
  307.8 3.7 %fusion.10 = f32[64,32,128]{2,1,0:T(8,128)S(1)} fusion(f32[64,32,128]{2,1,0:T(8,128)S(1)} %bitcast.98, f32[128,128,64]{1,0,2:T(8,128)S(1)} %copy-done.1, pred[128,128]{1,0:T(8,128)(4,1)S(1)} %fusion.83), kind=kOutput, calls=%fused_computation.13 | convolution fusion | flops 403701760 | bytes 6307840 | tf_op jit(solution)/shard_map/kja,kab->kjb/dot_general | solution.py:30
  311.5 0.0 copy-start.3
  311.5 6.3 %collective-permute-done.2 = f32[64,128]{1,0:T(8,128)S(1)} collective-permute-done((f32[64,128]{1,0:T(8,128)S(1)}, f32[64,128]{1,0:T(8,128)S(1)}, u32[]{:S(2)}, u32[]{:S(2)}) %collective-permute-start.2) | collective-permute-done | bytes 32800 | tf_op jit(solution)/shard_map/ppermute | solution.py:12
  317.9 3.8 %fusion.49 = f32[64,32,128]{2,1,0:T(8,128)S(1)} fusion(f32[64,32,128]{2,1,0:T(8,128)S(1)} %fusion.10, f32[128,128,64]{1,0,2:T(8,128)S(1)} %copy-done.1, pred[128,128]{1,0:T(8,128)(4,1)S(1)} %fusion.82, f32[64,31,128]{2,1,0:T(8,128)S(1)} %bitcast.99, f32[64,1,128]{2,1,0:T(1,128)S(1)} %bitcast.114), kind=kOutput, calls=%fused_computation.46 | convolution fusion | flops 404226048 | bytes 7356416 | tf_op jit(solution)/shard_map/kja,kab->kjb/dot_general | solution.py:31
  321.7 0.0 copy-done.3
  321.7 1.6 convolution_subtract_fusion
  323.3 0.2 copy.23
  323.5 4.8 %collective-permute-start.3 = (f32[64,128]{1,0:T(8,128)S(1)}, f32[64,128]{1,0:T(8,128)S(1)}, u32[]{:S(2)}, u32[]{:S(2)}) collective-permute-start(f32[64,128]{1,0:T(8,128)S(1)} %slice.40), channel_id=1, source_target_pairs={{1,0},{2,1},{3,2},{4,3},{5,4},{6,5},{7,6},{8,7},{9,8},{10,9},{11,1... | collective-permute-start | bytes 98312 | tf_op jit(solution)/shard_map/ppermute | solution.py:12
  328.3 6.6 %fusion.8 = f32[64,32,128]{2,1,0:T(8,128)S(1)} fusion(f32[64,32,128]{2,1,0:T(8,128)S(1)} %bitcast.100, f32[128,128,64]{1,0,2:T(8,128)S(1)} %copy-done.1, pred[128,128]{1,0:T(8,128)(4,1)S(1)} %fusion.83), kind=kOutput, calls=%fused_computation.11 | convolution fusion | flops 403701760 | bytes 6307840 | tf_op jit(solution)/shard_map/kjb,kab->kja/dot_general | solution.py:42
  334.9 0.1 slice.39
  335.0 0.0 collective-permute-done.3
  335.0 6.7 %fusion.52 = f32[64,32,128]{2,1,0:T(8,128)S(1)} fusion(f32[64,32,128]{2,1,0:T(8,128)S(1)} %fusion.8, f32[128,128,64]{1,0,2:T(8,128)S(1)} %copy-done.1, pred[128,128]{1,0:T(8,128)(4,1)S(1)} %fusion.82, f32[64,1,128]{2,1,0:T(1,128)S(1)} %bitcast.112, f32[64,31,128]{2,1,0:T(8,128)S(1)} %slice.39), kind=kOutput, calls=%fused_computation.47 | convolution fusion | flops 404226048 | bytes 7356416 | tf_op jit(solution)/shard_map/kjb,kab->kja/dot_general | solution.py:43
  341.7 1.8 fusion.57
  (5 shorter events, 0.1 us)
Async XLA Ops:
  6.5 4.5 %copy-start = (bf16[256,4096]{1,0:T(8,128)(2,1)S(1)}, bf16[256,4096]{1,0:T(8,128)(2,1)}, u32[]{:S(2)}) copy-start(bf16[256,4096]{1,0:T(8,128)(2,1)} %param.6) | copy-start | bytes 6291460
  6.5 7.5 %copy-start.4 = (f32[256,64]{0,1:T(8,128)S(1)}, f32[256,64]{0,1:T(8,128)}, u32[]{:S(2)}) copy-start(f32[256,64]{0,1:T(8,128)} %param.7) | copy-start | bytes 196612
  6.5 7.8 %copy-start.5 = (f32[64,128]{1,0:T(8,128)S(1)}, f32[64,128]{1,0:T(8,128)}, u32[]{:S(2)}) copy-start(f32[64,128]{1,0:T(8,128)} %param.8) | copy-start | bytes 98308
  6.5 270.2 %all-reduce.2.cloned.1.call-start = ((), (), s32[]{:S(2)}) async-start(), calls=%async_computation | async-start | bytes 2097152 | tf_op jit(solution)/shard_map/psum | solution.py:52
  7.5 200.5 %collective-permute-start = (f32[64,128]{1,0:T(8,128)S(1)}, f32[64,128]{1,0:T(8,128)S(1)}, u32[]{:S(2)}, u32[]{:S(2)}) collective-permute-start(f32[64,128]{1,0:T(8,128)S(1)} %slice.24), channel_id=1, source_target_pairs={{0,1},{1,2},{2,3},{3,4},{4,5},{5,6},{6,7},{7,8},{8,9},{9,10},{10,1... | collective-permute-start | bytes 98312 | tf_op jit(solution)/shard_map/ppermute | solution.py:12
  276.8 14.4 %copy-start.1 = (f32[128,128,64]{1,0,2:T(8,128)S(1)}, f32[128,128,64]{1,0,2:T(8,128)}, u32[]{:S(2)}) copy-start(f32[128,128,64]{1,0,2:T(8,128)} %copy.13) | copy-start | bytes 12582916
  280.3 17.7 %collective-permute-start.1 = (f32[64,128]{1,0:T(8,128)S(1)}, f32[64,128]{1,0:T(8,128)S(1)}, u32[]{:S(2)}, u32[]{:S(2)}) collective-permute-start(f32[64,128]{1,0:T(8,128)S(1)} %slice.36), channel_id=1, source_target_pairs={{1,0},{2,1},{3,2},{4,3},{5,4},{6,5},{7,6},{8,7},{9,8},{10,9},{11,1... | collective-permute-start | bytes 98312 | tf_op jit(solution)/shard_map/ppermute | solution.py:12
  297.9 6.7 %copy-start.2 = (f32[64,4096]{1,0:T(8,128)S(1)}, f32[64,4096]{1,0:T(8,128)}, u32[]{:S(2)}) copy-start(f32[64,4096]{1,0:T(8,128)} %param.9) | copy-start | bytes 3145732
  297.9 6.7 %copy-start.6 = (f32[64]{0:T(128)S(1)}, f32[64]{0:T(128)}, u32[]{:S(2)}) copy-start(f32[64]{0:T(128)} %param.10) | copy-start | bytes 772
  305.7 12.2 %collective-permute-start.2 = (f32[64,128]{1,0:T(8,128)S(1)}, f32[64,128]{1,0:T(8,128)S(1)}, u32[]{:S(2)}, u32[]{:S(2)}) collective-permute-start(f32[64,128]{1,0:T(8,128)S(1)} %slice.37), channel_id=1, source_target_pairs={{0,1},{1,2},{2,3},{3,4},{4,5},{5,6},{6,7},{7,8},{8,9},{9,10},{10,1... | collective-permute-start | bytes 98312 | tf_op jit(solution)/shard_map/ppermute | solution.py:12
  311.5 10.2 %copy-start.3 = (f32[64,4096]{1,0:T(8,128)S(1)}, f32[64,4096]{1,0:T(8,128)}, u32[]{:S(2)}) copy-start(f32[64,4096]{1,0:T(8,128)} %all-reduce.2.cloned.1.call-done) | copy-start | bytes 3145732
  323.5 11.5 %collective-permute-start.3 = (f32[64,128]{1,0:T(8,128)S(1)}, f32[64,128]{1,0:T(8,128)S(1)}, u32[]{:S(2)}, u32[]{:S(2)}) collective-permute-start(f32[64,128]{1,0:T(8,128)S(1)} %slice.40), channel_id=1, source_target_pairs={{1,0},{2,1},{3,2},{4,3},{5,4},{6,5},{7,6},{8,7},{9,8},{10,9},{11,1... | collective-permute-start | bytes 98312 | tf_op jit(solution)/shard_map/ppermute | solution.py:12
Sparse Core Ops, SparseCore 0:
  14.2 262.5 all-reduce.1
where the time goes:
time: 357 us; the launch traced here: 351 us
  blocking collectives  123 us (34%)
  waiting for transfers between devices  68.8 us (19%)
  local copies, waits for them, and re-layouts  65.5 us (18%)
  matrix products  54.8 us (15%)
  starting transfers between devices  21.3 us (6%)
  between operations  14.7 us (4%)
    psum x1, blocking collectives, per_device(): lax.psum((jnp.dot(spatial.T, spatial, precision=lax.Precision.HIGHEST, pr...  123 us
    psum x1, waiting for transfers between devices, per_device(): lax.psum((jnp.dot(spatial.T, spatial, precision=lax.Precision.HIGHEST, pr...  62.5 us
    gather x2, local copies, waits for them, and re-layouts, make_bands(): lookup_table = temporal[:, offsets % length]  62.2 us
    ppermute x4, starting transfers between devices, passed_along(): return lax.ppermute(block, axis, route)  21.3 us
    dot_general x2, matrix products, corr_blocks(): jnp.einsum('kjb,kab->kja', after, carry_band, precision=lax.Precision.HIG...  13.3 us
    dot_general x2, matrix products, corr_blocks(): jnp.einsum('kjb,kab->kja', blocks, current_band, precision=lax.Precision....  13.2 us
    dot_general x2, matrix products, conv_blocks(): jnp.einsum('kja,kab->kjb', before, carry_band, precision=lax.Precision.HI...  10.2 us
    dot_general x2, matrix products, conv_blocks(): jnp.einsum('kja,kab->kjb', blocks, current_band, precision=lax.Precision....  10.1 us
  transfers between devices with their start and end apart: 5, of which 2 were waited for; matrix products, arithmetic and copies ran while one was open for 28% of the time, Pallas kernels for 0%

commit v1 on v0

v1 whole, which is shorter than its diff:
```python
import jax
import jax.numpy as jnp
from jax import lax
from jax.experimental import pallas as pl
from jax.experimental.pallas import tpu as pltpu
from jax.sharding import Mesh, PartitionSpec as P

ATOMS = 64
LENGTH = 128
CHUNK = 512
HALF = CHUNK // 2
CHUNKS = 8
LANES = 2 * ATOMS
ROWS = ATOMS + 8
GROUP = 16
HIGHEST = lax.Precision.HIGHEST
F32 = jnp.float32
VMEM = pl.BlockSpec(memory_space=pltpu.VMEM)
SMEM = pl.BlockSpec(memory_space=pltpu.SMEM)


def cost(flops, bytes_accessed):
    return pl.CostEstimate(flops=flops, bytes_accessed=bytes_accessed, transcendentals=0)


def project_body(half_ref, spatial_ref, signal_ref, out_ref, parts_ref, gram_ref):
    @pl.when(pl.program_id(0) == 0)
    def _():
        spatial = spatial_ref[...]
        high = spatial.astype(jnp.bfloat16)
        low = (spatial - high.astype(F32)).astype(jnp.bfloat16)
        parts_ref[:, :ATOMS] = high
        parts_ref[:, ATOMS:] = low
        gram = lax.dot_general(
            spatial, spatial, (((0,), (0,)), ((), ())), precision=HIGHEST, preferred_element_type=F32
        )
        gram_ref[...] = jnp.concatenate([gram[8 * i : 8 * i + 8] for i in range(8)], axis=1)

    product = lax.dot_general(
        parts_ref[...], signal_ref[...], (((0,), (0,)), ((), ())), preferred_element_type=F32
    )
    out_ref[0, :ATOMS] = product[:ATOMS] + product[ATOMS:]
    out_ref[0, ATOMS:] = gram_ref[...]


def project_half(half, spatial, signal):
    channels, width = signal.shape
    count = width // (2 * CHUNK)
    return pl.pallas_call(
        project_body,
        grid_spec=pltpu.PrefetchScalarGridSpec(
            num_scalar_prefetch=1,
            grid=(count,),
            in_specs=[
                pl.BlockSpec((channels, ATOMS), lambda i, half: (0, 0)),
                pl.BlockSpec((channels, CHUNK), lambda i, half: (0, half[0] * count + i)),
            ],
            out_specs=pl.BlockSpec((1, ROWS, CHUNK), lambda i, half: (i, 0, 0)),
            scratch_shapes=[pltpu.VMEM((channels, LANES), jnp.bfloat16), pltpu.VMEM((8, CHUNK), F32)],
        ),
        out_shape=jax.ShapeDtypeStruct((count, ROWS, CHUNK), F32),
        cost_estimate=cost(2 * channels * LANES * width // 2, channels * width),
    )(half, spatial, signal)


def spread_taps(temporal_ref, taps_ref):
    temporal = temporal_ref[...]
    columns = jnp.concatenate([temporal, temporal], axis=0).T
    for tap in range(LENGTH):
        taps_ref[tap] = jnp.broadcast_to(columns[tap : tap + 1], (8, LANES))


def filter_rows(source_ref, shifted_ref, taps_ref, outputs, reverse, emit):
    inputs = outputs + 15
    for b in range(8):
        start = b + 1 if reverse else b
        shifted_ref[b, :inputs] = source_ref[start : start + 8 * inputs].reshape(inputs, 8, LANES)
    for first in range(0, outputs, GROUP):
        count = min(GROUP, outputs - first)

        def add_taps(b, sums):
            sums = list(sums)
            taps = [taps_ref[LENGTH - 1 - 8 * a - b if reverse else 8 * a + b] for a in range(16)]
            for j in range(count + 15):
                value = shifted_ref[b, first + j]
                for a in range(max(0, j - count + 1), min(16, j + 1)):
                    sums[j - a] = sums[j - a] + value * taps[a]
            return tuple(sums)

        zeros = tuple(jnp.zeros((8, LANES), F32) for _ in range(count))
        sums = lax.fori_loop(0, 8, add_taps, zeros)
        emit(8 * first, jnp.concatenate(sums, axis=0))


def rebuild_body(
    place_ref, temporal_ref, before_ref, first_ref, second_ref, after_ref, edge_ref,
    rebuilt_ref, point_ref, taps_ref, wide_ref, rows_ref, shifted_ref,
):
    place = place_ref[0]
    spread_taps(temporal_ref, taps_ref)
    edge = edge_ref[...]
    before = jnp.where(place == 0, edge, before_ref[...])
    after = jnp.where(place == CHUNKS - 1, edge, after_ref[...])
    first, second = first_ref[...], second_ref[...]
    for lane, piece in enumerate((before, first, second)):
        wide_ref[:ATOMS, lane * HALF : (lane + 1) * HALF] = piece
    for lane, piece in enumerate((first, second, after)):
        wide_ref[ATOMS:, lane * HALF : (lane + 1) * HALF] = piece
    rows_ref[...] = wide_ref[...].T
    point_ref[...] = rows_ref[LENGTH : LENGTH + CHUNK]

    def emit(row, values):
        rebuilt_ref[row : row + values.shape[0]] = values

    filter_rows(rows_ref, shifted_ref, taps_ref, 80, True, emit)


def rebuild(place, temporal, activations, edge):
    atoms, width = activations.shape
    last = width // HALF - 1
    block = (atoms, HALF)
    return pl.pallas_call(
        rebuild_body,
        grid_spec=pltpu.PrefetchScalarGridSpec(
            num_scalar_prefetch=1,
            grid=(1,),
            in_specs=[
                pl.BlockSpec((ATOMS, LENGTH), lambda i, place: (0, 0)),
                pl.BlockSpec(block, lambda i, place: (0, jnp.maximum(2 * place[0] - 1, 0))),
                pl.BlockSpec(block, lambda i, place: (0, 2 * place[0])),
                pl.BlockSpec(block, lambda i, place: (0, 2 * place[0] + 1)),
                pl.BlockSpec(block, lambda i, place: (0, jnp.minimum(2 * place[0] + 2, last))),
                pl.BlockSpec(block, lambda i, place: (0, 0)),
            ],
            out_specs=[
                pl.BlockSpec((640, LANES), lambda i, place: (0, 0)),
                pl.BlockSpec((512, LANES), lambda i, place: (0, 0)),
            ],
            scratch_shapes=[
                pltpu.VMEM((LENGTH, 8, LANES), F32),
                pltpu.VMEM((LANES, 768), F32),
                pltpu.VMEM((768, LANES), F32),
                pltpu.VMEM((8, 95, 8, LANES), F32),
            ],
        ),
        out_shape=[
            jax.ShapeDtypeStruct((640, LANES), F32),
            jax.ShapeDtypeStruct((512, LANES), F32),
        ],
        cost_estimate=cost(2 * 640 * LANES * LENGTH, 2**20),
    )(place, temporal, activations, activations, activations, activations, edge)


def steps_body(
    where_ref, step_ref, mine_ref, left_ref, right_ref, rebuilt_ref, point_ref, temporal_ref,
    threshold_ref, out_ref, taps_ref, wide_ref, cross_ref, proj_ref, next_ref, shifted_ref, mix_ref,
):
    begin, total = where_ref[0], where_ref[1]
    rate = step_ref[0]
    spread_taps(temporal_ref, taps_ref)
    gram_rows = mine_ref[ATOMS:]
    gram = jnp.concatenate([gram_rows[:, ATOMS * i : ATOMS * (i + 1)] for i in range(8)], axis=0)
    mix_ref[...] = jnp.zeros_like(mix_ref)
    mix_ref[:ATOMS, :ATOMS] = gram
    mix_ref[ATOMS:, ATOMS:] = gram
    mine = mine_ref[:ATOMS]
    wide_ref[:ATOMS, :128] = left_ref[...]
    wide_ref[:ATOMS, 128:640] = mine
    wide_ref[ATOMS:, :384] = mine[:, 128:]
    wide_ref[ATOMS:, 384:] = right_ref[...]
    cross_ref[...] = wide_ref[...].T

    segment = lax.broadcasted_iota(jnp.int32, (1, LANES), 1) // ATOMS * HALF + begin

    def sample(first, rows):
        return lax.broadcasted_iota(jnp.int32, (rows, 1), 0) + first + segment

    def mixed(rebuilt):
        return jnp.dot(rebuilt, mix_ref[...], precision=HIGHEST, preferred_element_type=F32)

    shrink = threshold_ref[...]

    proj = mixed(rebuilt_ref[...]) - cross_ref[...]
    proj_ref[...] = jnp.where(sample(-128, 640) < total, proj, 0.0)

    inertia = 1.0
    inertia_next = (1.0 + (1.0 + 4.0 * inertia * inertia) ** 0.5) / 2.0
    momentum = (inertia - 1.0) / inertia_next

    def first_step(row, gradient):
        count = gradient.shape[0]
        point = point_ref[row : row + count]
        update = jnp.maximum(point - rate * (gradient + shrink), 0.0)
        point = update + momentum * (update - point)
        next_ref[row : row + count] = jnp.where(sample(row - 128, count) >= 0, point, 0.0)

    filter_rows(proj_ref, shifted_ref, taps_ref, 64, False, first_step)

    def second_rebuilt(row, values):
        cross_part = cross_ref[128 + row : 128 + row + values.shape[0]]
        proj = mixed(values) - cross_part
        proj_ref[row : row + values.shape[0]] = jnp.where(
            sample(row, values.shape[0]) < total, proj, 0.0
        )

    filter_rows(next_ref, shifted_ref, taps_ref, 48, True, second_rebuilt)

    def second_step(row, gradient):
        count = gradient.shape[0]
        point = next_ref[128 + row : 128 + row + count]
        update = jnp.maximum(point - rate * (gradient + shrink), 0.0)
        columns = update.T
        out_ref[:, row : row + count] = columns[:ATOMS]
        out_ref[:, HALF + row : HALF + row + count] = columns[ATOMS:]

    filter_rows(proj_ref, shifted_ref, taps_ref, 32, False, second_step)


def steps(where, step_size, mine, left, right, rebuilt, point, temporal, threshold):
    return pl.pallas_call(
        steps_body,
        in_specs=[SMEM, SMEM] + [VMEM] * 7,
        out_specs=VMEM,
        out_shape=jax.ShapeDtypeStruct((ATOMS, CHUNK), F32),
        scratch_shapes=[
            pltpu.VMEM((LENGTH, 8, LANES), F32),
            pltpu.VMEM((LANES, 640), F32),
            pltpu.VMEM((640, LANES), F32),
            pltpu.VMEM((640, LANES), F32),
            pltpu.VMEM((512, LANES), F32),
            pltpu.VMEM((8, 79, 8, LANES), F32),
            pltpu.VMEM((LANES, LANES), F32),
        ],
        cost_estimate=cost(2 * 1152 * LANES * LENGTH, 2**20),
    )(where, step_size, mine, left, right, rebuilt, point, temporal, threshold)


def place_body(half_ref, mine_ref, other_ref, out_ref):
    first = pl.program_id(0) // 4 == half_ref[0]
    out_ref[...] = jnp.where(first, mine_ref[0], other_ref[0])


def place_chunks(half, mine, other):
    count = mine.shape[0]
    block = (1, ATOMS, CHUNK)
    return pl.pallas_call(
        place_body,
        grid_spec=pltpu.PrefetchScalarGridSpec(
            num_scalar_prefetch=1,
            grid=(2 * count,),
            in_specs=[pl.BlockSpec(block, lambda i, half: (i % count, 0, 0))] * 2,
            out_specs=pl.BlockSpec((ATOMS, CHUNK), lambda i, half: (0, i)),
        ),
        out_shape=jax.ShapeDtypeStruct((ATOMS, 2 * count * CHUNK), F32),
        cost_estimate=cost(0, 3 * 2**20),
    )(half, mine, other)


def solution(mesh):
    blocks = mesh.shape["tm"]
    split = Mesh(mesh.devices.reshape(2, 4, 2, blocks), ("zh", "y", "c", "tm"))
    swap = [(0, 1), (1, 0)]
    line = ("y", "c", "tm")

    def device(y, c, tm):
        return (y * 2 + c) * blocks + tm

    order = [device(q % 4, q // 4, tm) for tm in range(blocks) for q in range(CHUNKS)]
    to_next = list(zip(order[:-1], order[1:]))
    to_previous = list(zip(order[1:], order[:-1]))
    rims = []
    for tm in range(blocks - 1):
        last, first = device(3, 1, tm), device(0, 0, tm + 1)
        rims += [(last, first), (first, last)]

    def per_device(signal, spatial, temporal, activations, threshold, step_size):
        half = lax.axis_index("c").astype(jnp.int32)
        place = half * 4 + lax.axis_index("y").astype(jnp.int32)
        time_block = lax.axis_index("tm").astype(jnp.int32)
        width = activations.shape[1]

        away = project_half((1 - half)[None], spatial, signal)
        arrived = lax.ppermute(away, "c", swap)
        kept = project_half(half[None], spatial, signal)
        pieces = lax.all_to_all(kept + arrived, "y", 0, 0, tiled=True)
        group_sum = jnp.sum(pieces, axis=0)
        other_sum = lax.ppermute(group_sum, "zh", swap)

        edge = jnp.where(place == 0, activations[:, :HALF], activations[:, width - HALF :])
        edge = lax.ppermute(edge, line, rims)
        rebuilt, point = rebuild(place[None], temporal, activations, edge)

        mine = group_sum + other_sum
        right = lax.ppermute(mine[:ATOMS, :256], line, to_previous)
        left = lax.ppermute(mine[:ATOMS, CHUNK - 128 :], line, to_next)
        where = jnp.stack([time_block * width + place * CHUNK, jnp.int32(blocks * width)])
        shrink = jnp.concatenate([threshold, threshold])[None, :]
        update = steps(where, step_size, mine, left, right, rebuilt, point, temporal, shrink)

        gathered = lax.all_gather(update, "y", axis=0)
        other = lax.ppermute(gathered, "c", swap)
        return place_chunks(half[None], gathered, other)

    chan = ("zh", "y", "c")
    in_specs = (P(chan, "tm"), P(chan, None), P(), P(None, "tm"), P(), P())
    return jax.shard_map(
        per_device, mesh=split, in_specs=in_specs, out_specs=P(None, "tm"), check_vma=False
    )
```

time: 357 us -> 110 us (0.31)
  the two profiles are of different devices: /device:TPU:31 before, /device:TPU:7 now
where the time goes in v1:
time: 110 us; the launch traced here: 109 us
  starting transfers between devices  41.3 us (38%)
  Pallas kernels  28 us (25%)
  blocking collectives  19.1 us (17%)
  waiting for transfers between devices  12.5 us (11%)
  other arithmetic  4.15 us (4%)
  local copies, waits for them, and re-layouts  3.63 us (3%)
    all_gather x1, blocking collectives, per_device(): gathered = lax.all_gather(update, 'y', axis=0)  19.1 us
    ppermute x1, starting transfers between devices, per_device(): other_sum = lax.ppermute(group_sum, 'zh', swap)  15.4 us
    ppermute x1, starting transfers between devices, per_device(): other = lax.ppermute(gathered, 'c', swap)  11.8 us
    all_to_all x1, waiting for transfers between devices, per_device(): pieces = lax.all_to_all(kept + arrived, 'y', 0, 0, tiled=True)  10 us
    pallas_call x1, Pallas kernels, steps(): pl.pallas_call(steps_body, in_specs=[SMEM, SMEM] + [VMEM] * 7, out_specs=...  9.19 us
    pallas_call x2, Pallas kernels, project_half(): pl.pallas_call(project_body, grid_spec=pltpu.PrefetchScalarGridSpec(num_s...  8.07 us
    pallas_call x1, Pallas kernels, place_chunks(): pl.pallas_call(place_body, grid_spec=pltpu.PrefetchScalarGridSpec(num_sca...  5.51 us
    pallas_call x1, Pallas kernels, rebuild(): pl.pallas_call(rebuild_body, grid_spec=pltpu.PrefetchScalarGridSpec(num_s...  5.24 us
  transfers between devices with their start and end apart: 7, of which 3 were waited for; matrix products, arithmetic and copies ran while one was open for 2% of the time, Pallas kernels for 8%

profile of v1, /device:TPU:7, one launch (start us, length us, event | category | flops | bytes accessed | tf_op | source)
XLA Modules:
  0.0 109.4 jit_solution(5467560775861795282)
XLA Ops:
  0.0 1.6 %copy.7.spatial_ref = f32[256,64]{1,0:T(8,128)} copy(f32[256,64]{0,1:T(8,128)} %param.7) | data formatting | bytes 131072 | tf_op args[1]
  1.6 4.0 %shard_map.65 = f32[4,72,512]{2,1,0:T(8,128)} custom-call(s32[1]{0:T(128)} %bitcast.2.half_ref, f32[256,64]{1,0:T(8,128)} %copy.7.spatial_ref, bf16[256,4096]{1,0:T(8,128)(2,1)} %signal_ref.3), custom_call_target="tpu_custom_call" | custom-call | flops 134217728 | bytes 1048576 | tf_op jit(solution)/shard_map/pallas_call | solution.py:49
  5.6 2.6 %collective-permute-start = (f32[4,72,512]{2,1,0:T(8,128)}, f32[4,72,512]{2,1,0:T(8,128)S(1)}, u32[]{:S(2)}, u32[]{:S(2)}) collective-permute-start(f32[4,72,512]{2,1,0:T(8,128)} %shard_map.65), channel_id=1, source_target_pairs={{0,32},{32,0},{1,33},{33,1},{2,34},{34,2},{3,35},{35,3},{4,36},{36... | collective-permute-start | bytes 1769480 | tf_op jit(solution)/shard_map/ppermute | solution.py:283
  8.2 4.0 %shard_map.64 = f32[4,72,512]{2,1,0:T(8,128)} custom-call(s32[1]{0:T(128)} %bitcast.half_ref, f32[256,64]{1,0:T(8,128)} %copy.7.spatial_ref, bf16[256,4096]{1,0:T(8,128)(2,1)} %signal_ref.3), custom_call_target="tpu_custom_call" | custom-call | flops 134217728 | bytes 1048576 | tf_op jit(solution)/shard_map/pallas_call | solution.py:49
  12.2 0.0 copy-start.6
  12.2 0.0 collective-permute-done
  12.2 2.0 %add.14 = f32[4,72,512]{2,1,0:T(8,128)} add(f32[4,72,512]{2,1,0:T(8,128)} %shard_map.64, f32[4,72,512]{2,1,0:T(8,128)S(1)} %collective-permute-done) | non-fusion elementwise | flops 147456 | bytes 1769472 | tf_op jit(solution)/shard_map/add | solution.py:285
  14.2 4.2 %all-to-all-start = ((f32[4,72,512]{2,1,0:T(8,128)}), f32[4,72,512]{2,1,0:T(8,128)S(1)}, u32[]{:S(2)}, u32[]{:S(2)}) async-start(f32[4,72,512]{2,1,0:T(8,128)} %add.14), calls=%async_computation | async-start | bytes 1179648 | tf_op jit(solution)/shard_map/all_to_all | solution.py:285
  18.4 10.0 %all-to-all-done = f32[4,72,512]{2,1,0:T(8,128)S(1)} async-done(((f32[4,72,512]{2,1,0:T(8,128)}), f32[4,72,512]{2,1,0:T(8,128)S(1)}, u32[]{:S(2)}, u32[]{:S(2)}) %all-to-all-start) | async-done | bytes 589856 | tf_op jit(solution)/shard_map/all_to_all | solution.py:285
  28.5 15.4 %collective-permute-start.1 = (f32[72,512]{1,0:T(8,128)S(1)}, f32[72,512]{1,0:T(8,128)S(1)}, u32[]{:S(2)}, u32[]{:S(2)}) collective-permute-start(f32[72,512]{1,0:T(8,128)S(1)} %reduce_sum.9), channel_id=1, source_target_pairs={{0,256},{256,0},{1,257},{257,1},{2,258},{258,2},{3,259},{259,3},{4... | collective-permute-start | bytes 442376 | tf_op jit(solution)/shard_map/ppermute | solution.py:287
  43.9 0.9 slice_select_fusion
  44.8 0.7 collective-permute-start.4
  45.5 0.0 copy-done.6
  45.5 0.6 maximum_bitcast_fusion.threshold_ref
  46.1 0.9 collective-permute-done.1
  47.0 0.0 copy-start.1
  47.1 4.7 %collective-permute-start.3 = (f32[64,256]{1,0:T(8,128)S(1)}, f32[64,256]{1,0:T(8,128)S(1)}, u32[]{:S(2)}, u32[]{:S(2)}) collective-permute-start(f32[64,256]{1,0:T(8,128)S(1)} %slice.17), channel_id=1, source_target_pairs={{64,0},{128,64},{192,128},{32,192},{96,32},{160,96},{224,160},{1,2... | collective-permute-start | bytes 196616 | tf_op jit(solution)/shard_map/ppermute | solution.py:294
  51.8 1.9 %collective-permute-start.2 = (f32[64,128]{1,0:T(8,128)S(1)}, f32[64,128]{1,0:T(8,128)S(1)}, u32[]{:S(2)}, u32[]{:S(2)}) collective-permute-start(f32[64,128]{1,0:T(8,128)S(1)} %slice.16), channel_id=1, source_target_pairs={{0,64},{64,128},{128,192},{192,32},{32,96},{96,160},{160,224},{224... | collective-permute-start | bytes 98312 | tf_op jit(solution)/shard_map/ppermute | solution.py:295
  53.7 0.6 pad_add_fusion.where_ref
  55.0 0.0 collective-permute-done.4.edge_ref
  55.0 0.0 copy-start.3
  55.0 0.6 copy-done.3
  55.6 5.2 %shard_map.66 = (f32[640,128]{1,0:T(8,128)}, f32[512,128]{1,0:T(8,128)}) custom-call(s32[1]{0:T(128)} %bitcast.3.place_ref, f32[64,128]{1,0:T(8,128)} %temporal_ref.3, f32[64,4096]{1,0:T(8,128)} %after_ref.1, f32[64,4096]{1,0:T(8,128)} %after_ref.1, f32[64,4096]{1,0:T(8,128)} %after_ref.1, f32[64,4096]{1,0:T(8,128)} %after_ref.1, f32[64,256]{1,0:T(8,128)} %copy-done.3), custom_call_target="tpu_custom_call" | custom-call | flops 20971520 | bytes 1048576 | tf_op jit(solution)/shard_map/pallas_call | solution.py:122
  60.9 0.0 copy-done.1
  60.9 0.0 collective-permute-done.2.left_ref
  60.9 0.0 copy-start.5
  60.9 0.0 collective-permute-done.3.right_ref
  60.9 0.0 copy-start.4
  60.9 0.6 copy-done.5
  61.5 0.0 copy-done.4
  61.5 9.2 %shard_map.67 = f32[64,512]{1,0:T(8,128)} custom-call(s32[2]{0:T(128)} %pad_add_fusion.where_ref, f32[1]{0:T(128)S(6)} %copy.9.step_ref, f32[72,512]{1,0:T(8,128)} %copy-done.1, f32[64,128]{1,0:T(8,128)} %copy-done.5, f32[64,256]{1,0:T(8,128)} %copy-done.4, f32[640,128]{1,0:T(8,128)} %get-tuple-element.7.rebuilt_ref, f32[512,128]{1,0:T(8,128)} %get-tuple-element.8.point_ref, ...), custom_call_target="tpu_custom_call" | custom-call | flops 37748736 | bytes 1048576 | tf_op jit(solution)/shard_map/pallas_call | solution.py:220
  70.7 19.1 %all-gather = f32[256,512]{1,0:T(8,128)S(1)} all-gather(f32[64,512]{1,0:T(8,128)} %shard_map.67), channel_id=2, replica_groups=mesh['zh'=2,'y'=4,'c'=2,'tm'=32] {'y'}, dimensions={0}, use_global_device_ids=true | all-gather | bytes 655360 | tf_op jit(solution)/shard_map/all_gather | solution.py:300
  89.8 0.0 copy-start
  89.8 11.8 %collective-permute-start.5 = (f32[4,64,512]{2,1,0:T(8,128)S(1)}, f32[4,64,512]{2,1,0:T(8,128)S(1)}, u32[]{:S(2)}, u32[]{:S(2)}) collective-permute-start(f32[4,64,512]{2,1,0:T(8,128)S(1)} %bitcast.7), channel_id=1, source_target_pairs={{0,32},{32,0},{1,33},{33,1},{2,34},{34,2},{3,35},{35,3},{4,36},{36... | collective-permute-start | bytes 1572872 | tf_op jit(solution)/shard_map/ppermute | solution.py:301
  101.6 1.5 %collective-permute-done.5.other_ref = f32[4,64,512]{2,1,0:T(8,128)S(1)} collective-permute-done((f32[4,64,512]{2,1,0:T(8,128)S(1)}, f32[4,64,512]{2,1,0:T(8,128)S(1)}, u32[]{:S(2)}, u32[]{:S(2)}) %collective-permute-start.5) | collective-permute-done | bytes 524320 | tf_op jit(solution)/shard_map/ppermute | solution.py:301
  103.1 0.0 copy-done
  103.1 0.0 copy-start.2
  103.1 0.8 copy-done.2
  103.9 5.5 %shard_map.68 = f32[64,4096]{1,0:T(8,128)} custom-call(s32[1]{0:T(128)} %bitcast.half_ref, f32[4,64,512]{2,1,0:T(8,128)} %bitcast.8, f32[4,64,512]{2,1,0:T(8,128)} %copy-done.2), custom_call_target="tpu_custom_call" | custom-call | bytes 3145728 | tf_op jit(solution)/shard_map/pallas_call | solution.py:246
  (4 shorter events, 0.1 us)
Async XLA Ops:
  5.6 6.6 %collective-permute-start = (f32[4,72,512]{2,1,0:T(8,128)}, f32[4,72,512]{2,1,0:T(8,128)S(1)}, u32[]{:S(2)}, u32[]{:S(2)}) collective-permute-start(f32[4,72,512]{2,1,0:T(8,128)} %shard_map.65), channel_id=1, source_target_pairs={{0,32},{32,0},{1,33},{33,1},{2,34},{34,2},{3,35},{35,3},{4,36},{36... | collective-permute-start | bytes 1769480 | tf_op jit(solution)/shard_map/ppermute | solution.py:283
  12.2 33.3 %copy-start.6 = (f32[64]{0:T(128)S(1)}, f32[64]{0:T(128)}, u32[]{:S(2)}) copy-start(f32[64]{0:T(128)} %param.10) | copy-start | bytes 772
  14.2 14.2 %all-to-all-start = ((f32[4,72,512]{2,1,0:T(8,128)}), f32[4,72,512]{2,1,0:T(8,128)S(1)}, u32[]{:S(2)}, u32[]{:S(2)}) async-start(f32[4,72,512]{2,1,0:T(8,128)} %add.14), calls=%async_computation | async-start | bytes 1179648 | tf_op jit(solution)/shard_map/all_to_all | solution.py:285
  28.5 18.5 %collective-permute-start.1 = (f32[72,512]{1,0:T(8,128)S(1)}, f32[72,512]{1,0:T(8,128)S(1)}, u32[]{:S(2)}, u32[]{:S(2)}) collective-permute-start(f32[72,512]{1,0:T(8,128)S(1)} %reduce_sum.9), channel_id=1, source_target_pairs={{0,256},{256,0},{1,257},{257,1},{2,258},{258,2},{3,259},{259,3},{4... | collective-permute-start | bytes 442376 | tf_op jit(solution)/shard_map/ppermute | solution.py:287
  44.8 10.2 %collective-permute-start.4 = (f32[64,256]{1,0:T(8,128)S(1)}, f32[64,256]{1,0:T(8,128)S(1)}, u32[]{:S(2)}, u32[]{:S(2)}) collective-permute-start(f32[64,256]{1,0:T(8,128)S(1)} %slice_select_fusion), channel_id=1, source_target_pairs={{224,1},{1,224},{225,2},{2,225},{226,3},{3,226},{227,4},{4,227},{2... | collective-permute-start | bytes 196616 | tf_op jit(solution)/shard_map/ppermute | solution.py:290
  47.0 13.9 %copy-start.1 = (f32[72,512]{1,0:T(8,128)}, f32[72,512]{1,0:T(8,128)S(1)}, u32[]{:S(2)}) copy-start(f32[72,512]{1,0:T(8,128)S(1)} %add.15.mine_ref) | copy-start | bytes 442372
  47.1 13.8 %collective-permute-start.3 = (f32[64,256]{1,0:T(8,128)S(1)}, f32[64,256]{1,0:T(8,128)S(1)}, u32[]{:S(2)}, u32[]{:S(2)}) collective-permute-start(f32[64,256]{1,0:T(8,128)S(1)} %slice.17), channel_id=1, source_target_pairs={{64,0},{128,64},{192,128},{32,192},{96,32},{160,96},{224,160},{1,2... | collective-permute-start | bytes 196616 | tf_op jit(solution)/shard_map/ppermute | solution.py:294
  51.8 9.1 %collective-permute-start.2 = (f32[64,128]{1,0:T(8,128)S(1)}, f32[64,128]{1,0:T(8,128)S(1)}, u32[]{:S(2)}, u32[]{:S(2)}) collective-permute-start(f32[64,128]{1,0:T(8,128)S(1)} %slice.16), channel_id=1, source_target_pairs={{0,64},{64,128},{128,192},{192,32},{32,96},{96,160},{160,224},{224... | collective-permute-start | bytes 98312 | tf_op jit(solution)/shard_map/ppermute | solution.py:295
  55.0 0.6 copy-start.3
  60.9 0.6 copy-start.5
  60.9 0.6 copy-start.4
  89.8 13.4 %copy-start = (f32[256,512]{1,0:T(8,128)}, f32[256,512]{1,0:T(8,128)S(1)}, u32[]{:S(2)}) copy-start(f32[256,512]{1,0:T(8,128)S(1)} %all-gather) | copy-start | bytes 1572868
  89.8 13.4 %collective-permute-start.5 = (f32[4,64,512]{2,1,0:T(8,128)S(1)}, f32[4,64,512]{2,1,0:T(8,128)S(1)}, u32[]{:S(2)}, u32[]{:S(2)}) collective-permute-start(f32[4,64,512]{2,1,0:T(8,128)S(1)} %bitcast.7), channel_id=1, source_target_pairs={{0,32},{32,0},{1,33},{33,1},{2,34},{34,2},{3,35},{35,3},{4,36},{36... | collective-permute-start | bytes 1572872 | tf_op jit(solution)/shard_map/ppermute | solution.py:301
  103.1 0.8 copy-start.2

commit v2 on v1

v2 whole, which is shorter than its diff:
```python
import jax
import jax.numpy as jnp
from jax import lax
from jax.experimental import pallas as pl
from jax.experimental.pallas import tpu as pltpu
from jax.sharding import Mesh, PartitionSpec as P

ATOMS = 64
LENGTH = 128
CHUNK = 512
CHUNKS = 8
QUARTER = 4
LANES = 2 * ATOMS
ROWS = ATOMS + 8
SEGMENT = 56
SIDE = 8 * SEGMENT
WINDOW = 2 * SIDE
PHASE = SEGMENT // 4
REACH = 46
HIGHEST = lax.Precision.HIGHEST
F32 = jnp.float32
VMEM = pl.BlockSpec(memory_space=pltpu.VMEM)
SMEM = pl.BlockSpec(memory_space=pltpu.SMEM)
ANY = pl.BlockSpec(memory_space=pl.ANY)


def cost(flops, bytes_accessed):
    return pl.CostEstimate(flops=flops, bytes_accessed=bytes_accessed, transcendentals=0)


def params(mebibytes):
    return pltpu.CompilerParams(vmem_limit_bytes=mebibytes * 2**20)


def project_body(half_ref, spatial_ref, signal_ref, out_ref, block_ref, sems):
    def fetch(i):
        column = pl.multiple_of((half_ref[0] * QUARTER + i) * CHUNK, CHUNK)
        return pltpu.make_async_copy(
            signal_ref.at[:, pl.ds(column, CHUNK)], block_ref.at[i], sems.at[i]
        )

    for i in range(QUARTER):
        fetch(i).start()
    spatial = spatial_ref[...]
    high = spatial.astype(jnp.bfloat16)
    low = (spatial - high.astype(F32)).astype(jnp.bfloat16)
    parts = jnp.concatenate([high, low], axis=0)
    gram = lax.dot_general(
        spatial, spatial, (((1,), (1,)), ((), ())), precision=HIGHEST, preferred_element_type=F32
    )
    gram = jnp.concatenate([gram[8 * i : 8 * i + 8] for i in range(8)], axis=1)
    for i in range(QUARTER):
        out_ref[i, ATOMS:] = gram
    for i in range(QUARTER):
        fetch(i).wait()
        product = jnp.dot(parts, block_ref[i], preferred_element_type=F32)
        out_ref[i, :ATOMS] = product[:ATOMS] + product[ATOMS:]


def project_half(half, spatial, signal):
    channels, width = signal.shape
    return pl.pallas_call(
        project_body,
        in_specs=[SMEM, VMEM, ANY],
        out_specs=VMEM,
        out_shape=jax.ShapeDtypeStruct((QUARTER, ROWS, CHUNK), F32),
        scratch_shapes=[
            pltpu.VMEM((QUARTER, channels, CHUNK), jnp.bfloat16),
            pltpu.SemaphoreType.DMA((QUARTER,)),
        ],
        compiler_params=params(8),
        cost_estimate=cost(2 * channels * LANES * width // 2, channels * width),
    )(half, spatial, signal)


def to_segments(wide_ref, out_ref):
    columns = wide_ref[...].T
    for s in range(8):
        out_ref[pl.ds(s, SEGMENT, stride=8)] = columns[s * SEGMENT : (s + 1) * SEGMENT]


def spread_taps(temporal_ref, taps_ref):
    temporal = temporal_ref[...]
    columns = jnp.concatenate([temporal, temporal], axis=0).T
    for i in range(LENGTH // 4):
        c0, c1, c2, c3 = (
            jnp.broadcast_to(columns[4 * i + p : 4 * i + p + 1], (8, LANES)) for p in range(4)
        )
        even, odd = c0 + c1, c2 + c3
        for k, tap in enumerate((c0, c0 + c2, c2, even, even + odd, odd, c1, c1 + c3, c3)):
            taps_ref[k, i] = tap


def lane_half():
    return lax.broadcasted_iota(jnp.int32, (1, 8, LANES), 2) // ATOMS


def sublane():
    return lax.broadcasted_iota(jnp.int32, (1, 8, LANES), 1)


def later_segment(rows):
    up = pltpu.roll(rows, 7, 1)
    return jnp.where(sublane() == 7, pltpu.roll(up, ATOMS, 2), up)


def earlier_segment(rows):
    down = pltpu.roll(rows, 1, 1)
    return jnp.where(sublane() == 0, pltpu.roll(down, ATOMS, 2), down)


def spread_later(rows, spread_ref):
    for first in range(0, 4 * REACH, SEGMENT):
        count = min(SEGMENT, 4 * REACH - first)
        spread_ref[first // 4 : (first + count) // 4] = rows[:count].reshape(count // 4, 4, 8, LANES)
        if count == SEGMENT:
            rows = later_segment(rows)


def spread_earlier(rows, spread_ref, outside=None):
    start = LENGTH
    while True:
        skip = max(0, -start)
        kept = rows[skip:]
        first, count = start + skip, SEGMENT - skip
        spread_ref[first // 4 : (first + count) // 4] = kept.reshape(count // 4, 4, 8, LANES)
        if start <= 0:
            return
        rows = earlier_segment(rows)
        start -= SEGMENT
        if outside is not None:
            rim = outside(start)
            rows = jnp.where((sublane() == 0) & (lane_half() == 0), rim, rows)


def short_inputs(spread_ref, inputs_ref, offset):
    count = REACH - 1

    def x(p):
        p = p + offset
        return spread_ref[p // 4 : p // 4 + count, p % 4]

    x0, x1, x2, x3, x4, x5 = (x(p) for p in range(6))
    inputs_ref[0, :count] = (x0 - x1) - (x2 - x3)
    inputs_ref[1, :count] = x2 - x3
    inputs_ref[2, :count] = (x4 - x5) - (x2 - x3)
    inputs_ref[3, :count] = x1 - x3
    inputs_ref[4, :count] = x3
    inputs_ref[5, :count] = x5 - x3
    inputs_ref[6, :count] = (x2 - x1) - (x4 - x3)
    inputs_ref[7, :count] = x4 - x3
    last = min(count, REACH - (6 + offset) // 4)
    x6 = spread_ref[(6 + offset) // 4 : (6 + offset) // 4 + last, (6 + offset) % 4]
    inputs_ref[8, :last] = (x6 - x5[:last]) - (x4[:last] - x3[:last])


def filter_rows(inputs_ref, taps_ref, sums_ref, reverse):
    taps = LENGTH // 4

    @pl.loop(0, 9)
    def _(k):
        sums = [None] * PHASE
        held = {}
        for j in range(PHASE + taps - 1):
            if j < taps:
                held[j] = taps_ref[8 - k, taps - 1 - j] if reverse else taps_ref[k, j]
            value = inputs_ref[k, j]
            for m in range(max(0, j - PHASE + 1), min(taps, j + 1)):
                term = value * held[m]
                sums[j - m] = term if sums[j - m] is None else sums[j - m] + term
        for i in range(PHASE):
            sums_ref[k, i] = sums[i]

    a, b, c = sums_ref[0] + sums_ref[1], sums_ref[3] + sums_ref[4], sums_ref[6] + sums_ref[7]
    d, e, f = sums_ref[1] + sums_ref[2], sums_ref[4] + sums_ref[5], sums_ref[7] + sums_ref[8]
    rows = jnp.stack([a + b, b + c, d + e, e + f], axis=1)
    return rows.reshape(SEGMENT, 8, LANES)


FILTER_SCRATCH = [
    pltpu.VMEM((9, LENGTH // 4, 8, LANES), F32),
    pltpu.VMEM((REACH, 4, 8, LANES), F32),
    pltpu.VMEM((9, REACH, 8, LANES), F32),
    pltpu.VMEM((9, PHASE, 8, LANES), F32),
    pltpu.VMEM((LANES, 512), F32),
]


def rebuild_body(
    place_ref, temporal_ref, before_ref, first_ref, second_ref, after_ref, edge_ref,
    rebuilt_ref, point_ref, taps_ref, spread_ref, inputs_ref, sums_ref, wide_ref, rim_ref,
):
    place = place_ref[0]
    spread_taps(temporal_ref, taps_ref)
    edge = edge_ref[...]
    before = jnp.where(place == 0, edge, before_ref[...])
    after = jnp.where(place == CHUNKS - 1, edge, after_ref[...])
    second = second_ref[...]
    wide_ref[:ATOMS] = jnp.concatenate([before[:, 128:], first_ref[...], second[:, :128]], axis=1)
    wide_ref[ATOMS:] = jnp.concatenate([second[:, 64:], after, after[:, :64]], axis=1)
    to_segments(wide_ref, point_ref)
    rim = before[:, :128]
    rim_ref[...] = jnp.concatenate([rim, rim], axis=0).T

    def outside(start):
        count = min(SEGMENT, SEGMENT + start)
        rows = rim_ref[max(start, 0) : max(start, 0) + count].reshape(count, 1, LANES)
        rows = jnp.broadcast_to(rows, (count, 8, LANES))
        if count < SEGMENT:
            rows = jnp.concatenate([jnp.zeros((SEGMENT - count, 8, LANES), F32), rows], axis=0)
        return rows

    rows = point_ref[...].reshape(SEGMENT, 8, LANES)
    spread_earlier(rows, spread_ref, outside)
    short_inputs(spread_ref, inputs_ref, 1)
    rebuilt_ref[...] = filter_rows(inputs_ref, taps_ref, sums_ref, True).reshape(SIDE, LANES)


def rebuild(place, temporal, activations, edge):
    atoms, width = activations.shape
    half = CHUNK // 2
    last = width // half - 1
    block = (atoms, half)
    return pl.pallas_call(
        rebuild_body,
        grid_spec=pltpu.PrefetchScalarGridSpec(
            num_scalar_prefetch=1,
            grid=(1,),
            in_specs=[
                pl.BlockSpec((ATOMS, LENGTH), lambda i, place: (0, 0)),
                pl.BlockSpec(block, lambda i, place: (0, jnp.maximum(2 * place[0] - 1, 0))),
                pl.BlockSpec(block, lambda i, place: (0, 2 * place[0])),
                pl.BlockSpec(block, lambda i, place: (0, 2 * place[0] + 1)),
                pl.BlockSpec(block, lambda i, place: (0, jnp.minimum(2 * place[0] + 2, last))),
                pl.BlockSpec(block, lambda i, place: (0, 0)),
            ],
            out_specs=[pl.BlockSpec((SIDE, LANES), lambda i, place: (0, 0))] * 2,
            scratch_shapes=FILTER_SCRATCH + [pltpu.VMEM((LENGTH, LANES), F32)],
        ),
        out_shape=[jax.ShapeDtypeStruct((SIDE, LANES), F32)] * 2,
        compiler_params=params(12),
        cost_estimate=cost(2 * SIDE * LANES * LENGTH, 2**20),
    )(place, temporal, activations, activations, activations, activations, edge)


def steps_body(
    total, begin_ref, step_ref, mine_ref, left_ref, right_ref, rebuilt_ref, point_ref,
    temporal_ref, threshold_ref, out_ref, taps_ref, spread_ref, inputs_ref, sums_ref, wide_ref,
    cross_ref, mix_ref,
):
    begin = begin_ref[0]
    rate = step_ref[0]
    spread_taps(temporal_ref, taps_ref)
    gram_rows = mine_ref[ATOMS:]
    gram = jnp.concatenate([gram_rows[:, ATOMS * i : ATOMS * (i + 1)] for i in range(8)], axis=0)
    mix_ref[...] = jnp.zeros_like(mix_ref)
    mix_ref[:ATOMS, :ATOMS] = gram
    mix_ref[ATOMS:, ATOMS:] = gram
    mine = mine_ref[:ATOMS]
    right = right_ref[...]
    wide_ref[:ATOMS] = jnp.concatenate([left_ref[...], mine[:, :384]], axis=1)
    wide_ref[ATOMS:] = jnp.concatenate([mine[:, 320:], right, right[:, :64]], axis=1)
    to_segments(wide_ref, cross_ref)

    shape = (SEGMENT, 8, LANES)
    sample = lax.broadcasted_iota(jnp.int32, shape, 0) + (
        (lane_half() * 8 + sublane()) * SEGMENT + (begin - LENGTH)
    )
    shrink = threshold_ref[...]
    shrink = jnp.concatenate([shrink, shrink], axis=1).reshape(1, 1, LANES)

    def projected(rebuilt):
        mixed = jnp.dot(rebuilt, mix_ref[...], precision=HIGHEST, preferred_element_type=F32)
        rows = (mixed - cross_ref[...]).reshape(shape)
        return jnp.where(sample < total, rows, 0.0)

    def stepped(point, rows):
        spread_later(rows, spread_ref)
        short_inputs(spread_ref, inputs_ref, 0)
        gradient = filter_rows(inputs_ref, taps_ref, sums_ref, False)
        return jnp.maximum(point - rate * (gradient + shrink), 0.0)

    inertia = 1.0
    inertia_next = (1.0 + (1.0 + 4.0 * inertia * inertia) ** 0.5) / 2.0
    momentum = (inertia - 1.0) / inertia_next
    previous = point_ref[...].reshape(shape)
    update = stepped(previous, projected(rebuilt_ref[...]))
    point = update + momentum * (update - previous)
    point = jnp.where(sample >= 0, point, 0.0)

    spread_earlier(point, spread_ref)
    short_inputs(spread_ref, inputs_ref, 1)
    rebuilt = filter_rows(inputs_ref, taps_ref, sums_ref, True)
    update = stepped(point, projected(rebuilt.reshape(SIDE, LANES)))

    cross_ref[...] = update.reshape(SIDE, LANES)
    rows = [cross_ref[pl.ds(s, SEGMENT, stride=8)] for s in range(8)]
    rows.append(jnp.zeros((512 - SIDE, LANES), F32))
    columns = jnp.concatenate(rows, axis=0).T
    out_ref[...] = jnp.concatenate([columns[:ATOMS, 128:SIDE], columns[ATOMS:, :192]], axis=1)


def steps(total, begin, step_size, mine, left, right, rebuilt, point, temporal, threshold):
    def body(*refs):
        steps_body(total, *refs)

    return pl.pallas_call(
        body,
        in_specs=[SMEM, SMEM] + [VMEM] * 7,
        out_specs=VMEM,
        out_shape=jax.ShapeDtypeStruct((ATOMS, CHUNK), F32),
        scratch_shapes=FILTER_SCRATCH
        + [pltpu.VMEM((SIDE, LANES), F32), pltpu.VMEM((LANES, LANES), F32)],
        compiler_params=params(12),
        cost_estimate=cost(6 * SIDE * LANES * LENGTH, 2**20),
    )(begin, step_size, mine, left, right, rebuilt, point, temporal, threshold)


def place_copies(half, chunks_ref, out_ref, sems):
    copies = []
    for i in range(QUARTER):
        column = pl.multiple_of((half * QUARTER + i) * CHUNK, CHUNK)
        copies.append(
            pltpu.make_async_copy(chunks_ref.at[i], out_ref.at[:, pl.ds(column, CHUNK)], sems.at[i])
        )
    for copy in copies:
        copy.start()
    for copy in copies:
        copy.wait()


def place_mine_body(half_ref, chunks_ref, out_ref, sems):
    place_copies(half_ref[0], chunks_ref, out_ref, sems)


def place_other_body(half_ref, chunks_ref, begun_ref, out_ref, sems):
    place_copies(1 - half_ref[0], chunks_ref, out_ref, sems)


def place_half(half, chunks, begun=None):
    out_shape = jax.ShapeDtypeStruct((ATOMS, CHUNKS * CHUNK), F32)
    first = begun is None
    return pl.pallas_call(
        place_mine_body if first else place_other_body,
        in_specs=[SMEM, ANY] + ([] if first else [ANY]),
        out_specs=ANY,
        out_shape=out_shape,
        scratch_shapes=[pltpu.SemaphoreType.DMA((QUARTER,))],
        input_output_aliases={} if first else {2: 0},
        compiler_params=params(4),
        cost_estimate=cost(0, 2**20),
    )(half, chunks, *([] if first else [begun]))


def solution(mesh):
    blocks = mesh.shape["tm"]
    split = Mesh(mesh.devices.reshape(2, 4, 2, blocks), ("zh", "y", "c", "tm"))
    swap = [(0, 1), (1, 0)]
    line = ("y", "c", "tm")

    def device(y, c, tm):
        return (y * 2 + c) * blocks + tm

    order = [device(q % 4, q // 4, tm) for tm in range(blocks) for q in range(CHUNKS)]
    to_next = list(zip(order[:-1], order[1:]))
    to_previous = list(zip(order[1:], order[:-1]))
    rims = []
    for tm in range(blocks - 1):
        last, first = device(3, 1, tm), device(0, 0, tm + 1)
        rims += [(last, first), (first, last)]

    def per_device(signal, spatial, temporal, activations, threshold, step_size):
        half = lax.axis_index("c").astype(jnp.int32)
        place = half * 4 + lax.axis_index("y").astype(jnp.int32)
        time_block = lax.axis_index("tm").astype(jnp.int32)
        width = activations.shape[1]
        spatial = spatial.T

        away = project_half((1 - half)[None], spatial, signal)
        arrived = lax.ppermute(away, "c", swap)
        kept = project_half(half[None], spatial, signal)
        summed = kept + arrived
        rim = CHUNK // 2
        edge = jnp.where(place == 0, activations[:, :rim], activations[:, width - rim :])
        edge, summed = lax.optimization_barrier((edge, summed))
        pieces = lax.all_to_all(summed, "y", 0, 0, tiled=True)
        edge = lax.ppermute(edge, line, rims)
        rebuilt, point = rebuild(place[None], temporal, activations, edge)
        group_sum = jnp.sum(pieces, axis=0)
        group_sum, rebuilt, point = lax.optimization_barrier((group_sum, rebuilt, point))
        mine = group_sum + lax.ppermute(group_sum, "zh", swap)

        right = lax.ppermute(mine[:ATOMS, :256], line, to_previous)
        left = lax.ppermute(mine[:ATOMS, CHUNK - 128 :], line, to_next)
        begin = time_block * width + place * CHUNK
        update = steps(
            blocks * width, begin[None], step_size, mine, left, right, rebuilt, point, temporal,
            threshold[None, :],
        )

        gathered = lax.all_gather(update, "y", axis=0)
        other = lax.ppermute(gathered, "c", swap)
        return place_half(half[None], other, place_half(half[None], gathered))

    chan = ("zh", "y", "c")
    in_specs = (P(chan, "tm"), P(chan, None), P(), P(None, "tm"), P(), P())
    return jax.shard_map(
        per_device, mesh=split, in_specs=in_specs, out_specs=P(None, "tm"), check_vma=False
    )
```

time: 110 us -> 103 us (0.936)
  Pallas kernels: 28 us -> 11.7 us
  starting transfers between devices: 41.3 us -> 57.4 us
  blocking collectives: 19.1 us -> 12.6 us
  other arithmetic: 4.15 us -> 0.98 us
  waiting for transfers between devices: 12.5 us -> 14.9 us
    ppermute x1, starting transfers between devices: 11.8 us -> 25.7 us  [per_device(): other = lax.ppermute(gathered, 'c', swap)]
    pallas_call x4 -> x5, Pallas kernels: 22.8 us -> 9.84 us  [the longest x1 5.79 us: steps(): pl.pallas_call(body, in_specs=[SMEM, SMEM] + [VMEM] * 7, out_specs=VMEM,...]
    all_gather x1, blocking collectives: 19.1 us -> 12.6 us  [per_device(): gathered = lax.all_gather(update, 'y', axis=0)]
    ppermute x1, waiting for transfers between devices: 0.01 us -> 3.86 us  [per_device(): left = lax.ppermute(mine[:ATOMS, CHUNK - 128:], line, to_next)]
    pallas_call x1, Pallas kernels: 5.24 us -> 1.82 us  [rebuild(): pl.pallas_call(rebuild_body, grid_spec=pltpu.PrefetchScalarGridSpec(num_s...]
    all_to_all x1, waiting for transfers between devices: 10 us -> 7.5 us  [per_device(): pieces = lax.all_to_all(summed, 'y', 0, 0, tiled=True)]
    ppermute x1, starting transfers between devices: 4.7 us -> 6.93 us  [per_device(): right = lax.ppermute(mine[:ATOMS, :256], line, to_previous)]
    ppermute x1, waiting for transfers between devices: 0.91 us -> 2.82 us  [per_device(): mine = group_sum + lax.ppermute(group_sum, 'zh', swap)]
  transfers between devices with their start and end apart: 7 -> 7, of which waited for: 3 -> 4; matrix products, arithmetic and copies ran while one was open for 2% -> 0% of each run, Pallas kernels for 8% -> 4%
where the time goes in v2:
time: 103 us; the launch traced here: 102 us
  starting transfers between devices  57.4 us (56%)
  waiting for transfers between devices  14.9 us (14%)
  blocking collectives  12.6 us (12%)
  Pallas kernels  11.7 us (11%)
  local copies, waits for them, and re-layouts  4.05 us (4%)
    ppermute x1, starting transfers between devices, per_device(): other = lax.ppermute(gathered, 'c', swap)  25.7 us
    ppermute x1, starting transfers between devices, per_device(): mine = group_sum + lax.ppermute(group_sum, 'zh', swap)  15.4 us
    all_gather x1, blocking collectives, per_device(): gathered = lax.all_gather(update, 'y', axis=0)  12.6 us
    all_to_all x1, waiting for transfers between devices, per_device(): pieces = lax.all_to_all(summed, 'y', 0, 0, tiled=True)  7.5 us
    ppermute x1, starting transfers between devices, per_device(): right = lax.ppermute(mine[:ATOMS, :256], line, to_previous)  6.93 us
    pallas_call x1, Pallas kernels, steps(): pl.pallas_call(body, in_specs=[SMEM, SMEM] + [VMEM] * 7, out_specs=VMEM,...  5.79 us
    all_to_all x1, starting transfers between devices, per_device(): pieces = lax.all_to_all(summed, 'y', 0, 0, tiled=True)  4.19 us
    unnamed x14, local copies, waits for them, and re-layouts  4.04 us
  transfers between devices with their start and end apart: 7, of which 4 were waited for; matrix products, arithmetic and copies ran while one was open for 0% of the time, Pallas kernels for 4%

profile of v2, /device:TPU:7, one launch (start us, length us, event | category | flops | bytes accessed | tf_op | source)
XLA Modules:
  0.0 102.4 jit_solution(13729459373814854256)
XLA Ops:
  0.0 0.0 copy-start.1
  0.0 1.6 %copy-done.1 = bf16[256,4096]{1,0:T(8,128)(2,1)S(1)} copy-done((bf16[256,4096]{1,0:T(8,128)(2,1)S(1)}, bf16[256,4096]{1,0:T(8,128)(2,1)}, u32[]{:S(2)}) %copy-start.1) | copy-done | bytes 2097176
  1.6 0.0 copy-start.3
  1.6 0.8 copy-done.3
  2.4 0.0 copy-start.4
  2.4 0.0 copy-start
  2.4 1.2 %shard_map.65 = f32[4,72,512]{2,1,0:T(8,128)S(1)} custom-call(s32[1]{0:T(128)} %bitcast.3.half_ref, f32[64,256]{1,0:T(8,128)S(1)} %bitcast.9, bf16[256,4096]{1,0:T(8,128)(2,1)S(1)} %copy-done.1), custom_call_target="tpu_custom_call" | custom-call | flops 134217728 | bytes 1048576 | tf_op jit(solution)/shard_map/pallas_call | solution.py:62
  3.7 2.6 %collective-permute-start = (f32[4,72,512]{2,1,0:T(8,128)S(1)}, f32[4,72,512]{2,1,0:T(8,128)S(1)}, u32[]{:S(2)}, u32[]{:S(2)}) collective-permute-start(f32[4,72,512]{2,1,0:T(8,128)S(1)} %shard_map.65), channel_id=1, source_target_pairs={{0,32},{32,0},{1,33},{33,1},{2,34},{34,2},{3,35},{35,3},{4,36},{36... | collective-permute-start | bytes 1769480 | tf_op jit(solution)/shard_map/ppermute | solution.py:380
  6.3 0.0 copy-done.4
  6.3 0.0 copy-start.2
  6.3 1.6 %copy-done.2 = bf16[256,4096]{1,0:T(8,128)(2,1)S(1)} copy-done((bf16[256,4096]{1,0:T(8,128)(2,1)S(1)}, bf16[256,4096]{1,0:T(8,128)(2,1)}, u32[]{:S(2)}) %copy-start.2) | copy-done | bytes 2097176
  7.9 1.2 %shard_map.64 = f32[4,72,512]{2,1,0:T(8,128)S(1)} custom-call(s32[1]{0:T(128)} %bitcast.half_ref, f32[64,256]{1,0:T(8,128)S(1)} %bitcast.10, bf16[256,4096]{1,0:T(8,128)(2,1)S(1)} %copy-done.2), custom_call_target="tpu_custom_call" | custom-call | flops 134217728 | bytes 1048576 | tf_op jit(solution)/shard_map/pallas_call | solution.py:62
  9.1 0.0 copy-done
  9.1 0.0 copy-start.5
  9.1 0.0 collective-permute-done
  9.1 0.9 add.14
  10.0 4.2 %all-to-all-start = ((f32[4,72,512]{2,1,0:T(8,128)}), f32[4,72,512]{2,1,0:T(8,128)S(1)}, u32[]{:S(2)}, u32[]{:S(2)}) async-start(f32[4,72,512]{2,1,0:T(8,128)} %add.14), calls=%async_computation | async-start | bytes 1179648 | tf_op jit(solution)/shard_map/all_to_all | solution.py:386
  14.2 0.7 collective-permute-start.1
  14.9 0.0 collective-permute-done.1.edge_ref
  14.9 0.0 copy-done.5
  14.9 0.0 copy-start.6
  14.9 1.8 %shard_map.66 = (f32[448,128]{1,0:T(8,128)S(1)}, f32[448,128]{1,0:T(8,128)S(1)}) custom-call(s32[1]{0:T(128)} %bitcast.4.place_ref, f32[64,128]{1,0:T(8,128)S(1)} %copy-done.5, f32[64,4096]{1,0:T(8,128)S(1)} %copy-done, f32[64,4096]{1,0:T(8,128)S(1)} %copy-done, f32[64,4096]{1,0:T(8,128)S(1)} %copy-done, f32[64,4096]{1,0:T(8,128)S(1)} %copy-done, ...), custom_call_target="tpu_custom_call" | custom-call | flops 14680064 | bytes 1048576 | tf_op jit(solution)/shard_map/pallas_call | solution.py:224
  16.7 7.5 %all-to-all-done = f32[4,72,512]{2,1,0:T(8,128)S(1)} async-done(((f32[4,72,512]{2,1,0:T(8,128)}), f32[4,72,512]{2,1,0:T(8,128)S(1)}, u32[]{:S(2)}, u32[]{:S(2)}) %all-to-all-start) | async-done | bytes 589856 | tf_op jit(solution)/shard_map/all_to_all | solution.py:386
  24.3 15.4 %collective-permute-start.2 = (f32[72,512]{1,0:T(8,128)S(1)}, f32[72,512]{1,0:T(8,128)S(1)}, u32[]{:S(2)}, u32[]{:S(2)}) collective-permute-start(f32[72,512]{1,0:T(8,128)S(1)} %reduce_sum.9), channel_id=1, source_target_pairs={{0,256},{256,0},{1,257},{257,1},{2,258},{258,2},{3,259},{259,3},{4... | collective-permute-start | bytes 442376 | tf_op jit(solution)/shard_map/ppermute | solution.py:391
  39.7 2.8 %collective-permute-done.2 = f32[72,512]{1,0:T(8,128)S(1)} collective-permute-done((f32[72,512]{1,0:T(8,128)S(1)}, f32[72,512]{1,0:T(8,128)S(1)}, u32[]{:S(2)}, u32[]{:S(2)}) %collective-permute-start.2) | collective-permute-done | bytes 147488 | tf_op jit(solution)/shard_map/ppermute | solution.py:391
  42.6 6.9 %collective-permute-start.4 = (f32[64,256]{1,0:T(8,128)S(1)}, f32[64,256]{1,0:T(8,128)S(1)}, u32[]{:S(2)}, u32[]{:S(2)}) collective-permute-start(f32[64,256]{1,0:T(8,128)S(1)} %slice.17), channel_id=1, source_target_pairs={{64,0},{128,64},{192,128},{32,192},{96,32},{160,96},{224,160},{1,2... | collective-permute-start | bytes 196616 | tf_op jit(solution)/shard_map/ppermute | solution.py:393
  49.6 1.9 %collective-permute-start.3 = (f32[64,128]{1,0:T(8,128)S(1)}, f32[64,128]{1,0:T(8,128)S(1)}, u32[]{:S(2)}, u32[]{:S(2)}) collective-permute-start(f32[64,128]{1,0:T(8,128)S(1)} %slice.16), channel_id=1, source_target_pairs={{0,64},{64,128},{128,192},{192,32},{32,96},{96,160},{160,224},{224... | collective-permute-start | bytes 98312 | tf_op jit(solution)/shard_map/ppermute | solution.py:394
  52.1 3.9 %collective-permute-done.3.refs_3_ = f32[64,128]{1,0:T(8,128)S(1)} collective-permute-done((f32[64,128]{1,0:T(8,128)S(1)}, f32[64,128]{1,0:T(8,128)S(1)}, u32[]{:S(2)}, u32[]{:S(2)}) %collective-permute-start.3) | collective-permute-done | bytes 32800 | tf_op jit(solution)/shard_map/ppermute | solution.py:394
  56.0 0.0 collective-permute-done.4.refs_4_
  56.0 0.0 copy-done.6
  56.0 5.8 %shard_map.67 = f32[64,512]{1,0:T(8,128)S(1)} custom-call(s32[1]{0:T(128)} %bitcast.1.refs_0_, f32[1]{0:T(128)S(6)} %copy.9.refs_1_, f32[72,512]{1,0:T(8,128)S(1)} %add.15.refs_2_, f32[64,128]{1,0:T(8,128)S(1)} %collective-permute-done.3.refs_3_, f32[64,256]{1,0:T(8,128)S(1)} %collective-permute-done.4.refs_4_, f32[448,128]{1,0:T(8,128)S(1)} %get-tuple-element.17.refs_5_, ...), custom_call_target="tpu_custom_call" | custom-call | flops 44040192 | bytes 1048576 | tf_op jit(solution)/shard_map/pallas_call | solution.py:307
  61.8 12.6 %all-gather = f32[256,512]{1,0:T(8,128)S(1)} all-gather(f32[64,512]{1,0:T(8,128)S(1)} %shard_map.67), channel_id=2, replica_groups=mesh['zh'=2,'y'=4,'c'=2,'tm'=32] {'y'}, dimensions={0}, use_global_device_ids=true | all-gather | bytes 655360 | tf_op jit(solution)/shard_map/all_gather | solution.py:401
  74.4 25.7 %collective-permute-start.5 = (f32[4,64,512]{2,1,0:T(8,128)S(1)}, f32[4,64,512]{2,1,0:T(8,128)S(1)}, u32[]{:S(2)}, u32[]{:S(2)}) collective-permute-start(f32[4,64,512]{2,1,0:T(8,128)S(1)} %bitcast.7), channel_id=1, source_target_pairs={{0,32},{32,0},{1,33},{33,1},{2,34},{34,2},{3,35},{35,3},{4,36},{36... | collective-permute-start | bytes 1572872 | tf_op jit(solution)/shard_map/ppermute | solution.py:402
  100.1 0.8 shard_map.68.begun_ref
  100.9 0.7 collective-permute-done.5.chunks_ref
  101.6 0.8 shard_map.69
  (5 shorter events, 0.1 us)
Async XLA Ops:
  0.0 1.6 %copy-start.1 = (bf16[256,4096]{1,0:T(8,128)(2,1)S(1)}, bf16[256,4096]{1,0:T(8,128)(2,1)}, u32[]{:S(2)}) copy-start(bf16[256,4096]{1,0:T(8,128)(2,1)} %signal_ref.3) | copy-start | bytes 6291460
  1.6 0.8 copy-start.3
  2.4 3.8 %copy-start.4 = (f32[256,64]{0,1:T(8,128)S(1)}, f32[256,64]{0,1:T(8,128)}, u32[]{:S(2)}) copy-start(f32[256,64]{0,1:T(8,128)} %param.7) | copy-start | bytes 196612
  2.4 6.6 %copy-start = (f32[64,4096]{1,0:T(8,128)S(1)}, f32[64,4096]{1,0:T(8,128)}, u32[]{:S(2)}) copy-start(f32[64,4096]{1,0:T(8,128)} %after_ref.1) | copy-start | bytes 3145732
  3.7 5.5 %collective-permute-start = (f32[4,72,512]{2,1,0:T(8,128)S(1)}, f32[4,72,512]{2,1,0:T(8,128)S(1)}, u32[]{:S(2)}, u32[]{:S(2)}) collective-permute-start(f32[4,72,512]{2,1,0:T(8,128)S(1)} %shard_map.65), channel_id=1, source_target_pairs={{0,32},{32,0},{1,33},{33,1},{2,34},{34,2},{3,35},{35,3},{4,36},{36... | collective-permute-start | bytes 1769480 | tf_op jit(solution)/shard_map/ppermute | solution.py:380
  6.3 1.6 %copy-start.2 = (bf16[256,4096]{1,0:T(8,128)(2,1)S(1)}, bf16[256,4096]{1,0:T(8,128)(2,1)}, u32[]{:S(2)}) copy-start(bf16[256,4096]{1,0:T(8,128)(2,1)} %signal_ref.3) | copy-start | bytes 6291460
  9.1 5.8 %copy-start.5 = (f32[64,128]{1,0:T(8,128)S(1)}, f32[64,128]{1,0:T(8,128)}, u32[]{:S(2)}) copy-start(f32[64,128]{1,0:T(8,128)} %refs_7_.1) | copy-start | bytes 98308
  10.0 14.2 %all-to-all-start = ((f32[4,72,512]{2,1,0:T(8,128)}), f32[4,72,512]{2,1,0:T(8,128)S(1)}, u32[]{:S(2)}, u32[]{:S(2)}) async-start(f32[4,72,512]{2,1,0:T(8,128)} %add.14), calls=%async_computation | async-start | bytes 1179648 | tf_op jit(solution)/shard_map/all_to_all | solution.py:386
  14.2 0.7 collective-permute-start.1
  14.9 41.1 %copy-start.6 = (f32[64]{0:T(128)S(1)}, f32[64]{0:T(128)}, u32[]{:S(2)}) copy-start(f32[64]{0:T(128)} %param.10) | copy-start | bytes 772
  24.3 18.3 %collective-permute-start.2 = (f32[72,512]{1,0:T(8,128)S(1)}, f32[72,512]{1,0:T(8,128)S(1)}, u32[]{:S(2)}, u32[]{:S(2)}) collective-permute-start(f32[72,512]{1,0:T(8,128)S(1)} %reduce_sum.9), channel_id=1, source_target_pairs={{0,256},{256,0},{1,257},{257,1},{2,258},{258,2},{3,259},{259,3},{4... | collective-permute-start | bytes 442376 | tf_op jit(solution)/shard_map/ppermute | solution.py:391
  42.6 13.4 %collective-permute-start.4 = (f32[64,256]{1,0:T(8,128)S(1)}, f32[64,256]{1,0:T(8,128)S(1)}, u32[]{:S(2)}, u32[]{:S(2)}) collective-permute-start(f32[64,256]{1,0:T(8,128)S(1)} %slice.17), channel_id=1, source_target_pairs={{64,0},{128,64},{192,128},{32,192},{96,32},{160,96},{224,160},{1,2... | collective-permute-start | bytes 196616 | tf_op jit(solution)/shard_map/ppermute | solution.py:393
  49.6 6.4 %collective-permute-start.3 = (f32[64,128]{1,0:T(8,128)S(1)}, f32[64,128]{1,0:T(8,128)S(1)}, u32[]{:S(2)}, u32[]{:S(2)}) collective-permute-start(f32[64,128]{1,0:T(8,128)S(1)} %slice.16), channel_id=1, source_target_pairs={{0,64},{64,128},{128,192},{192,32},{32,96},{96,160},{160,224},{224... | collective-permute-start | bytes 98312 | tf_op jit(solution)/shard_map/ppermute | solution.py:394
  74.4 27.2 %collective-permute-start.5 = (f32[4,64,512]{2,1,0:T(8,128)S(1)}, f32[4,64,512]{2,1,0:T(8,128)S(1)}, u32[]{:S(2)}, u32[]{:S(2)}) collective-permute-start(f32[4,64,512]{2,1,0:T(8,128)S(1)} %bitcast.7), channel_id=1, source_target_pairs={{0,32},{32,0},{1,33},{33,1},{2,34},{34,2},{3,35},{35,3},{4,36},{36... | collective-permute-start | bytes 1572872 | tf_op jit(solution)/shard_map/ppermute | solution.py:402

commit v3 on v2

--- a/solution.py
+++ b/solution.py
@@ -22,6 +22,8 @@
 VMEM = pl.BlockSpec(memory_space=pltpu.VMEM)
 SMEM = pl.BlockSpec(memory_space=pltpu.SMEM)
 ANY = pl.BlockSpec(memory_space=pl.ANY)
+HBM = pl.BlockSpec(memory_space=pltpu.HBM)
+RUN = 8
 
 
 def cost(flops, bytes_accessed):
@@ -34,7 +36,7 @@
 
 def project_body(half_ref, spatial_ref, signal_ref, out_ref, block_ref, sems):
     def fetch(i):
-        column = pl.multiple_of((half_ref[0] * QUARTER + i) * CHUNK, CHUNK)
+        column = pl.multiple_of((2 * i + half_ref[0]) * CHUNK, CHUNK)
         return pltpu.make_async_copy(
             signal_ref.at[:, pl.ds(column, CHUNK)], block_ref.at[i], sems.at[i]
         )
@@ -61,7 +63,7 @@
     channels, width = signal.shape
     return pl.pallas_call(
         project_body,
-        in_specs=[SMEM, VMEM, ANY],
+        in_specs=[SMEM, VMEM, HBM],
         out_specs=VMEM,
         out_shape=jax.ShapeDtypeStruct((QUARTER, ROWS, CHUNK), F32),
         scratch_shapes=[
@@ -244,7 +246,7 @@
 
 
 def steps_body(
-    total, begin_ref, step_ref, mine_ref, left_ref, right_ref, rebuilt_ref, point_ref,
+    total, begin_ref, half_ref, step_ref, mine_ref, inner_ref, outer_ref, rebuilt_ref, point_ref,
     temporal_ref, threshold_ref, out_ref, taps_ref, spread_ref, inputs_ref, sums_ref, wide_ref,
     cross_ref, mix_ref,
 ):
@@ -257,8 +259,10 @@
     mix_ref[:ATOMS, :ATOMS] = gram
     mix_ref[ATOMS:, ATOMS:] = gram
     mine = mine_ref[:ATOMS]
-    right = right_ref[...]
-    wide_ref[:ATOMS] = jnp.concatenate([left_ref[...], mine[:, :384]], axis=1)
+    first = half_ref[0] == 0
+    left = jnp.where(first, outer_ref[:, 128:], inner_ref[:, 128:])
+    right = jnp.where(first, inner_ref[...], outer_ref[...])
+    wide_ref[:ATOMS] = jnp.concatenate([left, mine[:, :384]], axis=1)
     wide_ref[ATOMS:] = jnp.concatenate([mine[:, 320:], right, right[:, :64]], axis=1)
     to_segments(wide_ref, cross_ref)
 
@@ -300,26 +304,26 @@
     out_ref[...] = jnp.concatenate([columns[:ATOMS, 128:SIDE], columns[ATOMS:, :192]], axis=1)
 
 
-def steps(total, begin, step_size, mine, left, right, rebuilt, point, temporal, threshold):
+def steps(total, begin, half, step_size, mine, inner, outer, rebuilt, point, temporal, threshold):
     def body(*refs):
         steps_body(total, *refs)
 
     return pl.pallas_call(
         body,
-        in_specs=[SMEM, SMEM] + [VMEM] * 7,
+        in_specs=[SMEM] * 3 + [VMEM] * 7,
         out_specs=VMEM,
         out_shape=jax.ShapeDtypeStruct((ATOMS, CHUNK), F32),
         scratch_shapes=FILTER_SCRATCH
         + [pltpu.VMEM((SIDE, LANES), F32), pltpu.VMEM((LANES, LANES), F32)],
         compiler_params=params(12),
         cost_estimate=cost(6 * SIDE * LANES * LENGTH, 2**20),
-    )(begin, step_size, mine, left, right, rebuilt, point, temporal, threshold)
+    )(begin, half, step_size, mine, inner, outer, rebuilt, point, temporal, threshold)
 
 
 def place_copies(half, chunks_ref, out_ref, sems):
     copies = []
     for i in range(QUARTER):
-        column = pl.multiple_of((half * QUARTER + i) * CHUNK, CHUNK)
+        column = pl.multiple_of((2 * i + half) * CHUNK, CHUNK)
         copies.append(
             pltpu.make_async_copy(chunks_ref.at[i], out_ref.at[:, pl.ds(column, CHUNK)], sems.at[i])
         )
@@ -356,22 +360,25 @@
     blocks = mesh.shape["tm"]
     split = Mesh(mesh.devices.reshape(2, 4, 2, blocks), ("zh", "y", "c", "tm"))
     swap = [(0, 1), (1, 0)]
-    line = ("y", "c", "tm")
-
-    def device(y, c, tm):
-        return (y * 2 + c) * blocks + tm
-
-    order = [device(q % 4, q // 4, tm) for tm in range(blocks) for q in range(CHUNKS)]
-    to_next = list(zip(order[:-1], order[1:]))
-    to_previous = list(zip(order[1:], order[:-1]))
-    rims = []
-    for tm in range(blocks - 1):
-        last, first = device(3, 1, tm), device(0, 0, tm + 1)
-        rims += [(last, first), (first, last)]
+    line = ("zh", "y", "c", "tm")
+
+    def device(zh, q, tm):
+        return (zh * CHUNKS + q) * blocks + tm
+
+    inside, rims = [], []
+    for zh in range(2):
+        for tm in range(blocks):
+            for q in range(1, CHUNKS - 1, 2):
+                inside.append((device(zh, q, tm), device(zh, q + 1, tm)))
+            if tm + 1 < blocks:
+                near = 1 - zh if (tm + 1) % RUN == 0 else zh
+                rims.append((device(zh, CHUNKS - 1, tm), device(near, 0, tm + 1)))
+    rims = rims + [(b, a) for a, b in rims]
+    outside = rims + inside + [(b, a) for a, b in inside]
 
     def per_device(signal, spatial, temporal, activations, threshold, step_size):
         half = lax.axis_index("c").astype(jnp.int32)
-        place = half * 4 + lax.axis_index("y").astype(jnp.int32)
+        place = lax.axis_index("y").astype(jnp.int32) * 2 + half
         time_block = lax.axis_index("tm").astype(jnp.int32)
         width = activations.shape[1]
         spatial = spatial.T
@@ -390,12 +397,14 @@
         group_sum, rebuilt, point = lax.optimization_barrier((group_sum, rebuilt, point))
         mine = group_sum + lax.ppermute(group_sum, "zh", swap)
 
-        right = lax.ppermute(mine[:ATOMS, :256], line, to_previous)
-        left = lax.ppermute(mine[:ATOMS, CHUNK - 128 :], line, to_next)
+        start, end = mine[:ATOMS, :rim], mine[:ATOMS, CHUNK - rim :]
+        first = half == 0
+        outer = lax.ppermute(jnp.where(first, start, end), line, outside)
+        inner = lax.ppermute(jnp.where(first, end, start), "c", swap)
         begin = time_block * width + place * CHUNK
         update = steps(
-            blocks * width, begin[None], step_size, mine, left, right, rebuilt, point, temporal,
-            threshold[None, :],
+            blocks * width, begin[None], half[None], step_size, mine, inner, outer, rebuilt, point,
+            temporal, threshold[None, :],
         )
 
         gathered = lax.all_gather(update, "y", axis=0)

time: 103 us -> 86.2 us (0.84)
  starting transfers between devices: 57.4 us -> 47.1 us
  waiting for transfers between devices: 14.9 us -> 11.2 us
  blocking collectives: 12.6 us -> 9.9 us
    ppermute x1, starting transfers between devices: 25.7 us -> 6.17 us  [per_device(): other = lax.ppermute(gathered, 'c', swap)]
    ppermute x2, starting transfers between devices: 8.85 us -> 17.7 us  [the longest x1 13.8 us: per_device(): inner = lax.ppermute(jnp.where(first, end, start), 'c', swap)]
    ppermute x2, waiting for transfers between devices: 3.86 us -> 0.22 us  [the longest x1 0.21 us: per_device(): inner = lax.ppermute(jnp.where(first, end, start), 'c', swap)]
    all_gather x1, blocking collectives: 12.6 us -> 9.9 us  [per_device(): gathered = lax.all_gather(update, 'y', axis=0)]
where the time goes in v3:
time: 86.2 us; the launch traced here: 85.8 us
  starting transfers between devices  47.1 us (55%)
  Pallas kernels  11.7 us (14%)
  waiting for transfers between devices  11.2 us (13%)
  blocking collectives  9.9 us (11%)
  local copies, waits for them, and re-layouts  4.04 us (5%)
  other arithmetic  1 us (1%)
    ppermute x1, starting transfers between devices, per_device(): mine = group_sum + lax.ppermute(group_sum, 'zh', swap)  15.9 us
    ppermute x1, starting transfers between devices, per_device(): inner = lax.ppermute(jnp.where(first, end, start), 'c', swap)  13.8 us
    all_gather x1, blocking collectives, per_device(): gathered = lax.all_gather(update, 'y', axis=0)  9.9 us
    all_to_all x1, waiting for transfers between devices, per_device(): pieces = lax.all_to_all(summed, 'y', 0, 0, tiled=True)  7.5 us
    ppermute x1, starting transfers between devices, per_device(): other = lax.ppermute(gathered, 'c', swap)  6.17 us
    pallas_call x1, Pallas kernels, steps(): pl.pallas_call(body, in_specs=[SMEM] * 3 + [VMEM] * 7, out_specs=VMEM, ou...  5.79 us
    all_to_all x1, starting transfers between devices, per_device(): pieces = lax.all_to_all(summed, 'y', 0, 0, tiled=True)  4.18 us
    unnamed x14, local copies, waits for them, and re-layouts  4.04 us
  transfers between devices with their start and end apart: 7, of which 4 were waited for; matrix products, arithmetic and copies ran while one was open for 0% of the time, Pallas kernels for 4%

profile of v3, /device:TPU:7, one launch (start us, length us, event | category | flops | bytes accessed | tf_op | source)
XLA Modules:
  0.0 85.8 jit_solution(17998177991396163155)
XLA Ops:
  0.0 0.0 copy-start.1
  0.0 1.6 %copy-done.1 = bf16[256,4096]{1,0:T(8,128)(2,1)S(1)} copy-done((bf16[256,4096]{1,0:T(8,128)(2,1)S(1)}, bf16[256,4096]{1,0:T(8,128)(2,1)}, u32[]{:S(2)}) %copy-start.1) | copy-done | bytes 2097176
  1.6 0.0 copy-start.3
  1.6 0.8 copy-done.3
  2.4 0.0 copy-start.4
  2.4 0.0 copy-start
  2.4 1.2 %shard_map.65 = f32[4,72,512]{2,1,0:T(8,128)S(1)} custom-call(s32[1]{0:T(128)} %bitcast.3.half_ref, f32[64,256]{1,0:T(8,128)S(1)} %bitcast.9, bf16[256,4096]{1,0:T(8,128)(2,1)S(1)} %copy-done.1), custom_call_target="tpu_custom_call" | custom-call | flops 134217728 | bytes 1048576 | tf_op jit(solution)/shard_map/pallas_call | solution.py:64
  3.7 2.6 %collective-permute-start = (f32[4,72,512]{2,1,0:T(8,128)S(1)}, f32[4,72,512]{2,1,0:T(8,128)S(1)}, u32[]{:S(2)}, u32[]{:S(2)}) collective-permute-start(f32[4,72,512]{2,1,0:T(8,128)S(1)} %shard_map.65), channel_id=1, source_target_pairs={{0,32},{32,0},{1,33},{33,1},{2,34},{34,2},{3,35},{35,3},{4,36},{36... | collective-permute-start | bytes 1769480 | tf_op jit(solution)/shard_map/ppermute | solution.py:387
  6.3 0.0 copy-done.4
  6.3 0.0 copy-start.2
  6.3 1.6 %copy-done.2 = bf16[256,4096]{1,0:T(8,128)(2,1)S(1)} copy-done((bf16[256,4096]{1,0:T(8,128)(2,1)S(1)}, bf16[256,4096]{1,0:T(8,128)(2,1)}, u32[]{:S(2)}) %copy-start.2) | copy-done | bytes 2097176
  7.9 1.2 %shard_map.64 = f32[4,72,512]{2,1,0:T(8,128)S(1)} custom-call(s32[1]{0:T(128)} %bitcast.half_ref.refs_1_, f32[64,256]{1,0:T(8,128)S(1)} %bitcast.10, bf16[256,4096]{1,0:T(8,128)(2,1)S(1)} %copy-done.2), custom_call_target="tpu_custom_call" | custom-call | flops 134217728 | bytes 1048576 | tf_op jit(solution)/shard_map/pallas_call | solution.py:64
  9.1 0.0 copy-done
  9.1 0.0 copy-start.5
  9.1 0.0 collective-permute-done
  9.1 0.9 %add.14 = f32[4,72,512]{2,1,0:T(8,128)} add(f32[4,72,512]{2,1,0:T(8,128)S(1)} %shard_map.64, f32[4,72,512]{2,1,0:T(8,128)S(1)} %collective-permute-done) | non-fusion elementwise | flops 147456 | bytes 1769472 | tf_op jit(solution)/shard_map/add | solution.py:389
  10.0 4.2 %all-to-all-start = ((f32[4,72,512]{2,1,0:T(8,128)}), f32[4,72,512]{2,1,0:T(8,128)S(1)}, u32[]{:S(2)}, u32[]{:S(2)}) async-start(f32[4,72,512]{2,1,0:T(8,128)} %add.14), calls=%async_computation | async-start | bytes 1179648 | tf_op jit(solution)/shard_map/all_to_all | solution.py:393
  14.2 0.7 collective-permute-start.1
  14.9 0.0 collective-permute-done.1.edge_ref
  14.9 0.0 copy-done.5
  14.9 0.0 copy-start.6
  14.9 1.8 %shard_map.66 = (f32[448,128]{1,0:T(8,128)S(1)}, f32[448,128]{1,0:T(8,128)S(1)}) custom-call(s32[1]{0:T(128)} %bitcast.4.place_ref, f32[64,128]{1,0:T(8,128)S(1)} %copy-done.5, f32[64,4096]{1,0:T(8,128)S(1)} %copy-done, f32[64,4096]{1,0:T(8,128)S(1)} %copy-done, f32[64,4096]{1,0:T(8,128)S(1)} %copy-done, f32[64,4096]{1,0:T(8,128)S(1)} %copy-done, ...), custom_call_target="tpu_custom_call" | custom-call | flops 14680064 | bytes 1048576 | tf_op jit(solution)/shard_map/pallas_call | solution.py:226
  16.7 7.5 %all-to-all-done = f32[4,72,512]{2,1,0:T(8,128)S(1)} async-done(((f32[4,72,512]{2,1,0:T(8,128)}), f32[4,72,512]{2,1,0:T(8,128)S(1)}, u32[]{:S(2)}, u32[]{:S(2)}) %all-to-all-start) | async-done | bytes 589856 | tf_op jit(solution)/shard_map/all_to_all | solution.py:393
  24.3 15.9 %collective-permute-start.2 = (f32[72,512]{1,0:T(8,128)S(1)}, f32[72,512]{1,0:T(8,128)S(1)}, u32[]{:S(2)}, u32[]{:S(2)}) collective-permute-start(f32[72,512]{1,0:T(8,128)S(1)} %reduce_sum.9), channel_id=1, source_target_pairs={{0,256},{256,0},{1,257},{257,1},{2,258},{258,2},{3,259},{259,3},{4... | collective-permute-start | bytes 442376 | tf_op jit(solution)/shard_map/ppermute | solution.py:398
  40.2 2.8 %collective-permute-done.2 = f32[72,512]{1,0:T(8,128)S(1)} collective-permute-done((f32[72,512]{1,0:T(8,128)S(1)}, f32[72,512]{1,0:T(8,128)S(1)}, u32[]{:S(2)}, u32[]{:S(2)}) %collective-permute-start.2) | collective-permute-done | bytes 147488 | tf_op jit(solution)/shard_map/ppermute | solution.py:398
  43.0 3.9 %collective-permute-start.4 = (f32[64,256]{1,0:T(8,128)S(1)}, f32[64,256]{1,0:T(8,128)S(1)}, u32[]{:S(2)}, u32[]{:S(2)}) collective-permute-start(f32[64,256]{1,0:T(8,128)S(1)} %get-tuple-element.19), channel_id=1, source_target_pairs={{224,1},{225,2},{226,3},{227,4},{228,5},{229,6},{230,7},{231,264},... | collective-permute-start | bytes 196616 | tf_op jit(solution)/shard_map/ppermute | solution.py:402
  47.0 13.8 %collective-permute-start.3 = (f32[64,256]{1,0:T(8,128)S(1)}, f32[64,256]{1,0:T(8,128)S(1)}, u32[]{:S(2)}, u32[]{:S(2)}) collective-permute-start(f32[64,256]{1,0:T(8,128)S(1)} %get-tuple-element.20), channel_id=1, source_target_pairs={{0,32},{32,0},{1,33},{33,1},{2,34},{34,2},{3,35},{35,3},{4,36},{36... | collective-permute-start | bytes 196616 | tf_op jit(solution)/shard_map/ppermute | solution.py:403
  61.4 0.0 collective-permute-done.4.refs_5_
  61.4 0.2 collective-permute-done.3.refs_4_
  61.6 0.0 copy-done.6
  61.6 5.8 %shard_map.67 = f32[64,512]{1,0:T(8,128)S(1)} custom-call(s32[1]{0:T(128)} %bitcast.1.refs_0_, s32[1]{0:T(128)} %bitcast.half_ref.refs_1_, f32[1]{0:T(128)S(6)} %copy.9.refs_2_, f32[72,512]{1,0:T(8,128)S(1)} %add.15.refs_3_, f32[64,256]{1,0:T(8,128)S(1)} %collective-permute-done.3.refs_4_, f32[64,256]{1,0:T(8,128)S(1)} %collective-permute-done.4.refs_5_, ...), custom_call_target="tpu_custom_call" | custom-call | flops 44040192 | bytes 1048576 | tf_op jit(solution)/shard_map/pallas_call | solution.py:311
  67.4 9.9 %all-gather = f32[256,512]{1,0:T(8,128)S(1)} all-gather(f32[64,512]{1,0:T(8,128)S(1)} %shard_map.67), channel_id=2, replica_groups=mesh['zh'=2,'y'=4,'c'=2,'tm'=32] {'y'}, dimensions={0}, use_global_device_ids=true | all-gather | bytes 655360 | tf_op jit(solution)/shard_map/all_gather | solution.py:410
  77.3 6.2 %collective-permute-start.5 = (f32[4,64,512]{2,1,0:T(8,128)S(1)}, f32[4,64,512]{2,1,0:T(8,128)S(1)}, u32[]{:S(2)}, u32[]{:S(2)}) collective-permute-start(f32[4,64,512]{2,1,0:T(8,128)S(1)} %bitcast.7), channel_id=1, source_target_pairs={{0,32},{32,0},{1,33},{33,1},{2,34},{34,2},{3,35},{35,3},{4,36},{36... | collective-permute-start | bytes 1572872 | tf_op jit(solution)/shard_map/ppermute | solution.py:411
  83.5 0.8 shard_map.68.begun_ref
  84.3 0.7 collective-permute-done.5.chunks_ref
  85.0 0.8 shard_map.69
  (4 shorter events, 0.1 us)
Async XLA Ops:
  0.0 1.6 %copy-start.1 = (bf16[256,4096]{1,0:T(8,128)(2,1)S(1)}, bf16[256,4096]{1,0:T(8,128)(2,1)}, u32[]{:S(2)}) copy-start(bf16[256,4096]{1,0:T(8,128)(2,1)} %signal_ref.3) | copy-start | bytes 6291460
  1.6 0.8 copy-start.3
  2.4 3.8 %copy-start.4 = (f32[256,64]{0,1:T(8,128)S(1)}, f32[256,64]{0,1:T(8,128)}, u32[]{:S(2)}) copy-start(f32[256,64]{0,1:T(8,128)} %param.7) | copy-start | bytes 196612
  2.4 6.7 %copy-start = (f32[64,4096]{1,0:T(8,128)S(1)}, f32[64,4096]{1,0:T(8,128)}, u32[]{:S(2)}) copy-start(f32[64,4096]{1,0:T(8,128)} %after_ref.1) | copy-start | bytes 3145732
  3.7 5.5 %collective-permute-start = (f32[4,72,512]{2,1,0:T(8,128)S(1)}, f32[4,72,512]{2,1,0:T(8,128)S(1)}, u32[]{:S(2)}, u32[]{:S(2)}) collective-permute-start(f32[4,72,512]{2,1,0:T(8,128)S(1)} %shard_map.65), channel_id=1, source_target_pairs={{0,32},{32,0},{1,33},{33,1},{2,34},{34,2},{3,35},{35,3},{4,36},{36... | collective-permute-start | bytes 1769480 | tf_op jit(solution)/shard_map/ppermute | solution.py:387
  6.3 1.6 %copy-start.2 = (bf16[256,4096]{1,0:T(8,128)(2,1)S(1)}, bf16[256,4096]{1,0:T(8,128)(2,1)}, u32[]{:S(2)}) copy-start(bf16[256,4096]{1,0:T(8,128)(2,1)} %signal_ref.3) | copy-start | bytes 6291460
  9.1 5.8 %copy-start.5 = (f32[64,128]{1,0:T(8,128)S(1)}, f32[64,128]{1,0:T(8,128)}, u32[]{:S(2)}) copy-start(f32[64,128]{1,0:T(8,128)} %refs_8_.1) | copy-start | bytes 98308
  10.0 14.2 %all-to-all-start = ((f32[4,72,512]{2,1,0:T(8,128)}), f32[4,72,512]{2,1,0:T(8,128)S(1)}, u32[]{:S(2)}, u32[]{:S(2)}) async-start(f32[4,72,512]{2,1,0:T(8,128)} %add.14), calls=%async_computation | async-start | bytes 1179648 | tf_op jit(solution)/shard_map/all_to_all | solution.py:393
  14.2 0.7 collective-permute-start.1
  14.9 46.7 %copy-start.6 = (f32[64]{0:T(128)S(1)}, f32[64]{0:T(128)}, u32[]{:S(2)}) copy-start(f32[64]{0:T(128)} %param.10) | copy-start | bytes 772
  24.3 18.7 %collective-permute-start.2 = (f32[72,512]{1,0:T(8,128)S(1)}, f32[72,512]{1,0:T(8,128)S(1)}, u32[]{:S(2)}, u32[]{:S(2)}) collective-permute-start(f32[72,512]{1,0:T(8,128)S(1)} %reduce_sum.9), channel_id=1, source_target_pairs={{0,256},{256,0},{1,257},{257,1},{2,258},{258,2},{3,259},{259,3},{4... | collective-permute-start | bytes 442376 | tf_op jit(solution)/shard_map/ppermute | solution.py:398
  43.0 18.4 %collective-permute-start.4 = (f32[64,256]{1,0:T(8,128)S(1)}, f32[64,256]{1,0:T(8,128)S(1)}, u32[]{:S(2)}, u32[]{:S(2)}) collective-permute-start(f32[64,256]{1,0:T(8,128)S(1)} %get-tuple-element.19), channel_id=1, source_target_pairs={{224,1},{225,2},{226,3},{227,4},{228,5},{229,6},{230,7},{231,264},... | collective-permute-start | bytes 196616 | tf_op jit(solution)/shard_map/ppermute | solution.py:402
  47.0 14.6 %collective-permute-start.3 = (f32[64,256]{1,0:T(8,128)S(1)}, f32[64,256]{1,0:T(8,128)S(1)}, u32[]{:S(2)}, u32[]{:S(2)}) collective-permute-start(f32[64,256]{1,0:T(8,128)S(1)} %get-tuple-element.20), channel_id=1, source_target_pairs={{0,32},{32,0},{1,33},{33,1},{2,34},{34,2},{3,35},{35,3},{4,36},{36... | collective-permute-start | bytes 196616 | tf_op jit(solution)/shard_map/ppermute | solution.py:403
  77.3 7.7 %collective-permute-start.5 = (f32[4,64,512]{2,1,0:T(8,128)S(1)}, f32[4,64,512]{2,1,0:T(8,128)S(1)}, u32[]{:S(2)}, u32[]{:S(2)}) collective-permute-start(f32[4,64,512]{2,1,0:T(8,128)S(1)} %bitcast.7), channel_id=1, source_target_pairs={{0,32},{32,0},{1,33},{33,1},{2,34},{34,2},{3,35},{35,3},{4,36},{36... | collective-permute-start | bytes 1572872 | tf_op jit(solution)/shard_map/ppermute | solution.py:411

commit v4 on v3

--- a/solution.py
+++ b/solution.py
@@ -70,7 +70,7 @@
             pltpu.VMEM((QUARTER, channels, CHUNK), jnp.bfloat16),
             pltpu.SemaphoreType.DMA((QUARTER,)),
         ],
-        compiler_params=params(8),
+        compiler_params=params(60),
         cost_estimate=cost(2 * channels * LANES * width // 2, channels * width),
     )(half, spatial, signal)
 
@@ -188,13 +188,17 @@
 ]
 
 
-def rebuild_body(
-    place_ref, temporal_ref, before_ref, first_ref, second_ref, after_ref, edge_ref,
-    rebuilt_ref, point_ref, taps_ref, spread_ref, inputs_ref, sums_ref, wide_ref, rim_ref,
+def steps_body(
+    total, place_ref, begin_ref, step_ref, mine_ref, inner_ref, outer_ref, before_ref, first_ref,
+    second_ref, after_ref, temporal_ref, threshold_ref, out_ref, taps_ref, spread_ref, inputs_ref,
+    sums_ref, wide_ref, rim_ref, point_ref, cross_ref, mix_ref,
 ):
-    place = place_ref[0]
+    place, begin = place_ref[0], begin_ref[0]
+    rate = step_ref[0]
+    half = CHUNK // 2
     spread_taps(temporal_ref, taps_ref)
-    edge = edge_ref[...]
+
+    edge = outer_ref[:, half:]
     before = jnp.where(place == 0, edge, before_ref[...])
     after = jnp.where(place == CHUNKS - 1, edge, after_ref[...])
     second = second_ref[...]
@@ -212,59 +216,19 @@
             rows = jnp.concatenate([jnp.zeros((SEGMENT - count, 8, LANES), F32), rows], axis=0)
         return rows
 
-    rows = point_ref[...].reshape(SEGMENT, 8, LANES)
-    spread_earlier(rows, spread_ref, outside)
-    short_inputs(spread_ref, inputs_ref, 1)
-    rebuilt_ref[...] = filter_rows(inputs_ref, taps_ref, sums_ref, True).reshape(SIDE, LANES)
-
-
-def rebuild(place, temporal, activations, edge):
-    atoms, width = activations.shape
-    half = CHUNK // 2
-    last = width // half - 1
-    block = (atoms, half)
-    return pl.pallas_call(
-        rebuild_body,
-        grid_spec=pltpu.PrefetchScalarGridSpec(
-            num_scalar_prefetch=1,
-            grid=(1,),
-            in_specs=[
-                pl.BlockSpec((ATOMS, LENGTH), lambda i, place: (0, 0)),
-                pl.BlockSpec(block, lambda i, place: (0, jnp.maximum(2 * place[0] - 1, 0))),
-                pl.BlockSpec(block, lambda i, place: (0, 2 * place[0])),
-                pl.BlockSpec(block, lambda i, place: (0, 2 * place[0] + 1)),
-                pl.BlockSpec(block, lambda i, place: (0, jnp.minimum(2 * place[0] + 2, last))),
-                pl.BlockSpec(block, lambda i, place: (0, 0)),
-            ],
-            out_specs=[pl.BlockSpec((SIDE, LANES), lambda i, place: (0, 0))] * 2,
-            scratch_shapes=FILTER_SCRATCH + [pltpu.VMEM((LENGTH, LANES), F32)],
-        ),
-        out_shape=[jax.ShapeDtypeStruct((SIDE, LANES), F32)] * 2,
-        compiler_params=params(12),
-        cost_estimate=cost(2 * SIDE * LANES * LENGTH, 2**20),
-    )(place, temporal, activations, activations, activations, activations, edge)
-
-
-def steps_body(
-    total, begin_ref, half_ref, step_ref, mine_ref, inner_ref, outer_ref, rebuilt_ref, point_ref,
-    temporal_ref, threshold_ref, out_ref, taps_ref, spread_ref, inputs_ref, sums_ref, wide_ref,
-    cross_ref, mix_ref,
-):
-    begin = begin_ref[0]
-    rate = step_ref[0]
-    spread_taps(temporal_ref, taps_ref)
+    mine = mine_ref[:ATOMS]
+    first = place % 2 == 0
+    left = jnp.where(first, outer_ref[:, 128:half], inner_ref[:, 128:])
+    right = jnp.where(first, inner_ref[...], outer_ref[:, :half])
+    wide_ref[:ATOMS] = jnp.concatenate([left, mine[:, :384]], axis=1)
+    wide_ref[ATOMS:] = jnp.concatenate([mine[:, 320:], right, right[:, :64]], axis=1)
+    to_segments(wide_ref, cross_ref)
+
     gram_rows = mine_ref[ATOMS:]
     gram = jnp.concatenate([gram_rows[:, ATOMS * i : ATOMS * (i + 1)] for i in range(8)], axis=0)
     mix_ref[...] = jnp.zeros_like(mix_ref)
     mix_ref[:ATOMS, :ATOMS] = gram
     mix_ref[ATOMS:, ATOMS:] = gram
-    mine = mine_ref[:ATOMS]
-    first = half_ref[0] == 0
-    left = jnp.where(first, outer_ref[:, 128:], inner_ref[:, 128:])
-    right = jnp.where(first, inner_ref[...], outer_ref[...])
-    wide_ref[:ATOMS] = jnp.concatenate([left, mine[:, :384]], axis=1)
-    wide_ref[ATOMS:] = jnp.concatenate([mine[:, 320:], right, right[:, :64]], axis=1)
-    to_segments(wide_ref, cross_ref)
 
     shape = (SEGMENT, 8, LANES)
     sample = lax.broadcasted_iota(jnp.int32, shape, 0) + (
@@ -273,7 +237,10 @@
     shrink = threshold_ref[...]
     shrink = jnp.concatenate([shrink, shrink], axis=1).reshape(1, 1, LANES)
 
-    def projected(rebuilt):
+    def projected(point, samples_before=None):
+        spread_earlier(point, spread_ref, samples_before)
+        short_inputs(spread_ref, inputs_ref, 1)
+        rebuilt = filter_rows(inputs_ref, taps_ref, sums_ref, True).reshape(SIDE, LANES)
         mixed = jnp.dot(rebuilt, mix_ref[...], precision=HIGHEST, preferred_element_type=F32)
         rows = (mixed - cross_ref[...]).reshape(shape)
         return jnp.where(sample < total, rows, 0.0)
@@ -288,14 +255,10 @@
     inertia_next = (1.0 + (1.0 + 4.0 * inertia * inertia) ** 0.5) / 2.0
     momentum = (inertia - 1.0) / inertia_next
     previous = point_ref[...].reshape(shape)
-    update = stepped(previous, projected(rebuilt_ref[...]))
+    update = stepped(previous, projected(previous, outside))
     point = update + momentum * (update - previous)
     point = jnp.where(sample >= 0, point, 0.0)
-
-    spread_earlier(point, spread_ref)
-    short_inputs(spread_ref, inputs_ref, 1)
-    rebuilt = filter_rows(inputs_ref, taps_ref, sums_ref, True)
-    update = stepped(point, projected(rebuilt.reshape(SIDE, LANES)))
+    update = stepped(point, projected(point))
 
     cross_ref[...] = update.reshape(SIDE, LANES)
     rows = [cross_ref[pl.ds(s, SEGMENT, stride=8)] for s in range(8)]
@@ -304,20 +267,49 @@
     out_ref[...] = jnp.concatenate([columns[:ATOMS, 128:SIDE], columns[ATOMS:, :192]], axis=1)
 
 
-def steps(total, begin, half, step_size, mine, inner, outer, rebuilt, point, temporal, threshold):
+def steps(total, place, begin, step_size, mine, inner, outer, activations, temporal, threshold):
+    width = activations.shape[1]
+    half = CHUNK // 2
+    last = width // half - 1
+
     def body(*refs):
         steps_body(total, *refs)
 
+    def whole(array):
+        return pl.BlockSpec(array.shape, lambda i, place: (0, 0))
+
+    def piece(index):
+        return pl.BlockSpec((ATOMS, half), lambda i, place: (0, index(2 * place[0])))
+
     return pl.pallas_call(
         body,
-        in_specs=[SMEM] * 3 + [VMEM] * 7,
-        out_specs=VMEM,
+        grid_spec=pltpu.PrefetchScalarGridSpec(
+            num_scalar_prefetch=1,
+            grid=(1,),
+            in_specs=[SMEM, SMEM, whole(mine), whole(inner), whole(outer)]
+            + [
+                piece(lambda k: jnp.maximum(k - 1, 0)),
+                piece(lambda k: k),
+                piece(lambda k: k + 1),
+                piece(lambda k: jnp.minimum(k + 2, last)),
+            ]
+            + [whole(temporal), whole(threshold)],
+            out_specs=pl.BlockSpec((ATOMS, CHUNK), lambda i, place: (0, 0)),
+            scratch_shapes=FILTER_SCRATCH
+            + [
+                pltpu.VMEM((LENGTH, LANES), F32),
+                pltpu.VMEM((SIDE, LANES), F32),
+                pltpu.VMEM((SIDE, LANES), F32),
+                pltpu.VMEM((LANES, LANES), F32),
+            ],
+        ),
         out_shape=jax.ShapeDtypeStruct((ATOMS, CHUNK), F32),
-        scratch_shapes=FILTER_SCRATCH
-        + [pltpu.VMEM((SIDE, LANES), F32), pltpu.VMEM((LANES, LANES), F32)],
         compiler_params=params(12),
-        cost_estimate=cost(6 * SIDE * LANES * LENGTH, 2**20),
-    )(begin, half, step_size, mine, inner, outer, rebuilt, point, temporal, threshold)
+        cost_estimate=cost(8 * SIDE * LANES * LENGTH, 2**20),
+    )(
+        place, begin, step_size, mine, inner, outer, activations, activations, activations,
+        activations, temporal, threshold,
+    )
 
 
 def place_copies(half, chunks_ref, out_ref, sems):
@@ -387,23 +379,20 @@
         arrived = lax.ppermute(away, "c", swap)
         kept = project_half(half[None], spatial, signal)
         summed = kept + arrived
+        pieces = lax.all_to_all(summed, "y", 0, 0, tiled=True)
+        group_sum = jnp.sum(pieces, axis=0)
+        mine = group_sum + lax.ppermute(group_sum, "zh", swap)
+
         rim = CHUNK // 2
-        edge = jnp.where(place == 0, activations[:, :rim], activations[:, width - rim :])
-        edge, summed = lax.optimization_barrier((edge, summed))
-        pieces = lax.all_to_all(summed, "y", 0, 0, tiled=True)
-        edge = lax.ppermute(edge, line, rims)
-        rebuilt, point = rebuild(place[None], temporal, activations, edge)
-        group_sum = jnp.sum(pieces, axis=0)
-        group_sum, rebuilt, point = lax.optimization_barrier((group_sum, rebuilt, point))
-        mine = group_sum + lax.ppermute(group_sum, "zh", swap)
-
+        first = half == 0
+        edge = jnp.where(first, activations[:, :rim], activations[:, width - rim :])
         start, end = mine[:ATOMS, :rim], mine[:ATOMS, CHUNK - rim :]
-        first = half == 0
-        outer = lax.ppermute(jnp.where(first, start, end), line, outside)
+        outer = jnp.concatenate([jnp.where(first, start, end), edge], axis=1)
+        outer = lax.ppermute(outer, line, outside)
         inner = lax.ppermute(jnp.where(first, end, start), "c", swap)
         begin = time_block * width + place * CHUNK
         update = steps(
-            blocks * width, begin[None], half[None], step_size, mine, inner, outer, rebuilt, point,
+            blocks * width, place[None], begin[None], step_size, mine, inner, outer, activations,
             temporal, threshold[None, :],
         )
 

time: 86.2 us -> 88.6 us (1.028)
  the two profiles are of different devices: /device:TPU:7 before, /device:TPU:39 now
where the time goes in v4:
time: 88.6 us; the launch traced here: 88.1 us
  starting transfers between devices  34.2 us (39%)
  waiting for transfers between devices  23.7 us (27%)
  Pallas kernels  16.1 us (18%)
  blocking collectives  11.3 us (13%)
  other arithmetic  2.16 us (2%)
    ppermute x1, starting transfers between devices, per_device(): mine = group_sum + lax.ppermute(group_sum, 'zh', swap)  14.5 us
    ppermute x1, waiting for transfers between devices, per_device(): mine = group_sum + lax.ppermute(group_sum, 'zh', swap)  12.4 us
    all_gather x1, blocking collectives, per_device(): gathered = lax.all_gather(update, 'y', axis=0)  11.3 us
    all_to_all x1, waiting for transfers between devices, per_device(): pieces = lax.all_to_all(summed, 'y', 0, 0, tiled=True)  10 us
    pallas_call x1, Pallas kernels, steps(): pl.pallas_call(body, grid_spec=pltpu.PrefetchScalarGridSpec(num_scalar_pr...  7.59 us
    ppermute x1, starting transfers between devices, per_device(): other = lax.ppermute(gathered, 'c', swap)  7.11 us
    pallas_call x2, Pallas kernels, project_half(): pl.pallas_call(project_body, in_specs=[SMEM, VMEM, HBM], out_specs=VMEM,...  6.86 us
    all_to_all x1, starting transfers between devices, per_device(): pieces = lax.all_to_all(summed, 'y', 0, 0, tiled=True)  4.19 us
  transfers between devices with their start and end apart: 6, of which 4 were waited for; matrix products, arithmetic and copies ran while one was open for 0% of the time, Pallas kernels for 5%

profile of v4, /device:TPU:39, one launch (start us, length us, event | category | flops | bytes accessed | tf_op | source)
XLA Modules:
  0.0 88.1 jit_solution(14509580972020514791)
XLA Ops:
  0.0 3.4 %shard_map.65 = f32[4,72,512]{2,1,0:T(8,128)} custom-call(s32[1]{0:T(128)} %bitcast.4.half_ref, f32[64,256]{1,0:T(8,128)} %bitcast.10, bf16[256,4096]{1,0:T(8,128)(2,1)} %signal_ref.3), custom_call_target="tpu_custom_call" | custom-call | flops 134217728 | bytes 1048576 | tf_op jit(solution)/shard_map/pallas_call | solution.py:64
  3.4 2.6 %collective-permute-start = (f32[4,72,512]{2,1,0:T(8,128)}, f32[4,72,512]{2,1,0:T(8,128)S(1)}, u32[]{:S(2)}, u32[]{:S(2)}) collective-permute-start(f32[4,72,512]{2,1,0:T(8,128)} %shard_map.65), channel_id=1, source_target_pairs={{0,32},{32,0},{1,33},{33,1},{2,34},{34,2},{3,35},{35,3},{4,36},{36... | collective-permute-start | bytes 1769480 | tf_op jit(solution)/shard_map/ppermute | solution.py:379
  6.0 3.4 %shard_map.64 = f32[4,72,512]{2,1,0:T(8,128)} custom-call(s32[1]{0:T(128)} %bitcast.half_ref, f32[64,256]{1,0:T(8,128)} %bitcast.11, bf16[256,4096]{1,0:T(8,128)(2,1)} %signal_ref.3), custom_call_target="tpu_custom_call" | custom-call | flops 134217728 | bytes 1048576 | tf_op jit(solution)/shard_map/pallas_call | solution.py:64
  9.5 0.0 copy-start
  9.5 0.0 copy-start.1
  9.5 0.0 copy-start.2
  9.5 0.0 collective-permute-done
  9.5 2.1 %add.14 = f32[4,72,512]{2,1,0:T(8,128)} add(f32[4,72,512]{2,1,0:T(8,128)} %shard_map.64, f32[4,72,512]{2,1,0:T(8,128)S(1)} %collective-permute-done) | non-fusion elementwise | flops 147456 | bytes 1769472 | tf_op jit(solution)/shard_map/add | solution.py:381
  11.6 4.2 %all-to-all-start = ((f32[4,72,512]{2,1,0:T(8,128)}), f32[4,72,512]{2,1,0:T(8,128)S(1)}, u32[]{:S(2)}, u32[]{:S(2)}) async-start(f32[4,72,512]{2,1,0:T(8,128)} %add.14), calls=%async_computation | async-start | bytes 1179648 | tf_op jit(solution)/shard_map/all_to_all | solution.py:382
  15.8 10.0 %all-to-all-done = f32[4,72,512]{2,1,0:T(8,128)S(1)} async-done(((f32[4,72,512]{2,1,0:T(8,128)}), f32[4,72,512]{2,1,0:T(8,128)S(1)}, u32[]{:S(2)}, u32[]{:S(2)}) %all-to-all-start) | async-done | bytes 589856 | tf_op jit(solution)/shard_map/all_to_all | solution.py:382
  25.8 14.5 %collective-permute-start.1 = (f32[72,512]{1,0:T(8,128)S(1)}, f32[72,512]{1,0:T(8,128)S(1)}, u32[]{:S(2)}, u32[]{:S(2)}) collective-permute-start(f32[72,512]{1,0:T(8,128)S(1)} %reduce_sum.9), channel_id=1, source_target_pairs={{0,256},{256,0},{1,257},{257,1},{2,258},{258,2},{3,259},{259,3},{4... | collective-permute-start | bytes 442376 | tf_op jit(solution)/shard_map/ppermute | solution.py:384
  40.4 0.0 copy-done
  40.4 12.4 %collective-permute-done.1 = f32[72,512]{1,0:T(8,128)S(1)} collective-permute-done((f32[72,512]{1,0:T(8,128)S(1)}, f32[72,512]{1,0:T(8,128)S(1)}, u32[]{:S(2)}, u32[]{:S(2)}) %collective-permute-start.1) | collective-permute-done | bytes 147488 | tf_op jit(solution)/shard_map/ppermute | solution.py:384
  52.9 3.8 %collective-permute-start.3 = (f32[64,512]{1,0:T(8,128)S(1)}, f32[64,512]{1,0:T(8,128)S(1)}, u32[]{:S(2)}, u32[]{:S(2)}) collective-permute-start(f32[64,512]{1,0:T(8,128)S(1)} %pad_maximum_fusion), channel_id=1, source_target_pairs={{224,1},{225,2},{226,3},{227,4},{228,5},{229,6},{230,7},{231,264},... | collective-permute-start | bytes 393224 | tf_op jit(solution)/shard_map/ppermute | solution.py:391
  56.7 1.9 %collective-permute-start.2 = (f32[64,256]{1,0:T(8,128)S(1)}, f32[64,256]{1,0:T(8,128)S(1)}, u32[]{:S(2)}, u32[]{:S(2)}) collective-permute-start(f32[64,256]{1,0:T(8,128)S(1)} %get-tuple-element.6), channel_id=1, source_target_pairs={{0,32},{32,0},{1,33},{33,1},{2,34},{34,2},{3,35},{35,3},{4,36},{36... | collective-permute-start | bytes 196616 | tf_op jit(solution)/shard_map/ppermute | solution.py:392
  59.3 0.6 collective-permute-done.2.refs_4_
  59.8 0.0 collective-permute-done.3.refs_5_
  59.8 0.0 copy-done.1
  59.8 0.0 copy-done.2
  59.9 7.6 %shard_map.66 = f32[64,512]{1,0:T(8,128)S(1)} custom-call(s32[1]{0:T(128)} %bitcast.1.refs_0_, s32[1]{0:T(128)} %bitcast.2.refs_1_, f32[1]{0:T(128)S(6)} %copy.9.refs_2_, f32[72,512]{1,0:T(8,128)S(1)} %add.15.refs_3_, f32[64,256]{1,0:T(8,128)S(1)} %collective-permute-done.2.refs_4_, f32[64,512]{1,0:T(8,128)S(1)} %collective-permute-done.3.refs_5_, ...), custom_call_target="tpu_custom_call" | custom-call | flops 58720256 | bytes 1048576 | tf_op jit(solution)/shard_map/pallas_call | solution.py:284
  67.4 11.3 %all-gather = f32[256,512]{1,0:T(8,128)S(1)} all-gather(f32[64,512]{1,0:T(8,128)S(1)} %shard_map.66), channel_id=2, replica_groups=mesh['zh'=2,'y'=4,'c'=2,'tm'=32] {'y'}, dimensions={0}, use_global_device_ids=true | all-gather | bytes 655360 | tf_op jit(solution)/shard_map/all_gather | solution.py:399
  78.7 7.1 %collective-permute-start.4 = (f32[4,64,512]{2,1,0:T(8,128)S(1)}, f32[4,64,512]{2,1,0:T(8,128)S(1)}, u32[]{:S(2)}, u32[]{:S(2)}) collective-permute-start(f32[4,64,512]{2,1,0:T(8,128)S(1)} %bitcast.7), channel_id=1, source_target_pairs={{0,32},{32,0},{1,33},{33,1},{2,34},{34,2},{3,35},{35,3},{4,36},{36... | collective-permute-start | bytes 1572872 | tf_op jit(solution)/shard_map/ppermute | solution.py:400
  85.8 0.8 shard_map.67.begun_ref
  86.6 0.7 collective-permute-done.4.chunks_ref
  87.3 0.8 shard_map.68
  (5 shorter events, 0.1 us)
Async XLA Ops:
  3.4 6.1 %collective-permute-start = (f32[4,72,512]{2,1,0:T(8,128)}, f32[4,72,512]{2,1,0:T(8,128)S(1)}, u32[]{:S(2)}, u32[]{:S(2)}) collective-permute-start(f32[4,72,512]{2,1,0:T(8,128)} %shard_map.65), channel_id=1, source_target_pairs={{0,32},{32,0},{1,33},{33,1},{2,34},{34,2},{3,35},{35,3},{4,36},{36... | collective-permute-start | bytes 1769480 | tf_op jit(solution)/shard_map/ppermute | solution.py:379
  9.5 30.9 %copy-start = (f32[64,4096]{1,0:T(8,128)S(1)}, f32[64,4096]{1,0:T(8,128)}, u32[]{:S(2)}) copy-start(f32[64,4096]{1,0:T(8,128)} %refs_9_.1) | copy-start | bytes 3145732
  9.5 50.4 %copy-start.1 = (f32[64,128]{1,0:T(8,128)S(1)}, f32[64,128]{1,0:T(8,128)}, u32[]{:S(2)}) copy-start(f32[64,128]{1,0:T(8,128)} %refs_10_.1) | copy-start | bytes 98308
  9.5 50.4 %copy-start.2 = (f32[64]{0:T(128)S(1)}, f32[64]{0:T(128)}, u32[]{:S(2)}) copy-start(f32[64]{0:T(128)} %param.10) | copy-start | bytes 772
  11.6 14.2 %all-to-all-start = ((f32[4,72,512]{2,1,0:T(8,128)}), f32[4,72,512]{2,1,0:T(8,128)S(1)}, u32[]{:S(2)}, u32[]{:S(2)}) async-start(f32[4,72,512]{2,1,0:T(8,128)} %add.14), calls=%async_computation | async-start | bytes 1179648 | tf_op jit(solution)/shard_map/all_to_all | solution.py:382
  25.8 27.0 %collective-permute-start.1 = (f32[72,512]{1,0:T(8,128)S(1)}, f32[72,512]{1,0:T(8,128)S(1)}, u32[]{:S(2)}, u32[]{:S(2)}) collective-permute-start(f32[72,512]{1,0:T(8,128)S(1)} %reduce_sum.9), channel_id=1, source_target_pairs={{0,256},{256,0},{1,257},{257,1},{2,258},{258,2},{3,259},{259,3},{4... | collective-permute-start | bytes 442376 | tf_op jit(solution)/shard_map/ppermute | solution.py:384
  52.9 7.0 %collective-permute-start.3 = (f32[64,512]{1,0:T(8,128)S(1)}, f32[64,512]{1,0:T(8,128)S(1)}, u32[]{:S(2)}, u32[]{:S(2)}) collective-permute-start(f32[64,512]{1,0:T(8,128)S(1)} %pad_maximum_fusion), channel_id=1, source_target_pairs={{224,1},{225,2},{226,3},{227,4},{228,5},{229,6},{230,7},{231,264},... | collective-permute-start | bytes 393224 | tf_op jit(solution)/shard_map/ppermute | solution.py:391
  56.7 3.1 %collective-permute-start.2 = (f32[64,256]{1,0:T(8,128)S(1)}, f32[64,256]{1,0:T(8,128)S(1)}, u32[]{:S(2)}, u32[]{:S(2)}) collective-permute-start(f32[64,256]{1,0:T(8,128)S(1)} %get-tuple-element.6), channel_id=1, source_target_pairs={{0,32},{32,0},{1,33},{33,1},{2,34},{34,2},{3,35},{35,3},{4,36},{36... | collective-permute-start | bytes 196616 | tf_op jit(solution)/shard_map/ppermute | solution.py:392
  78.7 8.6 %collective-permute-start.4 = (f32[4,64,512]{2,1,0:T(8,128)S(1)}, f32[4,64,512]{2,1,0:T(8,128)S(1)}, u32[]{:S(2)}, u32[]{:S(2)}) collective-permute-start(f32[4,64,512]{2,1,0:T(8,128)S(1)} %bitcast.7), channel_id=1, source_target_pairs={{0,32},{32,0},{1,33},{33,1},{2,34},{34,2},{3,35},{35,3},{4,36},{36... | collective-permute-start | bytes 1572872 | tf_op jit(solution)/shard_map/ppermute | solution.py:400

commit v5 on v3

--- a/solution.py
+++ b/solution.py
@@ -34,45 +34,77 @@
     return pltpu.CompilerParams(vmem_limit_bytes=mebibytes * 2**20)
 
 
-def project_body(half_ref, spatial_ref, signal_ref, out_ref, block_ref, sems):
-    def fetch(i):
-        column = pl.multiple_of((2 * i + half_ref[0]) * CHUNK, CHUNK)
-        return pltpu.make_async_copy(
-            signal_ref.at[:, pl.ds(column, CHUNK)], block_ref.at[i], sems.at[i]
-        )
-
+def project_chunk(parts, signal):
+    product = jnp.dot(parts, signal, preferred_element_type=F32)
+    return product[:ATOMS] + product[ATOMS:]
+
+
+def gram_rows(parts):
+    gram = lax.dot_general(parts, parts, (((1,), (1,)), ((), ())), preferred_element_type=F32)
+    gram = gram[:ATOMS] + gram[ATOMS:]
+    gram = gram[:, :ATOMS] + gram[:, ATOMS:]
+    return jnp.concatenate([gram[8 * i : 8 * i + 8] for i in range(8)], axis=1)
+
+
+def project_away_body(half_ref, parts_ref, signal_ref, out_ref, kept_ref, block_ref, sems):
+    def fetch(i, half, target, sem):
+        column = pl.multiple_of((2 * i + half) * CHUNK, CHUNK)
+        return pltpu.make_async_copy(signal_ref.at[:, pl.ds(column, CHUNK)], target.at[i], sem)
+
+    half = half_ref[0]
+    away = [fetch(i, 1 - half, block_ref, sems.at[i]) for i in range(QUARTER)]
+    kept = [fetch(i, half, kept_ref, sems.at[QUARTER + i]) for i in range(QUARTER)]
+    for copy in away + kept:
+        copy.start()
+    parts = parts_ref[...]
+    rows = gram_rows(parts)
     for i in range(QUARTER):
-        fetch(i).start()
-    spatial = spatial_ref[...]
-    high = spatial.astype(jnp.bfloat16)
-    low = (spatial - high.astype(F32)).astype(jnp.bfloat16)
-    parts = jnp.concatenate([high, low], axis=0)
-    gram = lax.dot_general(
-        spatial, spatial, (((1,), (1,)), ((), ())), precision=HIGHEST, preferred_element_type=F32
-    )
-    gram = jnp.concatenate([gram[8 * i : 8 * i + 8] for i in range(8)], axis=1)
+        out_ref[i, ATOMS:] = rows
     for i in range(QUARTER):
-        out_ref[i, ATOMS:] = gram
+        away[i].wait()
+        out_ref[i, :ATOMS] = project_chunk(parts, block_ref[i])
+    for copy in kept:
+        copy.wait()
+
+
+def project_away(half, parts, signal):
+    channels, width = signal.shape
+    blocks = (QUARTER, channels, CHUNK)
+    return pl.pallas_call(
+        project_away_body,
+        in_specs=[SMEM, VMEM, HBM],
+        out_specs=[VMEM, VMEM],
+        out_shape=[
+            jax.ShapeDtypeStruct((QUARTER, ROWS, CHUNK), F32),
+            jax.ShapeDtypeStruct(blocks, jnp.bfloat16),
+        ],
+        scratch_shapes=[
+            pltpu.VMEM(blocks, jnp.bfloat16),
+            pltpu.SemaphoreType.DMA((2 * QUARTER,)),
+        ],
+        compiler_params=params(8),
+        cost_estimate=cost(channels * LANES * width, 2 * channels * width),
+    )(half, parts, signal)
+
+
+def project_kept_body(parts_ref, signal_ref, out_ref):
+    parts = parts_ref[...]
+    rows = gram_rows(parts)
     for i in range(QUARTER):
-        fetch(i).wait()
-        product = jnp.dot(parts, block_ref[i], preferred_element_type=F32)
-        out_ref[i, :ATOMS] = product[:ATOMS] + product[ATOMS:]
-
-
-def project_half(half, spatial, signal):
-    channels, width = signal.shape
+        out_ref[i, ATOMS:] = rows
+        out_ref[i, :ATOMS] = project_chunk(parts, signal_ref[i])
+
+
+def project_kept(parts, signal):
+    count, channels, width = signal.shape
     return pl.pallas_call(
-        project_body,
-        in_specs=[SMEM, VMEM, HBM],
+        project_kept_body,
+        in_specs=[VMEM, VMEM],
         out_specs=VMEM,
         out_shape=jax.ShapeDtypeStruct((QUARTER, ROWS, CHUNK), F32),
-        scratch_shapes=[
-            pltpu.VMEM((QUARTER, channels, CHUNK), jnp.bfloat16),
-            pltpu.SemaphoreType.DMA((QUARTER,)),
-        ],
         compiler_params=params(8),
-        cost_estimate=cost(2 * channels * LANES * width // 2, channels * width),
-    )(half, spatial, signal)
+        cost_estimate=cost(2 * channels * LANES * count * width, channels * count * width),
+    )(parts, signal)
 
 
 def to_segments(wide_ref, out_ref):
@@ -382,23 +414,26 @@
         time_block = lax.axis_index("tm").astype(jnp.int32)
         width = activations.shape[1]
         spatial = spatial.T
-
-        away = project_half((1 - half)[None], spatial, signal)
+        high = lax.reduce_precision(spatial, 8, 7)
+        parts = jnp.concatenate([high, spatial - high], axis=0).astype(jnp.bfloat16)
+
+        away, kept_signal = project_away(half[None], parts, signal)
         arrived = lax.ppermute(away, "c", swap)
-        kept = project_half(half[None], spatial, signal)
-        summed = kept + arrived
+        kept = project_kept(parts, kept_signal)
+        pieces = lax.all_to_all(kept + arrived, "y", 0, 0, tiled=True)
+        group_sum = jnp.sum(pieces, axis=0)
+
         rim = CHUNK // 2
-        edge = jnp.where(place == 0, activations[:, :rim], activations[:, width - rim :])
-        edge, summed = lax.optimization_barrier((edge, summed))
-        pieces = lax.all_to_all(summed, "y", 0, 0, tiled=True)
+        first = half == 0
+        activations, group_sum = lax.optimization_barrier((activations, group_sum))
+        edge = jnp.where(first, activations[:, :rim], activations[:, width - rim :])
+        other_sum = lax.ppermute(group_sum, "zh", swap)
         edge = lax.ppermute(edge, line, rims)
         rebuilt, point = rebuild(place[None], temporal, activations, edge)
-        group_sum = jnp.sum(pieces, axis=0)
-        group_sum, rebuilt, point = lax.optimization_barrier((group_sum, rebuilt, point))
-        mine = group_sum + lax.ppermute(group_sum, "zh", swap)
+        rebuilt, point, other_sum = lax.optimization_barrier((rebuilt, point, other_sum))
+        mine = group_sum + other_sum
 
         start, end = mine[:ATOMS, :rim], mine[:ATOMS, CHUNK - rim :]
-        first = half == 0
         outer = lax.ppermute(jnp.where(first, start, end), line, outside)
         inner = lax.ppermute(jnp.where(first, end, start), "c", swap)
         begin = time_block * width + place * CHUNK

time: 86.2 us -> 89.9 us (1.043)
  starting transfers between devices: 47.1 us -> 52.3 us
  local copies, waits for them, and re-layouts: 4.04 us -> 1.61 us
    ppermute x1, starting transfers between devices: 3.94 us -> 11.3 us  [per_device(): outer = lax.ppermute(jnp.where(first, start, end), line, outside)]
    ppermute x1, waiting for transfers between devices: 2.81 us -> 0.25 us  [per_device(): other_sum = lax.ppermute(group_sum, 'zh', swap)]
    unnamed x14 -> x8, local copies, waits for them, and re-layouts: 4.04 us -> 1.61 us
    all_to_all x1, waiting for transfers between devices: 7.5 us -> 9.61 us  [per_device(): pieces = lax.all_to_all(kept + arrived, 'y', 0, 0, tiled=True)]
    ppermute x1, starting transfers between devices: 13.8 us -> 12.4 us  [per_device(): inner = lax.ppermute(jnp.where(first, end, start), 'c', swap)]
    ppermute x1, waiting for transfers between devices: 0.01 us -> 1.24 us  [per_device(): arrived = lax.ppermute(away, 'c', swap)]
  transfers between devices with their start and end apart: 7 -> 7, of which waited for: 4 -> 5; matrix products, arithmetic and copies ran while one was open for 0% -> 0% of each run, Pallas kernels for 4% -> 3%
where the time goes in v5:
time: 89.9 us; the launch traced here: 89.5 us
  starting transfers between devices  52.3 us (58%)
  waiting for transfers between devices  12 us (13%)
  Pallas kernels  10.9 us (12%)
  blocking collectives  9.9 us (11%)
  other arithmetic  1.86 us (2%)
  local copies, waits for them, and re-layouts  1.61 us (2%)
    ppermute x1, starting transfers between devices, per_device(): other_sum = lax.ppermute(group_sum, 'zh', swap)  15.4 us
    ppermute x1, starting transfers between devices, per_device(): inner = lax.ppermute(jnp.where(first, end, start), 'c', swap)  12.4 us
    ppermute x1, starting transfers between devices, per_device(): outer = lax.ppermute(jnp.where(first, start, end), line, outside)  11.3 us
    all_gather x1, blocking collectives, per_device(): gathered = lax.all_gather(update, 'y', axis=0)  9.9 us
    all_to_all x1, waiting for transfers between devices, per_device(): pieces = lax.all_to_all(kept + arrived, 'y', 0, 0, tiled=True)  9.61 us
    pallas_call x1, Pallas kernels, steps(): pl.pallas_call(body, in_specs=[SMEM] * 3 + [VMEM] * 7, out_specs=VMEM, ou...  5.79 us
    ppermute x1, starting transfers between devices, per_device(): other = lax.ppermute(gathered, 'c', swap)  5.77 us
    all_to_all x1, starting transfers between devices, per_device(): pieces = lax.all_to_all(kept + arrived, 'y', 0, 0, tiled=True)  4.18 us
  transfers between devices with their start and end apart: 7, of which 5 were waited for; matrix products, arithmetic and copies ran while one was open for 0% of the time, Pallas kernels for 3%

profile of v5, /device:TPU:7, one launch (start us, length us, event | category | flops | bytes accessed | tf_op | source)
XLA Modules:
  0.0 89.5 jit_solution(3453345271981902853)
XLA Ops:
  0.0 0.8 reduce-precision_convert_fusion
  0.9 0.0 copy-start.1
  0.9 1.6 %copy-done.1 = bf16[256,4096]{1,0:T(8,128)(2,1)S(1)} copy-done((bf16[256,4096]{1,0:T(8,128)(2,1)S(1)}, bf16[256,4096]{1,0:T(8,128)(2,1)}, u32[]{:S(2)}) %copy-start.1) | copy-done | bytes 2097176
  2.5 1.3 %shard_map.64 = (f32[4,72,512]{2,1,0:T(8,128)S(1)}, bf16[4,256,512]{2,1,0:T(8,128)(2,1)S(1)}) custom-call(s32[1]{0:T(128)} %bitcast.half_ref.refs_1_, bf16[128,256]{1,0:T(8,128)(2,1)S(1)} %pad_maximum_fusion.parts_ref, bf16[256,4096]{1,0:T(8,128)(2,1)S(1)} %copy-done.1), custom_call_target="tpu_custom_call" | custom-call | flops 134217728 | bytes 2097152 | tf_op jit(solution)/shard_map/pallas_call | solution.py:73
  3.8 2.6 %collective-permute-start = (f32[4,72,512]{2,1,0:T(8,128)S(1)}, f32[4,72,512]{2,1,0:T(8,128)S(1)}, u32[]{:S(2)}, u32[]{:S(2)}) collective-permute-start(f32[4,72,512]{2,1,0:T(8,128)S(1)} %get-tuple-element.15), channel_id=1, source_target_pairs={{0,32},{32,0},{1,33},{33,1},{2,34},{34,2},{3,35},{35,3},{4,36},{36... | collective-permute-start | bytes 1769480 | tf_op jit(solution)/shard_map/ppermute | solution.py:421
  6.4 0.3 shard_map.65
  6.7 0.0 copy-start
  6.8 0.0 copy-start.2
  6.8 1.2 %collective-permute-done = f32[4,72,512]{2,1,0:T(8,128)S(1)} collective-permute-done((f32[4,72,512]{2,1,0:T(8,128)S(1)}, f32[4,72,512]{2,1,0:T(8,128)S(1)}, u32[]{:S(2)}, u32[]{:S(2)}) %collective-permute-start) | collective-permute-done | bytes 589856 | tf_op jit(solution)/shard_map/ppermute | solution.py:421
  8.0 0.9 %add.14 = f32[4,72,512]{2,1,0:T(8,128)} add(f32[4,72,512]{2,1,0:T(8,128)S(1)} %shard_map.65, f32[4,72,512]{2,1,0:T(8,128)S(1)} %collective-permute-done) | non-fusion elementwise | flops 147456 | bytes 1769472 | tf_op jit(solution)/shard_map/add | solution.py:423
  8.9 4.2 %all-to-all-start = ((f32[4,72,512]{2,1,0:T(8,128)}), f32[4,72,512]{2,1,0:T(8,128)S(1)}, u32[]{:S(2)}, u32[]{:S(2)}) async-start(f32[4,72,512]{2,1,0:T(8,128)} %add.14), calls=%async_computation | async-start | bytes 1179648 | tf_op jit(solution)/shard_map/all_to_all | solution.py:423
  13.1 9.6 %all-to-all-done = f32[4,72,512]{2,1,0:T(8,128)S(1)} async-done(((f32[4,72,512]{2,1,0:T(8,128)}), f32[4,72,512]{2,1,0:T(8,128)S(1)}, u32[]{:S(2)}, u32[]{:S(2)}) %all-to-all-start) | async-done | bytes 589856 | tf_op jit(solution)/shard_map/all_to_all | solution.py:423
  22.8 15.4 %collective-permute-start.2 = (f32[72,512]{1,0:T(8,128)S(1)}, f32[72,512]{1,0:T(8,128)S(1)}, u32[]{:S(2)}, u32[]{:S(2)}) collective-permute-start(f32[72,512]{1,0:T(8,128)S(1)} %reduce_sum.9), channel_id=1, source_target_pairs={{0,256},{256,0},{1,257},{257,1},{2,258},{258,2},{3,259},{259,3},{4... | collective-permute-start | bytes 442376 | tf_op jit(solution)/shard_map/ppermute | solution.py:430
  38.2 0.0 copy-done
  38.2 0.7 collective-permute-start.1
  38.9 0.0 collective-permute-done.1.edge_ref
  38.9 0.0 copy-done.2
  38.9 0.0 copy-start.3
  39.0 1.8 %shard_map.66 = (f32[448,128]{1,0:T(8,128)S(1)}, f32[448,128]{1,0:T(8,128)S(1)}) custom-call(s32[1]{0:T(128)} %bitcast.3.place_ref, f32[64,128]{1,0:T(8,128)S(1)} %copy-done.2, f32[64,4096]{1,0:T(8,128)S(1)} %copy-done, f32[64,4096]{1,0:T(8,128)S(1)} %copy-done, f32[64,4096]{1,0:T(8,128)S(1)} %copy-done, f32[64,4096]{1,0:T(8,128)S(1)} %copy-done, ...), custom_call_target="tpu_custom_call" | custom-call | flops 14680064 | bytes 1048576 | tf_op jit(solution)/shard_map/pallas_call | solution.py:258
  40.8 0.2 collective-permute-done.2
  41.1 11.3 %collective-permute-start.4 = (f32[64,256]{1,0:T(8,128)S(1)}, f32[64,256]{1,0:T(8,128)S(1)}, u32[]{:S(2)}, u32[]{:S(2)}) collective-permute-start(f32[64,256]{1,0:T(8,128)S(1)} %get-tuple-element.23), channel_id=1, source_target_pairs={{224,1},{225,2},{226,3},{227,4},{228,5},{229,6},{230,7},{231,264},... | collective-permute-start | bytes 196616 | tf_op jit(solution)/shard_map/ppermute | solution.py:437
  52.4 12.4 %collective-permute-start.3 = (f32[64,256]{1,0:T(8,128)S(1)}, f32[64,256]{1,0:T(8,128)S(1)}, u32[]{:S(2)}, u32[]{:S(2)}) collective-permute-start(f32[64,256]{1,0:T(8,128)S(1)} %get-tuple-element.24), channel_id=1, source_target_pairs={{0,32},{32,0},{1,33},{33,1},{2,34},{34,2},{3,35},{35,3},{4,36},{36... | collective-permute-start | bytes 196616 | tf_op jit(solution)/shard_map/ppermute | solution.py:438
  65.4 0.0 collective-permute-done.4.refs_5_
  65.4 0.2 collective-permute-done.3.refs_4_
  65.7 0.0 copy-done.3
  65.7 5.8 %shard_map.67 = f32[64,512]{1,0:T(8,128)S(1)} custom-call(s32[1]{0:T(128)} %bitcast.1.refs_0_, s32[1]{0:T(128)} %bitcast.half_ref.refs_1_, f32[1]{0:T(128)S(6)} %copy.9.refs_2_, f32[72,512]{1,0:T(8,128)S(1)} %add.15.refs_3_, f32[64,256]{1,0:T(8,128)S(1)} %collective-permute-done.3.refs_4_, f32[64,256]{1,0:T(8,128)S(1)} %collective-permute-done.4.refs_5_, ...), custom_call_target="tpu_custom_call" | custom-call | flops 44040192 | bytes 1048576 | tf_op jit(solution)/shard_map/pallas_call | solution.py:343
  71.5 9.9 %all-gather = f32[256,512]{1,0:T(8,128)S(1)} all-gather(f32[64,512]{1,0:T(8,128)S(1)} %shard_map.67), channel_id=2, replica_groups=mesh['zh'=2,'y'=4,'c'=2,'tm'=32] {'y'}, dimensions={0}, use_global_device_ids=true | all-gather | bytes 655360 | tf_op jit(solution)/shard_map/all_gather | solution.py:445
  81.4 5.8 %collective-permute-start.5 = (f32[4,64,512]{2,1,0:T(8,128)S(1)}, f32[4,64,512]{2,1,0:T(8,128)S(1)}, u32[]{:S(2)}, u32[]{:S(2)}) collective-permute-start(f32[4,64,512]{2,1,0:T(8,128)S(1)} %bitcast.8), channel_id=1, source_target_pairs={{0,32},{32,0},{1,33},{33,1},{2,34},{34,2},{3,35},{35,3},{4,36},{36... | collective-permute-start | bytes 1572872 | tf_op jit(solution)/shard_map/ppermute | solution.py:446
  87.1 0.8 shard_map.68.begun_ref
  88.0 0.7 collective-permute-done.5.chunks_ref
  88.7 0.8 shard_map.69
  (5 shorter events, 0.1 us)
Async XLA Ops:
  0.9 1.6 %copy-start.1 = (bf16[256,4096]{1,0:T(8,128)(2,1)S(1)}, bf16[256,4096]{1,0:T(8,128)(2,1)}, u32[]{:S(2)}) copy-start(bf16[256,4096]{1,0:T(8,128)(2,1)} %signal_ref.1) | copy-start | bytes 6291460
  3.8 4.2 %collective-permute-start = (f32[4,72,512]{2,1,0:T(8,128)S(1)}, f32[4,72,512]{2,1,0:T(8,128)S(1)}, u32[]{:S(2)}, u32[]{:S(2)}) collective-permute-start(f32[4,72,512]{2,1,0:T(8,128)S(1)} %get-tuple-element.15), channel_id=1, source_target_pairs={{0,32},{32,0},{1,33},{33,1},{2,34},{34,2},{3,35},{35,3},{4,36},{36... | collective-permute-start | bytes 1769480 | tf_op jit(solution)/shard_map/ppermute | solution.py:421
  6.7 31.5 %copy-start = (f32[64,4096]{1,0:T(8,128)S(1)}, f32[64,4096]{1,0:T(8,128)}, u32[]{:S(2)}) copy-start(f32[64,4096]{1,0:T(8,128)} %after_ref) | copy-start | bytes 3145732
  6.8 32.2 %copy-start.2 = (f32[64,128]{1,0:T(8,128)S(1)}, f32[64,128]{1,0:T(8,128)}, u32[]{:S(2)}) copy-start(f32[64,128]{1,0:T(8,128)} %refs_8_.1) | copy-start | bytes 98308
  8.9 13.8 %all-to-all-start = ((f32[4,72,512]{2,1,0:T(8,128)}), f32[4,72,512]{2,1,0:T(8,128)S(1)}, u32[]{:S(2)}, u32[]{:S(2)}) async-start(f32[4,72,512]{2,1,0:T(8,128)} %add.14), calls=%async_computation | async-start | bytes 1179648 | tf_op jit(solution)/shard_map/all_to_all | solution.py:423
  22.8 18.3 %collective-permute-start.2 = (f32[72,512]{1,0:T(8,128)S(1)}, f32[72,512]{1,0:T(8,128)S(1)}, u32[]{:S(2)}, u32[]{:S(2)}) collective-permute-start(f32[72,512]{1,0:T(8,128)S(1)} %reduce_sum.9), channel_id=1, source_target_pairs={{0,256},{256,0},{1,257},{257,1},{2,258},{258,2},{3,259},{259,3},{4... | collective-permute-start | bytes 442376 | tf_op jit(solution)/shard_map/ppermute | solution.py:430
  38.2 0.7 collective-permute-start.1
  38.9 26.7 %copy-start.3 = (f32[64]{0:T(128)S(1)}, f32[64]{0:T(128)}, u32[]{:S(2)}) copy-start(f32[64]{0:T(128)} %param.10) | copy-start | bytes 772
  41.1 24.4 %collective-permute-start.4 = (f32[64,256]{1,0:T(8,128)S(1)}, f32[64,256]{1,0:T(8,128)S(1)}, u32[]{:S(2)}, u32[]{:S(2)}) collective-permute-start(f32[64,256]{1,0:T(8,128)S(1)} %get-tuple-element.23), channel_id=1, source_target_pairs={{224,1},{225,2},{226,3},{227,4},{228,5},{229,6},{230,7},{231,264},... | collective-permute-start | bytes 196616 | tf_op jit(solution)/shard_map/ppermute | solution.py:437
  52.4 13.2 %collective-permute-start.3 = (f32[64,256]{1,0:T(8,128)S(1)}, f32[64,256]{1,0:T(8,128)S(1)}, u32[]{:S(2)}, u32[]{:S(2)}) collective-permute-start(f32[64,256]{1,0:T(8,128)S(1)} %get-tuple-element.24), channel_id=1, source_target_pairs={{0,32},{32,0},{1,33},{33,1},{2,34},{34,2},{3,35},{35,3},{4,36},{36... | collective-permute-start | bytes 196616 | tf_op jit(solution)/shard_map/ppermute | solution.py:438
  81.4 7.3 %collective-permute-start.5 = (f32[4,64,512]{2,1,0:T(8,128)S(1)}, f32[4,64,512]{2,1,0:T(8,128)S(1)}, u32[]{:S(2)}, u32[]{:S(2)}) collective-permute-start(f32[4,64,512]{2,1,0:T(8,128)S(1)} %bitcast.8), channel_id=1, source_target_pairs={{0,32},{32,0},{1,33},{33,1},{2,34},{34,2},{3,35},{35,3},{4,36},{36... | collective-permute-start | bytes 1572872 | tf_op jit(solution)/shard_map/ppermute | solution.py:446

commit v6 on v5

--- a/solution.py
+++ b/solution.py
@@ -22,7 +22,6 @@
 VMEM = pl.BlockSpec(memory_space=pltpu.VMEM)
 SMEM = pl.BlockSpec(memory_space=pltpu.SMEM)
 ANY = pl.BlockSpec(memory_space=pl.ANY)
-HBM = pl.BlockSpec(memory_space=pltpu.HBM)
 RUN = 8
 
 
@@ -46,65 +45,27 @@
     return jnp.concatenate([gram[8 * i : 8 * i + 8] for i in range(8)], axis=1)
 
 
-def project_away_body(half_ref, parts_ref, signal_ref, out_ref, kept_ref, block_ref, sems):
-    def fetch(i, half, target, sem):
-        column = pl.multiple_of((2 * i + half) * CHUNK, CHUNK)
-        return pltpu.make_async_copy(signal_ref.at[:, pl.ds(column, CHUNK)], target.at[i], sem)
-
+def project_body(half_ref, parts_ref, signal_ref, away_ref, kept_ref):
     half = half_ref[0]
-    away = [fetch(i, 1 - half, block_ref, sems.at[i]) for i in range(QUARTER)]
-    kept = [fetch(i, half, kept_ref, sems.at[QUARTER + i]) for i in range(QUARTER)]
-    for copy in away + kept:
-        copy.start()
     parts = parts_ref[...]
     rows = gram_rows(parts)
-    for i in range(QUARTER):
-        out_ref[i, ATOMS:] = rows
-    for i in range(QUARTER):
-        away[i].wait()
-        out_ref[i, :ATOMS] = project_chunk(parts, block_ref[i])
-    for copy in kept:
-        copy.wait()
-
-
-def project_away(half, parts, signal):
+    for out_ref, which in ((away_ref, 1 - half), (kept_ref, half)):
+        for i in range(QUARTER):
+            column = pl.multiple_of((2 * i + which) * CHUNK, CHUNK)
+            out_ref[i, :ATOMS] = project_chunk(parts, signal_ref[:, pl.ds(column, CHUNK)])
+            out_ref[i, ATOMS:] = rows
+
+
+def project(half, parts, signal):
     channels, width = signal.shape
-    blocks = (QUARTER, channels, CHUNK)
     return pl.pallas_call(
-        project_away_body,
-        in_specs=[SMEM, VMEM, HBM],
+        project_body,
+        in_specs=[SMEM, VMEM, VMEM],
         out_specs=[VMEM, VMEM],
-        out_shape=[
-            jax.ShapeDtypeStruct((QUARTER, ROWS, CHUNK), F32),
-            jax.ShapeDtypeStruct(blocks, jnp.bfloat16),
-        ],
-        scratch_shapes=[
-            pltpu.VMEM(blocks, jnp.bfloat16),
-            pltpu.SemaphoreType.DMA((2 * QUARTER,)),
-        ],
+        out_shape=[jax.ShapeDtypeStruct((QUARTER, ROWS, CHUNK), F32)] * 2,
         compiler_params=params(8),
-        cost_estimate=cost(channels * LANES * width, 2 * channels * width),
+        cost_estimate=cost(2 * channels * LANES * width, 2 * channels * width),
     )(half, parts, signal)
-
-
-def project_kept_body(parts_ref, signal_ref, out_ref):
-    parts = parts_ref[...]
-    rows = gram_rows(parts)
-    for i in range(QUARTER):
-        out_ref[i, ATOMS:] = rows
-        out_ref[i, :ATOMS] = project_chunk(parts, signal_ref[i])
-
-
-def project_kept(parts, signal):
-    count, channels, width = signal.shape
-    return pl.pallas_call(
-        project_kept_body,
-        in_specs=[VMEM, VMEM],
-        out_specs=VMEM,
-        out_shape=jax.ShapeDtypeStruct((QUARTER, ROWS, CHUNK), F32),
-        compiler_params=params(8),
-        cost_estimate=cost(2 * channels * LANES * count * width, channels * count * width),
-    )(parts, signal)
 
 
 def to_segments(wide_ref, out_ref):
@@ -417,21 +378,19 @@
         high = lax.reduce_precision(spatial, 8, 7)
         parts = jnp.concatenate([high, spatial - high], axis=0).astype(jnp.bfloat16)
 
-        away, kept_signal = project_away(half[None], parts, signal)
-        arrived = lax.ppermute(away, "c", swap)
-        kept = project_kept(parts, kept_signal)
-        pieces = lax.all_to_all(kept + arrived, "y", 0, 0, tiled=True)
-        group_sum = jnp.sum(pieces, axis=0)
+        away, kept = project(half[None], parts, signal)
+        summed = kept + lax.ppermute(away, "c", swap)
 
         rim = CHUNK // 2
         first = half == 0
-        activations, group_sum = lax.optimization_barrier((activations, group_sum))
+        activations, summed = lax.optimization_barrier((activations, summed))
         edge = jnp.where(first, activations[:, :rim], activations[:, width - rim :])
-        other_sum = lax.ppermute(group_sum, "zh", swap)
+        pieces = lax.all_to_all(summed, "y", 0, 0, tiled=True)
         edge = lax.ppermute(edge, line, rims)
         rebuilt, point = rebuild(place[None], temporal, activations, edge)
-        rebuilt, point, other_sum = lax.optimization_barrier((rebuilt, point, other_sum))
-        mine = group_sum + other_sum
+        group_sum = jnp.sum(pieces, axis=0)
+        group_sum, rebuilt, point = lax.optimization_barrier((group_sum, rebuilt, point))
+        mine = jnp.sum(lax.all_gather(group_sum, "zh", axis=0), axis=0)
 
         start, end = mine[:ATOMS, :rim], mine[:ATOMS, CHUNK - rim :]
         outer = lax.ppermute(jnp.where(first, start, end), line, outside)

time: 89.9 us -> 82.6 us (0.919)
  starting transfers between devices: 52.3 us -> 31.8 us
  blocking collectives: 9.9 us -> 26.9 us
  waiting for transfers between devices: 12 us -> 9.56 us
  Pallas kernels: 10.9 us -> 9.72 us
    all_gather x0 -> x1, blocking collectives: none -> 17 us  [per_device(): mine = jnp.sum(lax.all_gather(group_sum, 'zh', axis=0), axis=0)]
    ppermute x2 -> x1, starting transfers between devices: 18 us -> 2.59 us  [per_device(): summed = kept + lax.ppermute(away, 'c', swap)]
    ppermute x1, starting transfers between devices: 12.4 us -> 7.17 us  [per_device(): inner = lax.ppermute(jnp.where(first, end, start), 'c', swap)]
    all_to_all x1, waiting for transfers between devices: 9.61 us -> 7.05 us  [per_device(): pieces = lax.all_to_all(summed, 'y', 0, 0, tiled=True)]
    pallas_call x2 -> x1, Pallas kernels: 1.68 us -> 0.47 us  [project(): pl.pallas_call(project_body, in_specs=[SMEM, VMEM, VMEM], out_specs=[VMEM...]
  transfers between devices with their start and end apart: 7 -> 6, of which waited for: 5 -> 4; matrix products, arithmetic and copies ran while one was open for 0% -> 0% of each run, Pallas kernels for 3% -> 3%
where the time goes in v6:
time: 82.6 us; the launch traced here: 82.2 us
  starting transfers between devices  31.8 us (38%)
  blocking collectives  26.9 us (33%)
  Pallas kernels  9.72 us (12%)
  waiting for transfers between devices  9.56 us (12%)
  other arithmetic  1.85 us (2%)
  local copies, waits for them, and re-layouts  1.6 us (2%)
    all_gather x1, blocking collectives, per_device(): mine = jnp.sum(lax.all_gather(group_sum, 'zh', axis=0), axis=0)  17 us
    ppermute x1, starting transfers between devices, per_device(): outer = lax.ppermute(jnp.where(first, start, end), line, outside)  11.4 us
    all_gather x1, blocking collectives, per_device(): gathered = lax.all_gather(update, 'y', axis=0)  9.9 us
    ppermute x1, starting transfers between devices, per_device(): inner = lax.ppermute(jnp.where(first, end, start), 'c', swap)  7.17 us
    all_to_all x1, waiting for transfers between devices, per_device(): pieces = lax.all_to_all(summed, 'y', 0, 0, tiled=True)  7.05 us
    pallas_call x1, Pallas kernels, steps(): pl.pallas_call(body, in_specs=[SMEM] * 3 + [VMEM] * 7, out_specs=VMEM, ou...  5.79 us
    ppermute x1, starting transfers between devices, per_device(): other = lax.ppermute(gathered, 'c', swap)  5.77 us
    all_to_all x1, starting transfers between devices, per_device(): pieces = lax.all_to_all(summed, 'y', 0, 0, tiled=True)  4.18 us
  transfers between devices with their start and end apart: 6, of which 4 were waited for; matrix products, arithmetic and copies ran while one was open for 0% of the time, Pallas kernels for 3%

profile of v6, /device:TPU:7, one launch (start us, length us, event | category | flops | bytes accessed | tf_op | source)
XLA Modules:
  0.0 82.2 jit_solution(15940370024113252405)
XLA Ops:
  0.0 0.8 %reduce-precision_convert_fusion = (bf16[64,256]{1,0:T(8,128)(2,1)S(1)}, bf16[64,256]{1,0:T(8,128)(2,1)S(1)}) fusion(f32[256,64]{0,1:T(8,128)} %param.7), kind=kLoop, calls=%fused_computation.1 | loop fusion | flops 65536 | bytes 131072 | tf_op jit(solution)/shard_map/convert
  0.9 0.0 copy-start.1
  0.9 1.6 %copy-done.1 = bf16[256,4096]{1,0:T(8,128)(2,1)S(1)} copy-done((bf16[256,4096]{1,0:T(8,128)(2,1)S(1)}, bf16[256,4096]{1,0:T(8,128)(2,1)}, u32[]{:S(2)}) %copy-start.1) | copy-done | bytes 2097176
  2.5 0.0 copy-start
  2.5 0.5 shard_map.64
  2.9 0.0 copy-start.2
  3.0 2.6 %collective-permute-start = (f32[4,72,512]{2,1,0:T(8,128)S(1)}, f32[4,72,512]{2,1,0:T(8,128)S(1)}, u32[]{:S(2)}, u32[]{:S(2)}) collective-permute-start(f32[4,72,512]{2,1,0:T(8,128)S(1)} %get-tuple-element.15), channel_id=1, source_target_pairs={{0,32},{32,0},{1,33},{33,1},{2,34},{34,2},{3,35},{35,3},{4,36},{36... | collective-permute-start | bytes 1769480 | tf_op jit(solution)/shard_map/ppermute | solution.py:382
  5.5 1.6 %collective-permute-done = f32[4,72,512]{2,1,0:T(8,128)S(1)} collective-permute-done((f32[4,72,512]{2,1,0:T(8,128)S(1)}, f32[4,72,512]{2,1,0:T(8,128)S(1)}, u32[]{:S(2)}, u32[]{:S(2)}) %collective-permute-start) | collective-permute-done | bytes 589856 | tf_op jit(solution)/shard_map/ppermute | solution.py:382
  7.2 0.9 %add.11 = f32[4,72,512]{2,1,0:T(8,128)} add(f32[4,72,512]{2,1,0:T(8,128)S(1)} %get-tuple-element.14, f32[4,72,512]{2,1,0:T(8,128)S(1)} %collective-permute-done) | non-fusion elementwise | flops 147456 | bytes 1769472 | tf_op jit(solution)/shard_map/add | solution.py:382
  8.1 4.2 %all-to-all-start = ((f32[4,72,512]{2,1,0:T(8,128)}), f32[4,72,512]{2,1,0:T(8,128)S(1)}, u32[]{:S(2)}, u32[]{:S(2)}) async-start(f32[4,72,512]{2,1,0:T(8,128)} %add.11), calls=%async_computation | async-start | bytes 1179648 | tf_op jit(solution)/shard_map/all_to_all | solution.py:388
  12.2 0.0 copy-done
  12.3 0.7 collective-permute-start.1
  12.9 0.0 collective-permute-done.1.edge_ref
  13.0 0.0 copy-done.2
  13.0 0.0 copy-start.3
  13.0 1.8 %shard_map.65 = (f32[448,128]{1,0:T(8,128)S(1)}, f32[448,128]{1,0:T(8,128)S(1)}) custom-call(s32[1]{0:T(128)} %bitcast.3.place_ref, f32[64,128]{1,0:T(8,128)S(1)} %copy-done.2, f32[64,4096]{1,0:T(8,128)S(1)} %copy-done, f32[64,4096]{1,0:T(8,128)S(1)} %copy-done, f32[64,4096]{1,0:T(8,128)S(1)} %copy-done, f32[64,4096]{1,0:T(8,128)S(1)} %copy-done, ...), custom_call_target="tpu_custom_call" | custom-call | flops 14680064 | bytes 1048576 | tf_op jit(solution)/shard_map/pallas_call | solution.py:219
  14.8 7.0 %all-to-all-done = f32[4,72,512]{2,1,0:T(8,128)S(1)} async-done(((f32[4,72,512]{2,1,0:T(8,128)}), f32[4,72,512]{2,1,0:T(8,128)S(1)}, u32[]{:S(2)}, u32[]{:S(2)}) %all-to-all-start) | async-done | bytes 589856 | tf_op jit(solution)/shard_map/all_to_all | solution.py:388
  21.9 17.0 %all-gather = f32[144,512]{1,0:T(8,128)S(1)} all-gather(f32[72,512]{1,0:T(8,128)S(1)} %reduce_sum.18), channel_id=2, replica_groups=mesh['zh'=2,'y'=4,'c'=2,'tm'=32] {'zh'}, dimensions={0}, use_global_device_ids=true | all-gather | bytes 442368 | tf_op jit(solution)/shard_map/all_gather | solution.py:393
  39.0 11.4 %collective-permute-start.3 = (f32[64,256]{1,0:T(8,128)S(1)}, f32[64,256]{1,0:T(8,128)S(1)}, u32[]{:S(2)}, u32[]{:S(2)}) collective-permute-start(f32[64,256]{1,0:T(8,128)S(1)} %get-tuple-element.23), channel_id=1, source_target_pairs={{224,1},{225,2},{226,3},{227,4},{228,5},{229,6},{230,7},{231,264},... | collective-permute-start | bytes 196616 | tf_op jit(solution)/shard_map/ppermute | solution.py:396
  50.4 7.2 %collective-permute-start.2 = (f32[64,256]{1,0:T(8,128)S(1)}, f32[64,256]{1,0:T(8,128)S(1)}, u32[]{:S(2)}, u32[]{:S(2)}) collective-permute-start(f32[64,256]{1,0:T(8,128)S(1)} %get-tuple-element.24), channel_id=1, source_target_pairs={{0,32},{32,0},{1,33},{33,1},{2,34},{34,2},{3,35},{35,3},{4,36},{36... | collective-permute-start | bytes 196616 | tf_op jit(solution)/shard_map/ppermute | solution.py:397
  58.2 0.0 collective-permute-done.3.refs_5_
  58.2 0.2 collective-permute-done.2.refs_4_
  58.4 0.0 copy-done.3
  58.4 5.8 %shard_map.66 = f32[64,512]{1,0:T(8,128)S(1)} custom-call(s32[1]{0:T(128)} %bitcast.1.refs_0_, s32[1]{0:T(128)} %bitcast.half_ref.refs_1_, f32[1]{0:T(128)S(6)} %copy.9.refs_2_, f32[72,512]{1,0:T(8,128)S(1)} %reduce_sum.19.refs_3_, f32[64,256]{1,0:T(8,128)S(1)} %collective-permute-done.2.refs_4_, f32[64,256]{1,0:T(8,128)S(1)} %collective-permute-done.3.refs_5_, ...), custom_call_target="tpu_custom_call" | custom-call | flops 44040192 | bytes 1048576 | tf_op jit(solution)/shard_map/pallas_call | solution.py:304
  64.2 9.9 %all-gather.1 = f32[256,512]{1,0:T(8,128)S(1)} all-gather(f32[64,512]{1,0:T(8,128)S(1)} %shard_map.66), channel_id=3, replica_groups=mesh['zh'=2,'y'=4,'c'=2,'tm'=32] {'y'}, dimensions={0}, use_global_device_ids=true | all-gather | bytes 655360 | tf_op jit(solution)/shard_map/all_gather | solution.py:404
  74.1 5.8 %collective-permute-start.4 = (f32[4,64,512]{2,1,0:T(8,128)S(1)}, f32[4,64,512]{2,1,0:T(8,128)S(1)}, u32[]{:S(2)}, u32[]{:S(2)}) collective-permute-start(f32[4,64,512]{2,1,0:T(8,128)S(1)} %bitcast.9), channel_id=1, source_target_pairs={{0,32},{32,0},{1,33},{33,1},{2,34},{34,2},{3,35},{35,3},{4,36},{36... | collective-permute-start | bytes 1572872 | tf_op jit(solution)/shard_map/ppermute | solution.py:405
  79.9 0.8 %shard_map.67.begun_ref = f32[64,4096]{1,0:T(8,128)} custom-call(s32[1]{0:T(128)} %bitcast.half_ref.refs_1_, f32[4,64,512]{2,1,0:T(8,128)S(1)} %bitcast.10), custom_call_target="tpu_custom_call" | custom-call | bytes 1048576 | tf_op jit(solution)/shard_map/pallas_call | solution.py:340
  80.7 0.7 collective-permute-done.4.chunks_ref
  81.4 0.8 shard_map.68
  (5 shorter events, 0.1 us)
Async XLA Ops:
  0.9 1.6 %copy-start.1 = (bf16[256,4096]{1,0:T(8,128)(2,1)S(1)}, bf16[256,4096]{1,0:T(8,128)(2,1)}, u32[]{:S(2)}) copy-start(bf16[256,4096]{1,0:T(8,128)(2,1)} %signal_ref.1) | copy-start | bytes 6291460
  2.5 9.8 %copy-start = (f32[64,4096]{1,0:T(8,128)S(1)}, f32[64,4096]{1,0:T(8,128)}, u32[]{:S(2)}) copy-start(f32[64,4096]{1,0:T(8,128)} %after_ref) | copy-start | bytes 3145732
  2.9 10.0 %copy-start.2 = (f32[64,128]{1,0:T(8,128)S(1)}, f32[64,128]{1,0:T(8,128)}, u32[]{:S(2)}) copy-start(f32[64,128]{1,0:T(8,128)} %refs_8_.1) | copy-start | bytes 98308
  3.0 4.2 %collective-permute-start = (f32[4,72,512]{2,1,0:T(8,128)S(1)}, f32[4,72,512]{2,1,0:T(8,128)S(1)}, u32[]{:S(2)}, u32[]{:S(2)}) collective-permute-start(f32[4,72,512]{2,1,0:T(8,128)S(1)} %get-tuple-element.15), channel_id=1, source_target_pairs={{0,32},{32,0},{1,33},{33,1},{2,34},{34,2},{3,35},{35,3},{4,36},{36... | collective-permute-start | bytes 1769480 | tf_op jit(solution)/shard_map/ppermute | solution.py:382
  8.1 13.8 %all-to-all-start = ((f32[4,72,512]{2,1,0:T(8,128)}), f32[4,72,512]{2,1,0:T(8,128)S(1)}, u32[]{:S(2)}, u32[]{:S(2)}) async-start(f32[4,72,512]{2,1,0:T(8,128)} %add.11), calls=%async_computation | async-start | bytes 1179648 | tf_op jit(solution)/shard_map/all_to_all | solution.py:388
  12.3 0.7 collective-permute-start.1
  13.0 45.5 %copy-start.3 = (f32[64]{0:T(128)S(1)}, f32[64]{0:T(128)}, u32[]{:S(2)}) copy-start(f32[64]{0:T(128)} %param.10) | copy-start | bytes 772
  39.0 19.2 %collective-permute-start.3 = (f32[64,256]{1,0:T(8,128)S(1)}, f32[64,256]{1,0:T(8,128)S(1)}, u32[]{:S(2)}, u32[]{:S(2)}) collective-permute-start(f32[64,256]{1,0:T(8,128)S(1)} %get-tuple-element.23), channel_id=1, source_target_pairs={{224,1},{225,2},{226,3},{227,4},{228,5},{229,6},{230,7},{231,264},... | collective-permute-start | bytes 196616 | tf_op jit(solution)/shard_map/ppermute | solution.py:396
  50.4 8.1 %collective-permute-start.2 = (f32[64,256]{1,0:T(8,128)S(1)}, f32[64,256]{1,0:T(8,128)S(1)}, u32[]{:S(2)}, u32[]{:S(2)}) collective-permute-start(f32[64,256]{1,0:T(8,128)S(1)} %get-tuple-element.24), channel_id=1, source_target_pairs={{0,32},{32,0},{1,33},{33,1},{2,34},{34,2},{3,35},{35,3},{4,36},{36... | collective-permute-start | bytes 196616 | tf_op jit(solution)/shard_map/ppermute | solution.py:397
  74.1 7.3 %collective-permute-start.4 = (f32[4,64,512]{2,1,0:T(8,128)S(1)}, f32[4,64,512]{2,1,0:T(8,128)S(1)}, u32[]{:S(2)}, u32[]{:S(2)}) collective-permute-start(f32[4,64,512]{2,1,0:T(8,128)S(1)} %bitcast.9), channel_id=1, source_target_pairs={{0,32},{32,0},{1,33},{33,1},{2,34},{34,2},{3,35},{35,3},{4,36},{36... | collective-permute-start | bytes 1572872 | tf_op jit(solution)/shard_map/ppermute | solution.py:405

commit v7 on v6

v7 whole, which is shorter than its diff:
```python
import jax
import jax.numpy as jnp
from jax import lax
from jax.experimental import pallas as pl
from jax.experimental.pallas import tpu as pltpu
from jax.sharding import Mesh, PartitionSpec as P

ATOMS = 64
LENGTH = 128
CHUNK = 512
CHUNKS = 8
QUARTER = 4
LANES = 2 * ATOMS
TILES = CHUNK // LANES
BODY = TILES * ATOMS
ROWS = BODY + 16
HALO = BODY // 2 + 16
RIM = LANES + ATOMS
NARROW, WIDE = 48, 56
RUN = 8
HIGHEST = lax.Precision.HIGHEST
F32 = jnp.float32
VMEM = pl.BlockSpec(memory_space=pltpu.VMEM)
SMEM = pl.BlockSpec(memory_space=pltpu.SMEM)
ANY = pl.BlockSpec(memory_space=pl.ANY)


def cost(flops, bytes_accessed):
    return pl.CostEstimate(flops=flops, bytes_accessed=bytes_accessed, transcendentals=0)


def params(mebibytes):
    return pltpu.CompilerParams(vmem_limit_bytes=mebibytes * 2**20)


def project_body(half_ref, parts_ref, signal_ref, away_ref, kept_ref):
    first = half_ref[0] == 0
    parts = parts_ref[...]
    gram = lax.dot_general(parts, parts, (((1,), (1,)), ((), ())), preferred_element_type=F32)
    gram = gram[:ATOMS] + gram[ATOMS:]
    gram = gram[:, :ATOMS] + gram[:, ATOMS:]
    upper = jnp.concatenate([gram[:16], gram[16:32]], axis=1)
    lower = jnp.concatenate([gram[32:48], gram[48:]], axis=1)
    away_gram, kept_gram = jnp.where(first, lower, upper), jnp.where(first, upper, lower)
    for i in range(QUARTER):
        away_ref[i, BODY:] = away_gram
        kept_ref[i, BODY:] = kept_gram
    for out_ref, which in ((away_ref, 1 - half_ref[0]), (kept_ref, half_ref[0])):
        for i in range(QUARTER):
            column = pl.multiple_of((2 * i + which) * CHUNK, CHUNK)
            product = jnp.dot(
                parts, signal_ref[:, pl.ds(column, CHUNK)], preferred_element_type=F32
            )
            product = product[:ATOMS] + product[ATOMS:]
            for t in range(TILES):
                out_ref[i, t * ATOMS : (t + 1) * ATOMS] = product[:, t * LANES : (t + 1) * LANES]


def project(half, parts, signal):
    channels, width = signal.shape
    return pl.pallas_call(
        project_body,
        in_specs=[SMEM, VMEM, VMEM],
        out_specs=[VMEM, VMEM],
        out_shape=[jax.ShapeDtypeStruct((QUARTER, ROWS, LANES), F32)] * 2,
        compiler_params=params(8),
        cost_estimate=cost(2 * channels * LANES * width, 2 * channels * width),
    )(half, parts, signal)


def to_segments(rows, segment, out_ref):
    for s in range(8):
        out_ref[pl.ds(s, segment, stride=8)] = rows[s * segment : (s + 1) * segment]


def from_segments(ref, segment):
    return jnp.concatenate([ref[pl.ds(s, segment, stride=8)] for s in range(8)], axis=0)


def spread_taps(temporal_ref, taps_ref):
    temporal = temporal_ref[...]
    columns = jnp.concatenate([temporal, temporal], axis=0).T
    for i in range(LENGTH // 4):
        c0, c1, c2, c3 = (
            jnp.broadcast_to(columns[4 * i + p : 4 * i + p + 1], (8, LANES)) for p in range(4)
        )
        even, odd = c0 + c1, c2 + c3
        for k, tap in enumerate((c0, c0 + c2, c2, even, even + odd, odd, c1, c1 + c3, c3)):
            taps_ref[k, i] = tap


def lane_half():
    return lax.broadcasted_iota(jnp.int32, (1, 8, LANES), 2) // ATOMS


def sublane():
    return lax.broadcasted_iota(jnp.int32, (1, 8, LANES), 1)


def later_segment(rows):
    up = pltpu.roll(rows, 7, 1)
    return jnp.where(sublane() == 7, pltpu.roll(up, ATOMS, 2), up)


def earlier_segment(rows):
    down = pltpu.roll(rows, 1, 1)
    return jnp.where(sublane() == 0, pltpu.roll(down, ATOMS, 2), down)


def over_sublanes(rows):
    count = rows.shape[0]
    return jnp.broadcast_to(rows.reshape(count, 1, LANES), (count, 8, LANES))


def spread_later(rows, spread_ref, beyond=None):
    segment = rows.shape[0]
    reach = segment + LENGTH
    for first in range(0, reach, segment):
        count = min(segment, reach - first)
        rows = rows[:count]
        if first > 0:
            rows = later_segment(rows)
            if beyond is not None:
                last = (sublane() == 7) & (lane_half() == 1)
                start = first - segment
                rows = jnp.where(last, over_sublanes(beyond[start : start + count]), rows)
        spread_ref[first // 4 : (first + count) // 4] = rows.reshape(count // 4, 4, 8, LANES)


def spread_earlier(rows, spread_ref, before=None):
    segment = rows.shape[0]
    start = LENGTH
    while True:
        skip = max(0, -start)
        first, count = start + skip, segment - skip
        kept = rows[skip:]
        spread_ref[first // 4 : (first + count) // 4] = kept.reshape(count // 4, 4, 8, LANES)
        if start <= 0:
            return
        rows = earlier_segment(rows)
        start -= segment
        if before is not None:
            skip = max(0, -start)
            rim = over_sublanes(before[start + skip : start + segment])
            if skip:
                rim = jnp.concatenate([jnp.zeros((skip, 8, LANES), F32), rim], axis=0)
            rows = jnp.where((sublane() == 0) & (lane_half() == 0), rim, rows)


def short_inputs(segment, spread_ref, inputs_ref, offset):
    count = (segment + LENGTH) // 4 - 1

    def x(p):
        p = p + offset
        return spread_ref[p // 4 : p // 4 + count, p % 4]

    x0, x1, x2, x3, x4, x5, x6 = (x(p) for p in range(7))
    inputs_ref[0, :count] = (x0 - x1) - (x2 - x3)
    inputs_ref[1, :count] = x2 - x3
    inputs_ref[2, :count] = (x4 - x5) - (x2 - x3)
    inputs_ref[3, :count] = x1 - x3
    inputs_ref[4, :count] = x3
    inputs_ref[5, :count] = x5 - x3
    inputs_ref[6, :count] = (x2 - x1) - (x4 - x3)
    inputs_ref[7, :count] = x4 - x3
    inputs_ref[8, :count] = (x6 - x5) - (x4 - x3)


def filter_rows(segment, inputs_ref, taps_ref, sums_ref, reverse):
    taps = LENGTH // 4
    phase = segment // 4

    @pl.loop(0, 9, unroll=3)
    def _(k):
        sums = [None] * phase
        held = {}
        for j in range(phase + taps - 1):
            if j < taps:
                held[j] = taps_ref[8 - k, taps - 1 - j] if reverse else taps_ref[k, j]
            value = inputs_ref[k, j]
            for m in range(max(0, j - phase + 1), min(taps, j + 1)):
                term = value * held[m]
                sums[j - m] = term if sums[j - m] is None else sums[j - m] + term
        for i in range(phase):
            sums_ref[k, i] = sums[i]

    def total(i, k):
        return sums_ref[i, :phase] + sums_ref[k, :phase]

    a, b, c = total(0, 1), total(3, 4), total(6, 7)
    d, e, f = total(1, 2), total(4, 5), total(7, 8)
    rows = jnp.stack([a + b, b + c, d + e, e + f], axis=1)
    return rows.reshape(segment, 8, LANES)


def filter_scratch(segment):
    reach = (segment + LENGTH) // 4
    return [
        pltpu.VMEM((9, LENGTH // 4, 8, LANES), F32),
        pltpu.VMEM((reach, 4, 8, LANES), F32),
        pltpu.VMEM((9, reach, 8, LANES), F32),
        pltpu.VMEM((9, segment // 4, 8, LANES), F32),
    ]


def rebuild_body(
    place_ref, temporal_ref, before_ref, first_ref, second_ref, after_ref,
    rebuilt_ref, beyond_ref, point_ref, rim_ref, taps_ref, spread_ref, inputs_ref, sums_ref, wide_ref,
):
    place = place_ref[0]
    spread_taps(temporal_ref, taps_ref)
    before = jnp.where(place == 0, 0.0, before_ref[...])
    after = jnp.where(place == CHUNKS - 1, 0.0, after_ref[...])
    first, second = first_ref[...], second_ref[...]
    upper = jnp.concatenate([before[:, 128:], first], axis=1)
    lower = jnp.concatenate([second, after[:, :128]], axis=1)
    to_segments(jnp.concatenate([upper, lower], axis=0).T, NARROW, point_ref)

    upper = jnp.concatenate([upper, second[:, :128]], axis=1)
    lower = jnp.concatenate([second[:, 64:], after, after[:, :64]], axis=1)
    to_segments(jnp.concatenate([upper, lower], axis=0).T, WIDE, wide_ref)
    ahead = before[:, :128]
    ahead = jnp.concatenate([ahead, ahead], axis=0).T
    spread_earlier(wide_ref[...].reshape(WIDE, 8, LANES), spread_ref, ahead)
    short_inputs(WIDE, spread_ref, inputs_ref, 1)
    rebuilt = filter_rows(WIDE, inputs_ref, taps_ref, sums_ref, True)

    wide_ref[...] = rebuilt.reshape(8 * WIDE, LANES)
    rows = from_segments(wide_ref, WIDE)
    swapped = pltpu.roll(rows, ATOMS, 1)
    left = lax.broadcasted_iota(jnp.int32, (1, LANES), 1) < ATOMS
    lower = jnp.concatenate([swapped[384:], rows[:320]], axis=0)
    to_segments(jnp.where(left, rows[:384], lower), NARROW, rebuilt_ref)
    beyond_ref[...] = jnp.where(left, swapped[320:], rows[320:])

    starting = place % 2 == 0
    start = jnp.where(left, rows[128:256], swapped[256:384])
    end = jnp.where(left, swapped[64:192], rows[192:320])
    rim_ref[:LANES] = jnp.where(starting, start, end)
    rim_ref[LANES:] = jnp.where(starting, first[:, :128], second[:, 128:])


def rebuild(place, temporal, activations):
    atoms, width = activations.shape
    half = CHUNK // 2
    last = width // half - 1
    block = (atoms, half)
    shapes = [(8 * NARROW, LANES), (LENGTH, LANES), (8 * NARROW, LANES), (RIM, LANES)]
    return pl.pallas_call(
        rebuild_body,
        grid_spec=pltpu.PrefetchScalarGridSpec(
            num_scalar_prefetch=1,
            grid=(1,),
            in_specs=[
                pl.BlockSpec((ATOMS, LENGTH), lambda i, place: (0, 0)),
                pl.BlockSpec(block, lambda i, place: (0, jnp.maximum(2 * place[0] - 1, 0))),
                pl.BlockSpec(block, lambda i, place: (0, 2 * place[0])),
                pl.BlockSpec(block, lambda i, place: (0, 2 * place[0] + 1)),
                pl.BlockSpec(block, lambda i, place: (0, jnp.minimum(2 * place[0] + 2, last))),
            ],
            out_specs=[pl.BlockSpec(shape, lambda i, place: (0, 0)) for shape in shapes],
            scratch_shapes=filter_scratch(WIDE) + [pltpu.VMEM((8 * WIDE, LANES), F32)],
        ),
        out_shape=[jax.ShapeDtypeStruct(shape, F32) for shape in shapes],
        compiler_params=params(12),
        cost_estimate=cost(2 * 8 * WIDE * LANES * LENGTH, 2**20),
    )(place, temporal, activations, activations, activations, activations)


def steps_body(
    total, begin_ref, place_ref, step_ref, mine_ref, inner_ref, outer_ref, rebuilt_ref, beyond_ref,
    point_ref, temporal_ref, threshold_ref, out_ref, taps_ref, spread_ref, inputs_ref, sums_ref,
    cross_ref, side_ref, mix_ref,
):
    begin, place = begin_ref[0], place_ref[0]
    first = place % 2 == 0
    rate = step_ref[0]
    spread_taps(temporal_ref, taps_ref)

    own, other = mine_ref[BODY:], inner_ref[BODY // 2 :]
    upper, lower = jnp.where(first, own, other), jnp.where(first, other, own)
    gram = jnp.concatenate(
        [upper[:, :ATOMS], upper[:, ATOMS:], lower[:, :ATOMS], lower[:, ATOMS:]], axis=0
    )
    mix_ref[...] = jnp.zeros_like(mix_ref)
    mix_ref[:ATOMS, :ATOMS] = gram
    mix_ref[ATOMS:, ATOMS:] = gram

    near, far = slice(0, ATOMS), slice(ATOMS, 2 * ATOMS)
    left = jnp.where(first, outer_ref[far], inner_ref[far])
    right = jnp.where(first, inner_ref[near], outer_ref[near])
    beyond = jnp.where(first, inner_ref[far], outer_ref[far])
    tiles = [mine_ref[t * ATOMS : (t + 1) * ATOMS] for t in range(TILES)]
    upper = jnp.concatenate([left, tiles[0], tiles[1]], axis=1)
    lower = jnp.concatenate([tiles[2], tiles[3], right], axis=1)
    to_segments(jnp.concatenate([upper, lower], axis=0).T, NARROW, cross_ref)
    beyond = jnp.concatenate([beyond, beyond], axis=0).T

    left_half = lax.broadcasted_iota(jnp.int32, (1, LANES), 1) < ATOMS
    at_start = left_half & (place == 0)
    at_end = jnp.logical_not(left_half) & (place == CHUNKS - 1)
    added = outer_ref[HALO : HALO + LANES]
    swapped = pltpu.roll(added, ATOMS, 1)
    to_segments(
        jnp.concatenate(
            [
                jnp.where(at_start, added, 0.0),
                jnp.where(at_start, swapped, 0.0),
                jnp.where(at_end, swapped, 0.0),
            ],
            axis=0,
        ),
        NARROW,
        side_ref,
    )
    rebuilt = rebuilt_ref[...] + side_ref[...]
    added_beyond = jnp.where(left_half, swapped, added)
    rebuilt_beyond = beyond_ref[...] + jnp.where(place == CHUNKS - 1, added_beyond, 0.0)
    rim = outer_ref[HALO + LANES :]
    rim = jnp.concatenate([rim, rim], axis=0).T
    to_segments(
        jnp.concatenate(
            [jnp.where(at_start, rim, 0.0), jnp.zeros_like(rim), jnp.where(at_end, rim, 0.0)],
            axis=0,
        ),
        NARROW,
        side_ref,
    )

    shape = (NARROW, 8, LANES)
    sample = lax.broadcasted_iota(jnp.int32, shape, 0) + (
        (lane_half() * 8 + sublane()) * NARROW + (begin - LENGTH)
    )
    sample_beyond = lax.broadcasted_iota(jnp.int32, (LENGTH, LANES), 0) + (begin + CHUNK + LENGTH)
    shrink = threshold_ref[...]
    shrink = jnp.concatenate([shrink, shrink], axis=1).reshape(1, 1, LANES)

    def mixed(rebuilt):
        return jnp.dot(rebuilt, mix_ref[...], precision=HIGHEST, preferred_element_type=F32)

    def projected(rebuilt):
        rows = (mixed(rebuilt) - cross_ref[...]).reshape(shape)
        return jnp.where(sample < total, rows, 0.0)

    def stepped(point, rows, rows_beyond=None):
        spread_later(rows, spread_ref, rows_beyond)
        short_inputs(NARROW, spread_ref, inputs_ref, 0)
        gradient = filter_rows(NARROW, inputs_ref, taps_ref, sums_ref, False)
        return jnp.maximum(point - rate * (gradient + shrink), 0.0)

    inertia = 1.0
    inertia_next = (1.0 + (1.0 + 4.0 * inertia * inertia) ** 0.5) / 2.0
    momentum = (inertia - 1.0) / inertia_next
    previous = (point_ref[...] + side_ref[...]).reshape(shape)
    beyond = jnp.where(sample_beyond < total, mixed(rebuilt_beyond) - beyond, 0.0)
    update = stepped(previous, projected(rebuilt), beyond)
    point = update + momentum * (update - previous)
    point = jnp.where(sample >= 0, point, 0.0)

    spread_earlier(point, spread_ref)
    short_inputs(NARROW, spread_ref, inputs_ref, 1)
    rebuilt = filter_rows(NARROW, inputs_ref, taps_ref, sums_ref, True)
    update = stepped(point, projected(rebuilt.reshape(8 * NARROW, LANES)))

    cross_ref[...] = update.reshape(8 * NARROW, LANES)
    columns = from_segments(cross_ref, NARROW).T
    out_ref[...] = jnp.concatenate([columns[:ATOMS, 128:], columns[ATOMS:, :256]], axis=1)


def steps(total, begin, place, step_size, mine, inner, outer, before_steps, temporal, threshold):
    def body(*refs):
        steps_body(total, *refs)

    return pl.pallas_call(
        body,
        in_specs=[SMEM] * 3 + [VMEM] * 8,
        out_specs=VMEM,
        out_shape=jax.ShapeDtypeStruct((ATOMS, CHUNK), F32),
        scratch_shapes=filter_scratch(NARROW)
        + [pltpu.VMEM((8 * NARROW, LANES), F32)] * 2
        + [pltpu.VMEM((LANES, LANES), F32)],
        compiler_params=params(12),
        cost_estimate=cost(6 * 8 * NARROW * LANES * LENGTH, 2**20),
    )(begin, place, step_size, mine, inner, outer, *before_steps, temporal, threshold)


def place_copies(half, chunks_ref, out_ref, sems):
    copies = []
    for i in range(QUARTER):
        column = pl.multiple_of((2 * i + half) * CHUNK, CHUNK)
        copies.append(
            pltpu.make_async_copy(chunks_ref.at[i], out_ref.at[:, pl.ds(column, CHUNK)], sems.at[i])
        )
    for copy in copies:
        copy.start()
    for copy in copies:
        copy.wait()


def place_mine_body(half_ref, chunks_ref, out_ref, sems):
    place_copies(half_ref[0], chunks_ref, out_ref, sems)


def place_other_body(half_ref, chunks_ref, begun_ref, out_ref, sems):
    place_copies(1 - half_ref[0], chunks_ref, out_ref, sems)


def place_half(half, chunks, begun=None):
    out_shape = jax.ShapeDtypeStruct((ATOMS, CHUNKS * CHUNK), F32)
    first = begun is None
    return pl.pallas_call(
        place_mine_body if first else place_other_body,
        in_specs=[SMEM, ANY] + ([] if first else [ANY]),
        out_specs=ANY,
        out_shape=out_shape,
        scratch_shapes=[pltpu.SemaphoreType.DMA((QUARTER,))],
        input_output_aliases={} if first else {2: 0},
        compiler_params=params(4),
        cost_estimate=cost(0, 2**20),
    )(half, chunks, *([] if first else [begun]))


def solution(mesh):
    blocks = mesh.shape["tm"]
    split = Mesh(mesh.devices.reshape(2, 4, 2, blocks), ("zh", "y", "c", "tm"))
    swap = [(0, 1), (1, 0)]
    line = ("zh", "y", "c", "tm")

    def device(zh, q, tm):
        return (zh * CHUNKS + q) * blocks + tm

    inside, rims = [], []
    for zh in range(2):
        for tm in range(blocks):
            for q in range(1, CHUNKS - 1, 2):
                inside.append((device(zh, q, tm), device(zh, q + 1, tm)))
            if tm + 1 < blocks:
                near = 1 - zh if (tm + 1) % RUN == 0 else zh
                rims.append((device(zh, CHUNKS - 1, tm), device(near, 0, tm + 1)))
    rims = rims + [(b, a) for a, b in rims]
    outside = rims + inside + [(b, a) for a, b in inside]

    def per_device(signal, spatial, temporal, activations, threshold, step_size):
        half = lax.axis_index("c").astype(jnp.int32)
        place = lax.axis_index("y").astype(jnp.int32) * 2 + half
        time_block = lax.axis_index("tm").astype(jnp.int32)
        width = activations.shape[1]
        spatial = spatial.T
        high = lax.reduce_precision(spatial, 8, 7)
        parts = jnp.concatenate([high, spatial - high], axis=0).astype(jnp.bfloat16)
        away, kept = project(half[None], parts, signal)
        summed = kept + lax.ppermute(away, "c", swap)

        activations, summed = lax.optimization_barrier((activations, summed))
        pieces = lax.all_to_all(summed, "y", 0, 0, tiled=True)
        *before_steps, rim = rebuild(place[None], temporal, activations)
        group_sum = jnp.sum(pieces, axis=0)
        group_sum, before_steps, rim = lax.optimization_barrier((group_sum, before_steps, rim))
        mine = jnp.sum(lax.all_gather(group_sum, "zh", axis=0), axis=0)

        first = half == 0
        start, end, gram = mine[: BODY // 2], mine[BODY // 2 : BODY], mine[BODY:]
        outer = jnp.concatenate([jnp.where(first, start, end), gram, rim], axis=0)
        outer = lax.ppermute(outer, line, outside)
        inner = jnp.concatenate([jnp.where(first, end, start), gram], axis=0)
        inner = lax.ppermute(inner, "c", swap)
        begin = time_block * width + place * CHUNK
        update = steps(
            blocks * width, begin[None], place[None], step_size, mine, inner, outer, before_steps,
            temporal, threshold[None, :],
        )

        copies = jnp.broadcast_to(update[None], (QUARTER, ATOMS, CHUNK))
        gathered = lax.all_to_all(copies, "y", 0, 0, tiled=True)
        other = lax.ppermute(gathered, "c", swap)
        return place_half(half[None], other, place_half(half[None], gathered))

    chan = ("zh", "y", "c")
    in_specs = (P(chan, "tm"), P(chan, None), P(), P(None, "tm"), P(), P())
    return jax.shard_map(
        per_device, mesh=split, in_specs=in_specs, out_specs=P(None, "tm"), check_vma=False
    )
```

time: 82.6 us -> 79.7 us (0.965)
  starting transfers between devices: 31.8 us -> 28.6 us
  blocking collectives: 26.9 us -> 27.9 us
  Pallas kernels: 9.72 us -> 8.81 us
    all_to_all x0 -> x1, blocking collectives: none -> 10.9 us  [per_device(): gathered = lax.all_to_all(copies, 'y', 0, 0, tiled=True)]
    all_gather x1 -> x0, blocking collectives: 9.9 us -> none  [per_device(): gathered = lax.all_gather(update, 'y', axis=0)]
    ppermute x1, starting transfers between devices: 5.77 us -> 3.8 us  [per_device(): other = lax.ppermute(gathered, 'c', swap)]
    ppermute x3 -> x2, starting transfers between devices: 19.2 us -> 18 us  [the longest x1 10.8 us: per_device(): outer = lax.ppermute(outer, line, outside)]
    pallas_call x1, Pallas kernels: 5.79 us -> 4.83 us  [steps(): pl.pallas_call(body, in_specs=[SMEM] * 3 + [VMEM] * 8, out_specs=VMEM, ou...]
  transfers between devices with their start and end apart: 6 -> 5, of which waited for: 4 -> 4; matrix products, arithmetic and copies ran while one was open for 0% -> 0% of each run, Pallas kernels for 3% -> 3%
where the time goes in v7:
time: 79.7 us; the launch traced here: 79.3 us
  starting transfers between devices  28.6 us (36%)
  blocking collectives  27.9 us (35%)
  waiting for transfers between devices  9.85 us (12%)
  Pallas kernels  8.81 us (11%)
  other arithmetic  1.79 us (2%)
  local copies, waits for them, and re-layouts  1.66 us (2%)
  between operations  0.8 us (1%)
    all_gather x1, blocking collectives, per_device(): mine = jnp.sum(lax.all_gather(group_sum, 'zh', axis=0), axis=0)  16.9 us
    all_to_all x1, blocking collectives, per_device(): gathered = lax.all_to_all(copies, 'y', 0, 0, tiled=True)  10.9 us
    ppermute x1, starting transfers between devices, per_device(): outer = lax.ppermute(outer, line, outside)  10.8 us
    all_to_all x1, waiting for transfers between devices, per_device(): pieces = lax.all_to_all(summed, 'y', 0, 0, tiled=True)  7.36 us
    ppermute x1, starting transfers between devices, per_device(): inner = lax.ppermute(inner, 'c', swap)  7.21 us
    pallas_call x1, Pallas kernels, steps(): pl.pallas_call(body, in_specs=[SMEM] * 3 + [VMEM] * 8, out_specs=VMEM, ou...  4.83 us
    all_to_all x1, starting transfers between devices, per_device(): pieces = lax.all_to_all(summed, 'y', 0, 0, tiled=True)  4.18 us
    ppermute x1, starting transfers between devices, per_device(): other = lax.ppermute(gathered, 'c', swap)  3.8 us
  transfers between devices with their start and end apart: 5, of which 4 were waited for; matrix products, arithmetic and copies ran while one was open for 0% of the time, Pallas kernels for 3%

profile of v7, /device:TPU:7, one launch (start us, length us, event | category | flops | bytes accessed | tf_op | source)
XLA Modules:
  0.0 79.3 jit_solution(12031624107552573920)
XLA Ops:
  0.0 0.8 %reduce-precision_convert_fusion = (bf16[64,256]{1,0:T(8,128)(2,1)S(1)}, bf16[64,256]{1,0:T(8,128)(2,1)S(1)}) fusion(f32[256,64]{0,1:T(8,128)} %param.7), kind=kLoop, calls=%fused_computation.2 | loop fusion | flops 65536 | bytes 131072 | tf_op jit(solution)/shard_map/convert
  0.9 0.0 copy-start.1
  0.9 1.6 %copy-done.1 = bf16[256,4096]{1,0:T(8,128)(2,1)S(1)} copy-done((bf16[256,4096]{1,0:T(8,128)(2,1)S(1)}, bf16[256,4096]{1,0:T(8,128)(2,1)}, u32[]{:S(2)}) %copy-start.1) | copy-done | bytes 2097176
  2.5 0.0 copy-start
  2.5 0.0 copy-start.2
  2.5 0.5 shard_map.64
  2.9 2.6 %collective-permute-start = (f32[4,272,128]{2,1,0:T(8,128)S(1)}, f32[4,272,128]{2,1,0:T(8,128)S(1)}, u32[]{:S(2)}, u32[]{:S(2)}) collective-permute-start(f32[4,272,128]{2,1,0:T(8,128)S(1)} %get-tuple-element.19), channel_id=1, source_target_pairs={{0,32},{32,0},{1,33},{33,1},{2,34},{34,2},{3,35},{35,3},{4,36},{36... | collective-permute-start | bytes 1671176 | tf_op jit(solution)/shard_map/ppermute | solution.py:452
  5.5 1.6 %collective-permute-done = f32[4,272,128]{2,1,0:T(8,128)S(1)} collective-permute-done((f32[4,272,128]{2,1,0:T(8,128)S(1)}, f32[4,272,128]{2,1,0:T(8,128)S(1)}, u32[]{:S(2)}, u32[]{:S(2)}) %collective-permute-start) | collective-permute-done | bytes 557088 | tf_op jit(solution)/shard_map/ppermute | solution.py:452
  7.1 0.9 %add.11 = f32[4,272,128]{2,1,0:T(8,128)} add(f32[4,272,128]{2,1,0:T(8,128)S(1)} %get-tuple-element.18, f32[4,272,128]{2,1,0:T(8,128)S(1)} %collective-permute-done) | non-fusion elementwise | flops 139264 | bytes 1671168 | tf_op jit(solution)/shard_map/add | solution.py:452
  8.0 4.2 %all-to-all-start = ((f32[4,272,128]{2,1,0:T(8,128)}), f32[4,272,128]{2,1,0:T(8,128)S(1)}, u32[]{:S(2)}, u32[]{:S(2)}) async-start(f32[4,272,128]{2,1,0:T(8,128)} %add.11), calls=%async_computation | async-start | bytes 1114112 | tf_op jit(solution)/shard_map/all_to_all | solution.py:455
  12.1 0.0 copy-done
  12.1 0.0 copy-done.2
  12.2 1.9 %shard_map.65 = (f32[384,128]{1,0:T(8,128)S(1)}, f32[128,128]{1,0:T(8,128)S(1)}, f32[384,128]{1,0:T(8,128)S(1)}, f32[192,128]{1,0:T(8,128)S(1)}) custom-call(s32[1]{0:T(128)} %bitcast.2.place_ref.refs_1_, f32[64,128]{1,0:T(8,128)S(1)} %copy-done.2, f32[64,4096]{1,0:T(8,128)S(1)} %copy-done, f32[64,4096]{1,0:T(8,128)S(1)} %copy-done, f32[64,4096]{1,0:T(8,128)S(1)} %copy-done, ...), custom_call_target="tpu_custom_call" | custom-call | flops 14680064 | bytes 1048576 | tf_op jit(solution)/shard_map/pallas_call | solution.py:249
  14.0 0.0 copy-start.3
  14.0 7.4 %all-to-all-done = f32[4,272,128]{2,1,0:T(8,128)S(1)} async-done(((f32[4,272,128]{2,1,0:T(8,128)}), f32[4,272,128]{2,1,0:T(8,128)S(1)}, u32[]{:S(2)}, u32[]{:S(2)}) %all-to-all-start) | async-done | bytes 557088 | tf_op jit(solution)/shard_map/all_to_all | solution.py:455
  21.4 16.9 %all-gather = f32[544,128]{1,0:T(8,128)S(1)} all-gather(f32[272,128]{1,0:T(8,128)S(1)} %reduce_sum.18), channel_id=2, replica_groups=mesh['zh'=2,'y'=4,'c'=2,'tm'=32] {'zh'}, dimensions={0}, use_global_device_ids=true | all-gather | bytes 417792 | tf_op jit(solution)/shard_map/all_gather | solution.py:459
  38.4 10.8 %collective-permute-start.2 = (f32[336,128]{1,0:T(8,128)S(1)}, f32[336,128]{1,0:T(8,128)S(1)}, u32[]{:S(2)}, u32[]{:S(2)}) collective-permute-start(f32[336,128]{1,0:T(8,128)S(1)} %pad_maximum_fusion), channel_id=1, source_target_pairs={{224,1},{225,2},{226,3},{227,4},{228,5},{229,6},{230,7},{231,264},... | collective-permute-start | bytes 516104 | tf_op jit(solution)/shard_map/ppermute | solution.py:464
  49.3 7.2 %collective-permute-start.1 = (f32[144,128]{1,0:T(8,128)S(1)}, f32[144,128]{1,0:T(8,128)S(1)}, u32[]{:S(2)}, u32[]{:S(2)}) collective-permute-start(f32[144,128]{1,0:T(8,128)S(1)} %pad_maximum_fusion.1), channel_id=1, source_target_pairs={{0,32},{32,0},{1,33},{33,1},{2,34},{34,2},{3,35},{35,3},{4,36},{36... | collective-permute-start | bytes 221192 | tf_op jit(solution)/shard_map/ppermute | solution.py:466
  57.1 0.2 collective-permute-done.1.refs_4_
  57.4 0.0 collective-permute-done.2.refs_5_
  57.4 0.0 copy-done.3
  57.4 4.8 %shard_map.66 = f32[64,512]{1,0:T(8,128)S(1)} custom-call(s32[1]{0:T(128)} %bitcast.1.refs_0_, s32[1]{0:T(128)} %bitcast.2.place_ref.refs_1_, f32[1]{0:T(128)S(6)} %copy.9.refs_2_, f32[272,128]{1,0:T(8,128)S(1)} %reduce_sum.19.refs_3_, f32[144,128]{1,0:T(8,128)S(1)} %collective-permute-done.1.refs_4_, f32[336,128]{1,0:T(8,128)S(1)} %collective-permute-done.2.refs_5_, ...), custom_call_target="tpu_custom_call" | custom-call | flops 37748736 | bytes 1048576 | tf_op jit(solution)/shard_map/pallas_call | solution.py:374
  62.2 0.1 broadcast_in_dim.25
  62.3 10.9 %all_to_all.10.chunks_ref = f32[4,64,512]{2,1,0:T(8,128)S(1)} all-to-all(f32[4,64,512]{2,1,0:T(8,128)S(1)} %broadcast_in_dim.25), channel_id=1, replica_groups=mesh['zh'=2,'y'=4,'c'=2,'tm'=32] {'y'}, dimensions={0} | all-to-all | bytes 1048576 | tf_op jit(solution)/shard_map/all_to_all | solution.py:474
  73.2 3.8 %collective-permute-start.3 = (f32[4,64,512]{2,1,0:T(8,128)S(1)}, f32[4,64,512]{2,1,0:T(8,128)S(1)}, u32[]{:S(2)}, u32[]{:S(2)}) collective-permute-start(f32[4,64,512]{2,1,0:T(8,128)S(1)} %all_to_all.10.chunks_ref), channel_id=1, source_target_pairs={{0,32},{32,0},{1,33},{33,1},{2,34},{34,2},{3,35},{35,3},{4,36},{36... | collective-permute-start | bytes 1572872 | tf_op jit(solution)/shard_map/ppermute | solution.py:475
  77.0 0.8 %shard_map.67.begun_ref = f32[64,4096]{1,0:T(8,128)} custom-call(s32[1]{0:T(128)} %bitcast.half_ref, f32[4,64,512]{2,1,0:T(8,128)S(1)} %all_to_all.10.chunks_ref), custom_call_target="tpu_custom_call" | custom-call | bytes 1048576 | tf_op jit(solution)/shard_map/pallas_call | solution.py:411
  77.8 0.7 collective-permute-done.3.chunks_ref
  78.5 0.8 %shard_map.68 = f32[64,4096]{1,0:T(8,128)} custom-call(s32[1]{0:T(128)} %bitcast.half_ref, f32[4,64,512]{2,1,0:T(8,128)S(1)} %collective-permute-done.3.chunks_ref, f32[64,4096]{1,0:T(8,128)} %shard_map.67.begun_ref), custom_call_target="tpu_custom_call", output_to_operand_aliasing={{}: (2, {})} | custom-call | bytes 1048576 | tf_op jit(solution)/shard_map/pallas_call | solution.py:411
  (7 shorter events, 0.1 us)
Async XLA Ops:
  0.9 1.6 %copy-start.1 = (bf16[256,4096]{1,0:T(8,128)(2,1)S(1)}, bf16[256,4096]{1,0:T(8,128)(2,1)}, u32[]{:S(2)}) copy-start(bf16[256,4096]{1,0:T(8,128)(2,1)} %signal_ref.1) | copy-start | bytes 6291460
  2.5 9.7 %copy-start = (f32[64,4096]{1,0:T(8,128)S(1)}, f32[64,4096]{1,0:T(8,128)}, u32[]{:S(2)}) copy-start(f32[64,4096]{1,0:T(8,128)} %after_ref) | copy-start | bytes 3145732
  2.5 9.7 %copy-start.2 = (f32[64,128]{1,0:T(8,128)S(1)}, f32[64,128]{1,0:T(8,128)}, u32[]{:S(2)}) copy-start(f32[64,128]{1,0:T(8,128)} %refs_9_.1) | copy-start | bytes 98308
  2.9 4.2 %collective-permute-start = (f32[4,272,128]{2,1,0:T(8,128)S(1)}, f32[4,272,128]{2,1,0:T(8,128)S(1)}, u32[]{:S(2)}, u32[]{:S(2)}) collective-permute-start(f32[4,272,128]{2,1,0:T(8,128)S(1)} %get-tuple-element.19), channel_id=1, source_target_pairs={{0,32},{32,0},{1,33},{33,1},{2,34},{34,2},{3,35},{35,3},{4,36},{36... | collective-permute-start | bytes 1671176 | tf_op jit(solution)/shard_map/ppermute | solution.py:452
  8.0 13.4 %all-to-all-start = ((f32[4,272,128]{2,1,0:T(8,128)}), f32[4,272,128]{2,1,0:T(8,128)S(1)}, u32[]{:S(2)}, u32[]{:S(2)}) async-start(f32[4,272,128]{2,1,0:T(8,128)} %add.11), calls=%async_computation | async-start | bytes 1114112 | tf_op jit(solution)/shard_map/all_to_all | solution.py:455
  14.0 43.3 %copy-start.3 = (f32[64]{0:T(128)S(1)}, f32[64]{0:T(128)}, u32[]{:S(2)}) copy-start(f32[64]{0:T(128)} %param.10) | copy-start | bytes 772
  38.4 18.9 %collective-permute-start.2 = (f32[336,128]{1,0:T(8,128)S(1)}, f32[336,128]{1,0:T(8,128)S(1)}, u32[]{:S(2)}, u32[]{:S(2)}) collective-permute-start(f32[336,128]{1,0:T(8,128)S(1)} %pad_maximum_fusion), channel_id=1, source_target_pairs={{224,1},{225,2},{226,3},{227,4},{228,5},{229,6},{230,7},{231,264},... | collective-permute-start | bytes 516104 | tf_op jit(solution)/shard_map/ppermute | solution.py:464
  49.3 8.1 %collective-permute-start.1 = (f32[144,128]{1,0:T(8,128)S(1)}, f32[144,128]{1,0:T(8,128)S(1)}, u32[]{:S(2)}, u32[]{:S(2)}) collective-permute-start(f32[144,128]{1,0:T(8,128)S(1)} %pad_maximum_fusion.1), channel_id=1, source_target_pairs={{0,32},{32,0},{1,33},{33,1},{2,34},{34,2},{3,35},{35,3},{4,36},{36... | collective-permute-start | bytes 221192 | tf_op jit(solution)/shard_map/ppermute | solution.py:466
  73.2 5.3 %collective-permute-start.3 = (f32[4,64,512]{2,1,0:T(8,128)S(1)}, f32[4,64,512]{2,1,0:T(8,128)S(1)}, u32[]{:S(2)}, u32[]{:S(2)}) collective-permute-start(f32[4,64,512]{2,1,0:T(8,128)S(1)} %all_to_all.10.chunks_ref), channel_id=1, source_target_pairs={{0,32},{32,0},{1,33},{33,1},{2,34},{34,2},{3,35},{35,3},{4,36},{36... | collective-permute-start | bytes 1572872 | tf_op jit(solution)/shard_map/ppermute | solution.py:475

commit v8 on v7

--- a/solution.py
+++ b/solution.py
@@ -14,7 +14,6 @@
 TILES = CHUNK // LANES
 BODY = TILES * ATOMS
 ROWS = BODY + 16
-HALO = BODY // 2 + 16
 RIM = LANES + ATOMS
 NARROW, WIDE = 48, 56
 RUN = 8
@@ -268,9 +267,9 @@
 
 
 def steps_body(
-    total, begin_ref, place_ref, step_ref, mine_ref, inner_ref, outer_ref, rebuilt_ref, beyond_ref,
-    point_ref, temporal_ref, threshold_ref, out_ref, taps_ref, spread_ref, inputs_ref, sums_ref,
-    cross_ref, side_ref, mix_ref,
+    total, begin_ref, place_ref, step_ref, mine_ref, inner_ref, outer_ref, rim_ref, rebuilt_ref,
+    beyond_ref, point_ref, temporal_ref, threshold_ref, out_ref, taps_ref, spread_ref, inputs_ref,
+    sums_ref, cross_ref, side_ref, mix_ref,
 ):
     begin, place = begin_ref[0], place_ref[0]
     first = place % 2 == 0
@@ -299,7 +298,7 @@
     left_half = lax.broadcasted_iota(jnp.int32, (1, LANES), 1) < ATOMS
     at_start = left_half & (place == 0)
     at_end = jnp.logical_not(left_half) & (place == CHUNKS - 1)
-    added = outer_ref[HALO : HALO + LANES]
+    added = rim_ref[:LANES]
     swapped = pltpu.roll(added, ATOMS, 1)
     to_segments(
         jnp.concatenate(
@@ -316,7 +315,7 @@
     rebuilt = rebuilt_ref[...] + side_ref[...]
     added_beyond = jnp.where(left_half, swapped, added)
     rebuilt_beyond = beyond_ref[...] + jnp.where(place == CHUNKS - 1, added_beyond, 0.0)
-    rim = outer_ref[HALO + LANES :]
+    rim = rim_ref[LANES:]
     rim = jnp.concatenate([rim, rim], axis=0).T
     to_segments(
         jnp.concatenate(
@@ -364,24 +363,27 @@
 
     cross_ref[...] = update.reshape(8 * NARROW, LANES)
     columns = from_segments(cross_ref, NARROW).T
-    out_ref[...] = jnp.concatenate([columns[:ATOMS, 128:], columns[ATOMS:, :256]], axis=1)
-
-
-def steps(total, begin, place, step_size, mine, inner, outer, before_steps, temporal, threshold):
+    for i in range(QUARTER):
+        out_ref[i] = jnp.concatenate([columns[:ATOMS, 128:], columns[ATOMS:, :256]], axis=1)
+
+
+def steps(
+    total, begin, place, step_size, mine, inner, outer, rim, before_steps, temporal, threshold
+):
     def body(*refs):
         steps_body(total, *refs)
 
     return pl.pallas_call(
         body,
-        in_specs=[SMEM] * 3 + [VMEM] * 8,
+        in_specs=[SMEM] * 3 + [VMEM] * 9,
         out_specs=VMEM,
-        out_shape=jax.ShapeDtypeStruct((ATOMS, CHUNK), F32),
+        out_shape=jax.ShapeDtypeStruct((QUARTER, ATOMS, CHUNK), F32),
         scratch_shapes=filter_scratch(NARROW)
         + [pltpu.VMEM((8 * NARROW, LANES), F32)] * 2
         + [pltpu.VMEM((LANES, LANES), F32)],
         compiler_params=params(12),
         cost_estimate=cost(6 * 8 * NARROW * LANES * LENGTH, 2**20),
-    )(begin, place, step_size, mine, inner, outer, *before_steps, temporal, threshold)
+    )(begin, place, step_size, mine, inner, outer, rim, *before_steps, temporal, threshold)
 
 
 def place_copies(half, chunks_ref, out_ref, sems):
@@ -429,16 +431,18 @@
     def device(zh, q, tm):
         return (zh * CHUNKS + q) * blocks + tm
 
-    inside, rims = [], []
+    outside, rims = [], []
     for zh in range(2):
         for tm in range(blocks):
             for q in range(1, CHUNKS - 1, 2):
-                inside.append((device(zh, q, tm), device(zh, q + 1, tm)))
+                outside.append((device(zh, q, tm), device(zh, q + 1, tm)))
             if tm + 1 < blocks:
+                last = device(zh, CHUNKS - 1, tm)
                 near = 1 - zh if (tm + 1) % RUN == 0 else zh
-                rims.append((device(zh, CHUNKS - 1, tm), device(near, 0, tm + 1)))
+                outside.append((last, device(zh, 0, tm + 1)))
+                rims.append((last, device(near, 0, tm + 1)))
+    outside = outside + [(b, a) for a, b in outside]
     rims = rims + [(b, a) for a, b in rims]
-    outside = rims + inside + [(b, a) for a, b in inside]
 
     def per_device(signal, spatial, temporal, activations, threshold, step_size):
         half = lax.axis_index("c").astype(jnp.int32)
@@ -454,24 +458,24 @@
         activations, summed = lax.optimization_barrier((activations, summed))
         pieces = lax.all_to_all(summed, "y", 0, 0, tiled=True)
         *before_steps, rim = rebuild(place[None], temporal, activations)
+        rim = lax.ppermute(rim, line, rims)
         group_sum = jnp.sum(pieces, axis=0)
-        group_sum, before_steps, rim = lax.optimization_barrier((group_sum, before_steps, rim))
+        group_sum, before_steps = lax.optimization_barrier((group_sum, before_steps))
         mine = jnp.sum(lax.all_gather(group_sum, "zh", axis=0), axis=0)
 
         first = half == 0
         start, end, gram = mine[: BODY // 2], mine[BODY // 2 : BODY], mine[BODY:]
-        outer = jnp.concatenate([jnp.where(first, start, end), gram, rim], axis=0)
+        outer = jnp.concatenate([jnp.where(first, start, end), gram], axis=0)
         outer = lax.ppermute(outer, line, outside)
         inner = jnp.concatenate([jnp.where(first, end, start), gram], axis=0)
         inner = lax.ppermute(inner, "c", swap)
         begin = time_block * width + place * CHUNK
         update = steps(
-            blocks * width, begin[None], place[None], step_size, mine, inner, outer, before_steps,
-            temporal, threshold[None, :],
+            blocks * width, begin[None], place[None], step_size, mine, inner, outer, rim,
+            before_steps, temporal, threshold[None, :],
         )
 
-        copies = jnp.broadcast_to(update[None], (QUARTER, ATOMS, CHUNK))
-        gathered = lax.all_to_all(copies, "y", 0, 0, tiled=True)
+        gathered = lax.all_to_all(update, "y", 0, 0, tiled=True)
         other = lax.ppermute(gathered, "c", swap)
         return place_half(half[None], other, place_half(half[None], gathered))
 

time: 79.7 us -> 78.1 us (0.980)
  starting transfers between devices: 28.6 us -> 27.6 us
    ppermute x1, starting transfers between devices: 7.21 us -> 2.88 us  [per_device(): inner = lax.ppermute(inner, 'c', swap)]
    ppermute x1, starting transfers between devices: 3.8 us -> 6.47 us  [per_device(): other = lax.ppermute(gathered, 'c', swap)]
  transfers between devices with their start and end apart: 5 -> 6, of which waited for: 4 -> 4; matrix products, arithmetic and copies ran while one was open for 0% -> 0% of each run, Pallas kernels for 3% -> 3%
where the time goes in v8:
time: 78.1 us; the launch traced here: 77.7 us
  blocking collectives  28 us (36%)
  starting transfers between devices  27.6 us (35%)
  waiting for transfers between devices  9.16 us (12%)
  Pallas kernels  8.82 us (11%)
  other arithmetic  1.79 us (2%)
  local copies, waits for them, and re-layouts  1.6 us (2%)
  between operations  0.81 us (1%)
    all_gather x1, blocking collectives, per_device(): mine = jnp.sum(lax.all_gather(group_sum, 'zh', axis=0), axis=0)  16.9 us
    all_to_all x1, blocking collectives, per_device(): gathered = lax.all_to_all(update, 'y', 0, 0, tiled=True)  11.1 us
    ppermute x1, starting transfers between devices, per_device(): outer = lax.ppermute(outer, line, outside)  10.8 us
    all_to_all x1, waiting for transfers between devices, per_device(): pieces = lax.all_to_all(summed, 'y', 0, 0, tiled=True)  6.69 us
    ppermute x1, starting transfers between devices, per_device(): other = lax.ppermute(gathered, 'c', swap)  6.47 us
    pallas_call x1, Pallas kernels, steps(): pl.pallas_call(body, in_specs=[SMEM] * 3 + [VMEM] * 9, out_specs=VMEM, ou...  4.84 us
    all_to_all x1, starting transfers between devices, per_device(): pieces = lax.all_to_all(summed, 'y', 0, 0, tiled=True)  4.18 us
    ppermute x1, starting transfers between devices, per_device(): inner = lax.ppermute(inner, 'c', swap)  2.88 us
  transfers between devices with their start and end apart: 6, of which 4 were waited for; matrix products, arithmetic and copies ran while one was open for 0% of the time, Pallas kernels for 3%

profile of v8, /device:TPU:7, one launch (start us, length us, event | category | flops | bytes accessed | tf_op | source)
XLA Modules:
  0.0 77.7 jit_solution(14600276349181490794)
XLA Ops:
  0.0 0.8 %reduce-precision_convert_fusion = (bf16[64,256]{1,0:T(8,128)(2,1)S(1)}, bf16[64,256]{1,0:T(8,128)(2,1)S(1)}) fusion(f32[256,64]{0,1:T(8,128)} %param.7), kind=kLoop, calls=%fused_computation.3 | loop fusion | flops 65536 | bytes 131072 | tf_op jit(solution)/shard_map/convert
  0.9 0.0 copy-start.1
  0.9 1.6 %copy-done.1 = bf16[256,4096]{1,0:T(8,128)(2,1)S(1)} copy-done((bf16[256,4096]{1,0:T(8,128)(2,1)S(1)}, bf16[256,4096]{1,0:T(8,128)(2,1)}, u32[]{:S(2)}) %copy-start.1) | copy-done | bytes 2097176
  2.5 0.0 copy-start
  2.5 0.0 copy-start.2
  2.5 0.5 shard_map.64
  2.9 2.6 %collective-permute-start = (f32[4,272,128]{2,1,0:T(8,128)S(1)}, f32[4,272,128]{2,1,0:T(8,128)S(1)}, u32[]{:S(2)}, u32[]{:S(2)}) collective-permute-start(f32[4,272,128]{2,1,0:T(8,128)S(1)} %get-tuple-element.18), channel_id=1, source_target_pairs={{0,32},{32,0},{1,33},{33,1},{2,34},{34,2},{3,35},{35,3},{4,36},{36... | collective-permute-start | bytes 1671176 | tf_op jit(solution)/shard_map/ppermute | solution.py:456
  5.5 1.6 %collective-permute-done = f32[4,272,128]{2,1,0:T(8,128)S(1)} collective-permute-done((f32[4,272,128]{2,1,0:T(8,128)S(1)}, f32[4,272,128]{2,1,0:T(8,128)S(1)}, u32[]{:S(2)}, u32[]{:S(2)}) %collective-permute-start) | collective-permute-done | bytes 557088 | tf_op jit(solution)/shard_map/ppermute | solution.py:456
  7.1 0.9 %add.11 = f32[4,272,128]{2,1,0:T(8,128)} add(f32[4,272,128]{2,1,0:T(8,128)S(1)} %get-tuple-element.17, f32[4,272,128]{2,1,0:T(8,128)S(1)} %collective-permute-done) | non-fusion elementwise | flops 139264 | bytes 1671168 | tf_op jit(solution)/shard_map/add | solution.py:456
  8.0 4.2 %all-to-all-start = ((f32[4,272,128]{2,1,0:T(8,128)}), f32[4,272,128]{2,1,0:T(8,128)S(1)}, u32[]{:S(2)}, u32[]{:S(2)}) async-start(f32[4,272,128]{2,1,0:T(8,128)} %add.11), calls=%async_computation | async-start | bytes 1114112 | tf_op jit(solution)/shard_map/all_to_all | solution.py:459
  12.1 0.0 copy-done
  12.1 0.0 copy-done.2
  12.2 1.9 %shard_map.65 = (f32[384,128]{1,0:T(8,128)S(1)}, f32[128,128]{1,0:T(8,128)S(1)}, f32[384,128]{1,0:T(8,128)S(1)}, f32[192,128]{1,0:T(8,128)S(1)}) custom-call(s32[1]{0:T(128)} %bitcast.2.place_ref.refs_1_, f32[64,128]{1,0:T(8,128)S(1)} %copy-done.2, f32[64,4096]{1,0:T(8,128)S(1)} %copy-done, f32[64,4096]{1,0:T(8,128)S(1)} %copy-done, f32[64,4096]{1,0:T(8,128)S(1)} %copy-done, ...), custom_call_target="tpu_custom_call" | custom-call | flops 14680064 | bytes 1048576 | tf_op jit(solution)/shard_map/pallas_call | solution.py:248
  14.0 0.0 copy-start.3
  14.0 0.7 collective-permute-start.3
  14.7 6.7 %all-to-all-done = f32[4,272,128]{2,1,0:T(8,128)S(1)} async-done(((f32[4,272,128]{2,1,0:T(8,128)}), f32[4,272,128]{2,1,0:T(8,128)S(1)}, u32[]{:S(2)}, u32[]{:S(2)}) %all-to-all-start) | async-done | bytes 557088 | tf_op jit(solution)/shard_map/all_to_all | solution.py:459
  21.4 16.9 %all-gather = f32[544,128]{1,0:T(8,128)S(1)} all-gather(f32[272,128]{1,0:T(8,128)S(1)} %reduce_sum.18), channel_id=2, replica_groups=mesh['zh'=2,'y'=4,'c'=2,'tm'=32] {'zh'}, dimensions={0}, use_global_device_ids=true | all-gather | bytes 417792 | tf_op jit(solution)/shard_map/all_gather | solution.py:464
  38.4 10.8 %collective-permute-start.2 = (f32[144,128]{1,0:T(8,128)S(1)}, f32[144,128]{1,0:T(8,128)S(1)}, u32[]{:S(2)}, u32[]{:S(2)}) collective-permute-start(f32[144,128]{1,0:T(8,128)S(1)} %get-tuple-element.33), channel_id=1, source_target_pairs={{32,64},{96,128},{160,192},{224,1},{33,65},{97,129},{161,193},{225... | collective-permute-start | bytes 221192 | tf_op jit(solution)/shard_map/ppermute | solution.py:469
  49.2 2.9 %collective-permute-start.1 = (f32[144,128]{1,0:T(8,128)S(1)}, f32[144,128]{1,0:T(8,128)S(1)}, u32[]{:S(2)}, u32[]{:S(2)}) collective-permute-start(f32[144,128]{1,0:T(8,128)S(1)} %get-tuple-element.34), channel_id=1, source_target_pairs={{0,32},{32,0},{1,33},{33,1},{2,34},{34,2},{3,35},{35,3},{4,36},{36... | collective-permute-start | bytes 221192 | tf_op jit(solution)/shard_map/ppermute | solution.py:471
  52.8 0.0 collective-permute-done.3.refs_6_
  52.8 0.0 collective-permute-done.2.refs_5_
  52.8 0.2 collective-permute-done.1.refs_4_
  53.0 0.0 copy-done.3
  53.0 4.8 %shard_map.66 = f32[4,64,512]{2,1,0:T(8,128)S(1)} custom-call(s32[1]{0:T(128)} %bitcast.1.refs_0_, s32[1]{0:T(128)} %bitcast.2.place_ref.refs_1_, f32[1]{0:T(128)S(6)} %copy.9.refs_2_, f32[272,128]{1,0:T(8,128)S(1)} %reduce_sum.19.refs_3_, f32[144,128]{1,0:T(8,128)S(1)} %collective-permute-done.1.refs_4_, f32[144,128]{1,0:T(8,128)S(1)} %collective-permute-done.2.refs_5_, ...), custom_call_target="tpu_custom_call" | custom-call | flops 37748736 | bytes 1048576 | tf_op jit(solution)/shard_map/pallas_call | solution.py:376
  57.9 11.1 %all_to_all.10.chunks_ref = f32[4,64,512]{2,1,0:T(8,128)S(1)} all-to-all(f32[4,64,512]{2,1,0:T(8,128)S(1)} %shard_map.66), channel_id=1, replica_groups=mesh['zh'=2,'y'=4,'c'=2,'tm'=32] {'y'}, dimensions={0} | all-to-all | bytes 1048576 | tf_op jit(solution)/shard_map/all_to_all | solution.py:478
  68.9 6.5 %collective-permute-start.4 = (f32[4,64,512]{2,1,0:T(8,128)S(1)}, f32[4,64,512]{2,1,0:T(8,128)S(1)}, u32[]{:S(2)}, u32[]{:S(2)}) collective-permute-start(f32[4,64,512]{2,1,0:T(8,128)S(1)} %all_to_all.10.chunks_ref), channel_id=1, source_target_pairs={{0,32},{32,0},{1,33},{33,1},{2,34},{34,2},{3,35},{35,3},{4,36},{36... | collective-permute-start | bytes 1572872 | tf_op jit(solution)/shard_map/ppermute | solution.py:479
  75.4 0.8 %shard_map.67.begun_ref = f32[64,4096]{1,0:T(8,128)} custom-call(s32[1]{0:T(128)} %bitcast.half_ref, f32[4,64,512]{2,1,0:T(8,128)S(1)} %all_to_all.10.chunks_ref), custom_call_target="tpu_custom_call" | custom-call | bytes 1048576 | tf_op jit(solution)/shard_map/pallas_call | solution.py:413
  76.2 0.7 collective-permute-done.4.chunks_ref
  76.9 0.8 %shard_map.68 = f32[64,4096]{1,0:T(8,128)} custom-call(s32[1]{0:T(128)} %bitcast.half_ref, f32[4,64,512]{2,1,0:T(8,128)S(1)} %collective-permute-done.4.chunks_ref, f32[64,4096]{1,0:T(8,128)} %shard_map.67.begun_ref), custom_call_target="tpu_custom_call", output_to_operand_aliasing={{}: (2, {})} | custom-call | bytes 1048576 | tf_op jit(solution)/shard_map/pallas_call | solution.py:413
  (6 shorter events, 0.1 us)
Async XLA Ops:
  0.9 1.6 %copy-start.1 = (bf16[256,4096]{1,0:T(8,128)(2,1)S(1)}, bf16[256,4096]{1,0:T(8,128)(2,1)}, u32[]{:S(2)}) copy-start(bf16[256,4096]{1,0:T(8,128)(2,1)} %signal_ref.1) | copy-start | bytes 6291460
  2.5 9.7 %copy-start = (f32[64,4096]{1,0:T(8,128)S(1)}, f32[64,4096]{1,0:T(8,128)}, u32[]{:S(2)}) copy-start(f32[64,4096]{1,0:T(8,128)} %after_ref) | copy-start | bytes 3145732
  2.5 9.7 %copy-start.2 = (f32[64,128]{1,0:T(8,128)S(1)}, f32[64,128]{1,0:T(8,128)}, u32[]{:S(2)}) copy-start(f32[64,128]{1,0:T(8,128)} %refs_10_.1) | copy-start | bytes 98308
  2.9 4.2 %collective-permute-start = (f32[4,272,128]{2,1,0:T(8,128)S(1)}, f32[4,272,128]{2,1,0:T(8,128)S(1)}, u32[]{:S(2)}, u32[]{:S(2)}) collective-permute-start(f32[4,272,128]{2,1,0:T(8,128)S(1)} %get-tuple-element.18), channel_id=1, source_target_pairs={{0,32},{32,0},{1,33},{33,1},{2,34},{34,2},{3,35},{35,3},{4,36},{36... | collective-permute-start | bytes 1671176 | tf_op jit(solution)/shard_map/ppermute | solution.py:456
  8.0 13.4 %all-to-all-start = ((f32[4,272,128]{2,1,0:T(8,128)}), f32[4,272,128]{2,1,0:T(8,128)S(1)}, u32[]{:S(2)}, u32[]{:S(2)}) async-start(f32[4,272,128]{2,1,0:T(8,128)} %add.11), calls=%async_computation | async-start | bytes 1114112 | tf_op jit(solution)/shard_map/all_to_all | solution.py:459
  14.0 39.0 %copy-start.3 = (f32[64]{0:T(128)S(1)}, f32[64]{0:T(128)}, u32[]{:S(2)}) copy-start(f32[64]{0:T(128)} %param.10) | copy-start | bytes 772
  14.0 38.8 %collective-permute-start.3 = (f32[192,128]{1,0:T(8,128)S(1)}, f32[192,128]{1,0:T(8,128)S(1)}, u32[]{:S(2)}, u32[]{:S(2)}) collective-permute-start(f32[192,128]{1,0:T(8,128)S(1)} %get-tuple-element.25), channel_id=1, source_target_pairs={{224,1},{225,2},{226,3},{227,4},{228,5},{229,6},{230,7},{231,264},... | collective-permute-start | bytes 294920 | tf_op jit(solution)/shard_map/ppermute | solution.py:461
  38.4 14.4 %collective-permute-start.2 = (f32[144,128]{1,0:T(8,128)S(1)}, f32[144,128]{1,0:T(8,128)S(1)}, u32[]{:S(2)}, u32[]{:S(2)}) collective-permute-start(f32[144,128]{1,0:T(8,128)S(1)} %get-tuple-element.33), channel_id=1, source_target_pairs={{32,64},{96,128},{160,192},{224,1},{33,65},{97,129},{161,193},{225... | collective-permute-start | bytes 221192 | tf_op jit(solution)/shard_map/ppermute | solution.py:469
  49.2 3.8 %collective-permute-start.1 = (f32[144,128]{1,0:T(8,128)S(1)}, f32[144,128]{1,0:T(8,128)S(1)}, u32[]{:S(2)}, u32[]{:S(2)}) collective-permute-start(f32[144,128]{1,0:T(8,128)S(1)} %get-tuple-element.34), channel_id=1, source_target_pairs={{0,32},{32,0},{1,33},{33,1},{2,34},{34,2},{3,35},{35,3},{4,36},{36... | collective-permute-start | bytes 221192 | tf_op jit(solution)/shard_map/ppermute | solution.py:471
  68.9 8.0 %collective-permute-start.4 = (f32[4,64,512]{2,1,0:T(8,128)S(1)}, f32[4,64,512]{2,1,0:T(8,128)S(1)}, u32[]{:S(2)}, u32[]{:S(2)}) collective-permute-start(f32[4,64,512]{2,1,0:T(8,128)S(1)} %all_to_all.10.chunks_ref), channel_id=1, source_target_pairs={{0,32},{32,0},{1,33},{33,1},{2,34},{34,2},{3,35},{35,3},{4,36},{36... | collective-permute-start | bytes 1572872 | tf_op jit(solution)/shard_map/ppermute | solution.py:479

commit v9 on v8

--- a/solution.py
+++ b/solution.py
@@ -30,6 +30,25 @@
 
 def params(mebibytes):
     return pltpu.CompilerParams(vmem_limit_bytes=mebibytes * 2**20)
+
+
+def split_body(spatial_ref, parts_ref):
+    spatial = spatial_ref[...]
+    high = spatial.astype(jnp.bfloat16)
+    parts_ref[:ATOMS] = high
+    parts_ref[ATOMS:] = (spatial - high.astype(F32)).astype(jnp.bfloat16)
+
+
+def two_parts(spatial):
+    rows, channels = spatial.shape
+    return pl.pallas_call(
+        split_body,
+        in_specs=[VMEM],
+        out_specs=VMEM,
+        out_shape=jax.ShapeDtypeStruct((2 * rows, channels), jnp.bfloat16),
+        compiler_params=params(8),
+        cost_estimate=cost(2**30, 2**17),
+    )(spatial)
 
 
 def project_body(half_ref, parts_ref, signal_ref, away_ref, kept_ref):
@@ -449,9 +468,7 @@
         place = lax.axis_index("y").astype(jnp.int32) * 2 + half
         time_block = lax.axis_index("tm").astype(jnp.int32)
         width = activations.shape[1]
-        spatial = spatial.T
-        high = lax.reduce_precision(spatial, 8, 7)
-        parts = jnp.concatenate([high, spatial - high], axis=0).astype(jnp.bfloat16)
+        parts = two_parts(spatial.T)
         away, kept = project(half[None], parts, signal)
         summed = kept + lax.ppermute(away, "c", swap)
 

time: 78.1 us -> 77.3 us (0.990)
  other arithmetic: 1.79 us -> 0.93 us
    another operation x1 -> x0, other arithmetic: 0.85 us -> none
    unnamed x8 -> x10, local copies, waits for them, and re-layouts: 1.6 us -> 1.62 us
  transfers between devices with their start and end apart: 6 -> 6, of which waited for: 4 -> 4; matrix products, arithmetic and copies ran while one was open for 0% -> 0% of each run, Pallas kernels for 3% -> 4%
where the time goes in v9:
time: 77.3 us; the launch traced here: 76.9 us
  blocking collectives  28 us (36%)
  starting transfers between devices  27.6 us (36%)
  waiting for transfers between devices  9.16 us (12%)
  Pallas kernels  8.83 us (11%)
  local copies, waits for them, and re-layouts  1.62 us (2%)
  other arithmetic  0.93 us (1%)
  between operations  0.79 us (1%)
    all_gather x1, blocking collectives, per_device(): mine = jnp.sum(lax.all_gather(group_sum, 'zh', axis=0), axis=0)  16.9 us
    all_to_all x1, blocking collectives, per_device(): gathered = lax.all_to_all(update, 'y', 0, 0, tiled=True)  11.1 us
    ppermute x1, starting transfers between devices, per_device(): outer = lax.ppermute(outer, line, outside)  10.8 us
    all_to_all x1, waiting for transfers between devices, per_device(): pieces = lax.all_to_all(summed, 'y', 0, 0, tiled=True)  6.69 us
    ppermute x1, starting transfers between devices, per_device(): other = lax.ppermute(gathered, 'c', swap)  6.48 us
    pallas_call x1, Pallas kernels, steps(): pl.pallas_call(body, in_specs=[SMEM] * 3 + [VMEM] * 9, out_specs=VMEM, ou...  4.84 us
    all_to_all x1, starting transfers between devices, per_device(): pieces = lax.all_to_all(summed, 'y', 0, 0, tiled=True)  4.19 us
    ppermute x1, starting transfers between devices, per_device(): inner = lax.ppermute(inner, 'c', swap)  2.9 us
  transfers between devices with their start and end apart: 6, of which 4 were waited for; matrix products, arithmetic and copies ran while one was open for 0% of the time, Pallas kernels for 4%

profile of v9, /device:TPU:7, one launch (start us, length us, event | category | flops | bytes accessed | tf_op | source)
XLA Modules:
  0.0 76.9 jit_solution(2207760954831488077)
XLA Ops:
  0.0 0.0 copy-start.1
  0.0 0.0 copy-start.4
  0.0 1.0 %copy-done.4 = f32[256,64]{0,1:T(8,128)S(1)} copy-done((f32[256,64]{0,1:T(8,128)S(1)}, f32[256,64]{0,1:T(8,128)}, u32[]{:S(2)}) %copy-start.4) | copy-done | bytes 65560
  1.0 0.6 copy-done.1
  1.6 0.0 copy-start
  1.6 0.0 copy-start.2
  1.6 0.5 shard_map.65
  2.1 2.6 %collective-permute-start = (f32[4,272,128]{2,1,0:T(8,128)S(1)}, f32[4,272,128]{2,1,0:T(8,128)S(1)}, u32[]{:S(2)}, u32[]{:S(2)}) collective-permute-start(f32[4,272,128]{2,1,0:T(8,128)S(1)} %get-tuple-element.18), channel_id=1, source_target_pairs={{0,32},{32,0},{1,33},{33,1},{2,34},{34,2},{3,35},{35,3},{4,36},{36... | collective-permute-start | bytes 1671176 | tf_op jit(solution)/shard_map/ppermute | solution.py:473
  4.7 1.6 %collective-permute-done = f32[4,272,128]{2,1,0:T(8,128)S(1)} collective-permute-done((f32[4,272,128]{2,1,0:T(8,128)S(1)}, f32[4,272,128]{2,1,0:T(8,128)S(1)}, u32[]{:S(2)}, u32[]{:S(2)}) %collective-permute-start) | collective-permute-done | bytes 557088 | tf_op jit(solution)/shard_map/ppermute | solution.py:473
  6.3 0.9 %add.11 = f32[4,272,128]{2,1,0:T(8,128)} add(f32[4,272,128]{2,1,0:T(8,128)S(1)} %get-tuple-element.17, f32[4,272,128]{2,1,0:T(8,128)S(1)} %collective-permute-done) | non-fusion elementwise | flops 139264 | bytes 1671168 | tf_op jit(solution)/shard_map/add | solution.py:473
  7.1 4.2 %all-to-all-start = ((f32[4,272,128]{2,1,0:T(8,128)}), f32[4,272,128]{2,1,0:T(8,128)S(1)}, u32[]{:S(2)}, u32[]{:S(2)}) async-start(f32[4,272,128]{2,1,0:T(8,128)} %add.11), calls=%async_computation | async-start | bytes 1114112 | tf_op jit(solution)/shard_map/all_to_all | solution.py:476
  11.3 0.0 copy-done
  11.3 0.0 copy-done.2
  11.3 1.9 %shard_map.66 = (f32[384,128]{1,0:T(8,128)S(1)}, f32[128,128]{1,0:T(8,128)S(1)}, f32[384,128]{1,0:T(8,128)S(1)}, f32[192,128]{1,0:T(8,128)S(1)}) custom-call(s32[1]{0:T(128)} %bitcast.2.place_ref.refs_1_, f32[64,128]{1,0:T(8,128)S(1)} %copy-done.2, f32[64,4096]{1,0:T(8,128)S(1)} %copy-done, f32[64,4096]{1,0:T(8,128)S(1)} %copy-done, f32[64,4096]{1,0:T(8,128)S(1)} %copy-done, ...), custom_call_target="tpu_custom_call" | custom-call | flops 14680064 | bytes 1048576 | tf_op jit(solution)/shard_map/pallas_call | solution.py:267
  13.2 0.0 copy-start.3
  13.2 0.7 collective-permute-start.3
  13.9 6.7 %all-to-all-done = f32[4,272,128]{2,1,0:T(8,128)S(1)} async-done(((f32[4,272,128]{2,1,0:T(8,128)}), f32[4,272,128]{2,1,0:T(8,128)S(1)}, u32[]{:S(2)}, u32[]{:S(2)}) %all-to-all-start) | async-done | bytes 557088 | tf_op jit(solution)/shard_map/all_to_all | solution.py:476
  20.6 16.9 %all-gather = f32[544,128]{1,0:T(8,128)S(1)} all-gather(f32[272,128]{1,0:T(8,128)S(1)} %reduce_sum.18), channel_id=2, replica_groups=mesh['zh'=2,'y'=4,'c'=2,'tm'=32] {'zh'}, dimensions={0}, use_global_device_ids=true | all-gather | bytes 417792 | tf_op jit(solution)/shard_map/all_gather | solution.py:481
  37.6 10.8 %collective-permute-start.2 = (f32[144,128]{1,0:T(8,128)S(1)}, f32[144,128]{1,0:T(8,128)S(1)}, u32[]{:S(2)}, u32[]{:S(2)}) collective-permute-start(f32[144,128]{1,0:T(8,128)S(1)} %get-tuple-element.31), channel_id=1, source_target_pairs={{32,64},{96,128},{160,192},{224,1},{33,65},{97,129},{161,193},{225... | collective-permute-start | bytes 221192 | tf_op jit(solution)/shard_map/ppermute | solution.py:486
  48.4 2.9 %collective-permute-start.1 = (f32[144,128]{1,0:T(8,128)S(1)}, f32[144,128]{1,0:T(8,128)S(1)}, u32[]{:S(2)}, u32[]{:S(2)}) collective-permute-start(f32[144,128]{1,0:T(8,128)S(1)} %get-tuple-element.32), channel_id=1, source_target_pairs={{0,32},{32,0},{1,33},{33,1},{2,34},{34,2},{3,35},{35,3},{4,36},{36... | collective-permute-start | bytes 221192 | tf_op jit(solution)/shard_map/ppermute | solution.py:488
  52.0 0.0 collective-permute-done.3.refs_6_
  52.0 0.0 collective-permute-done.2.refs_5_
  52.0 0.2 collective-permute-done.1.refs_4_
  52.2 0.0 copy-done.3
  52.2 4.8 %shard_map.67 = f32[4,64,512]{2,1,0:T(8,128)S(1)} custom-call(s32[1]{0:T(128)} %bitcast.1.refs_0_, s32[1]{0:T(128)} %bitcast.2.place_ref.refs_1_, f32[1]{0:T(128)S(6)} %copy.9.refs_2_, f32[272,128]{1,0:T(8,128)S(1)} %reduce_sum.19.refs_3_, f32[144,128]{1,0:T(8,128)S(1)} %collective-permute-done.1.refs_4_, f32[144,128]{1,0:T(8,128)S(1)} %collective-permute-done.2.refs_5_, ...), custom_call_target="tpu_custom_call" | custom-call | flops 37748736 | bytes 1048576 | tf_op jit(solution)/shard_map/pallas_call | solution.py:395
  57.0 11.1 %all_to_all.10.chunks_ref = f32[4,64,512]{2,1,0:T(8,128)S(1)} all-to-all(f32[4,64,512]{2,1,0:T(8,128)S(1)} %shard_map.67), channel_id=1, replica_groups=mesh['zh'=2,'y'=4,'c'=2,'tm'=32] {'y'}, dimensions={0} | all-to-all | bytes 1048576 | tf_op jit(solution)/shard_map/all_to_all | solution.py:495
  68.1 6.5 %collective-permute-start.4 = (f32[4,64,512]{2,1,0:T(8,128)S(1)}, f32[4,64,512]{2,1,0:T(8,128)S(1)}, u32[]{:S(2)}, u32[]{:S(2)}) collective-permute-start(f32[4,64,512]{2,1,0:T(8,128)S(1)} %all_to_all.10.chunks_ref), channel_id=1, source_target_pairs={{0,32},{32,0},{1,33},{33,1},{2,34},{34,2},{3,35},{35,3},{4,36},{36... | collective-permute-start | bytes 1572872 | tf_op jit(solution)/shard_map/ppermute | solution.py:496
  74.6 0.8 %shard_map.68.begun_ref = f32[64,4096]{1,0:T(8,128)} custom-call(s32[1]{0:T(128)} %bitcast.half_ref, f32[4,64,512]{2,1,0:T(8,128)S(1)} %all_to_all.10.chunks_ref), custom_call_target="tpu_custom_call" | custom-call | bytes 1048576 | tf_op jit(solution)/shard_map/pallas_call | solution.py:432
  75.4 0.7 collective-permute-done.4.chunks_ref
  76.1 0.8 %shard_map.69 = f32[64,4096]{1,0:T(8,128)} custom-call(s32[1]{0:T(128)} %bitcast.half_ref, f32[4,64,512]{2,1,0:T(8,128)S(1)} %collective-permute-done.4.chunks_ref, f32[64,4096]{1,0:T(8,128)} %shard_map.68.begun_ref), custom_call_target="tpu_custom_call", output_to_operand_aliasing={{}: (2, {})} | custom-call | bytes 1048576 | tf_op jit(solution)/shard_map/pallas_call | solution.py:432
  (6 shorter events, 0.1 us)
Async XLA Ops:
  0.0 1.6 %copy-start.1 = (bf16[256,4096]{1,0:T(8,128)(2,1)S(1)}, bf16[256,4096]{1,0:T(8,128)(2,1)}, u32[]{:S(2)}) copy-start(bf16[256,4096]{1,0:T(8,128)(2,1)} %signal_ref.1) | copy-start | bytes 6291460
  0.0 1.0 %copy-start.4 = (f32[256,64]{0,1:T(8,128)S(1)}, f32[256,64]{0,1:T(8,128)}, u32[]{:S(2)}) copy-start(f32[256,64]{0,1:T(8,128)} %param.7) | copy-start | bytes 196612
  1.6 9.7 %copy-start = (f32[64,4096]{1,0:T(8,128)S(1)}, f32[64,4096]{1,0:T(8,128)}, u32[]{:S(2)}) copy-start(f32[64,4096]{1,0:T(8,128)} %after_ref) | copy-start | bytes 3145732
  1.6 9.7 %copy-start.2 = (f32[64,128]{1,0:T(8,128)S(1)}, f32[64,128]{1,0:T(8,128)}, u32[]{:S(2)}) copy-start(f32[64,128]{1,0:T(8,128)} %refs_10_.1) | copy-start | bytes 98308
  2.1 4.2 %collective-permute-start = (f32[4,272,128]{2,1,0:T(8,128)S(1)}, f32[4,272,128]{2,1,0:T(8,128)S(1)}, u32[]{:S(2)}, u32[]{:S(2)}) collective-permute-start(f32[4,272,128]{2,1,0:T(8,128)S(1)} %get-tuple-element.18), channel_id=1, source_target_pairs={{0,32},{32,0},{1,33},{33,1},{2,34},{34,2},{3,35},{35,3},{4,36},{36... | collective-permute-start | bytes 1671176 | tf_op jit(solution)/shard_map/ppermute | solution.py:473
  7.1 13.4 %all-to-all-start = ((f32[4,272,128]{2,1,0:T(8,128)}), f32[4,272,128]{2,1,0:T(8,128)S(1)}, u32[]{:S(2)}, u32[]{:S(2)}) async-start(f32[4,272,128]{2,1,0:T(8,128)} %add.11), calls=%async_computation | async-start | bytes 1114112 | tf_op jit(solution)/shard_map/all_to_all | solution.py:476
  13.2 39.0 %copy-start.3 = (f32[64]{0:T(128)S(1)}, f32[64]{0:T(128)}, u32[]{:S(2)}) copy-start(f32[64]{0:T(128)} %param.10) | copy-start | bytes 772
  13.2 38.8 %collective-permute-start.3 = (f32[192,128]{1,0:T(8,128)S(1)}, f32[192,128]{1,0:T(8,128)S(1)}, u32[]{:S(2)}, u32[]{:S(2)}) collective-permute-start(f32[192,128]{1,0:T(8,128)S(1)} %get-tuple-element.25), channel_id=1, source_target_pairs={{224,1},{225,2},{226,3},{227,4},{228,5},{229,6},{230,7},{231,264},... | collective-permute-start | bytes 294920 | tf_op jit(solution)/shard_map/ppermute | solution.py:478
  37.6 14.4 %collective-permute-start.2 = (f32[144,128]{1,0:T(8,128)S(1)}, f32[144,128]{1,0:T(8,128)S(1)}, u32[]{:S(2)}, u32[]{:S(2)}) collective-permute-start(f32[144,128]{1,0:T(8,128)S(1)} %get-tuple-element.31), channel_id=1, source_target_pairs={{32,64},{96,128},{160,192},{224,1},{33,65},{97,129},{161,193},{225... | collective-permute-start | bytes 221192 | tf_op jit(solution)/shard_map/ppermute | solution.py:486
  48.4 3.8 %collective-permute-start.1 = (f32[144,128]{1,0:T(8,128)S(1)}, f32[144,128]{1,0:T(8,128)S(1)}, u32[]{:S(2)}, u32[]{:S(2)}) collective-permute-start(f32[144,128]{1,0:T(8,128)S(1)} %get-tuple-element.32), channel_id=1, source_target_pairs={{0,32},{32,0},{1,33},{33,1},{2,34},{34,2},{3,35},{35,3},{4,36},{36... | collective-permute-start | bytes 221192 | tf_op jit(solution)/shard_map/ppermute | solution.py:488
  68.1 8.0 %collective-permute-start.4 = (f32[4,64,512]{2,1,0:T(8,128)S(1)}, f32[4,64,512]{2,1,0:T(8,128)S(1)}, u32[]{:S(2)}, u32[]{:S(2)}) collective-permute-start(f32[4,64,512]{2,1,0:T(8,128)S(1)} %all_to_all.10.chunks_ref), channel_id=1, source_target_pairs={{0,32},{32,0},{1,33},{33,1},{2,34},{34,2},{3,35},{35,3},{4,36},{36... | collective-permute-start | bytes 1572872 | tf_op jit(solution)/shard_map/ppermute | solution.py:496

commit v10 on v9

--- a/solution.py
+++ b/solution.py
@@ -32,11 +32,17 @@
     return pltpu.CompilerParams(vmem_limit_bytes=mebibytes * 2**20)
 
 
-def split_body(spatial_ref, parts_ref):
+def split_body(spatial_ref, parts_ref, gram_ref):
     spatial = spatial_ref[...]
     high = spatial.astype(jnp.bfloat16)
-    parts_ref[:ATOMS] = high
-    parts_ref[ATOMS:] = (spatial - high.astype(F32)).astype(jnp.bfloat16)
+    low = (spatial - high.astype(F32)).astype(jnp.bfloat16)
+    parts = jnp.concatenate([high, low], axis=0)
+    parts_ref[...] = parts
+    gram = lax.dot_general(parts, parts, (((1,), (1,)), ((), ())), preferred_element_type=F32)
+    gram = gram[:ATOMS] + gram[ATOMS:]
+    gram = gram[:, :ATOMS] + gram[:, ATOMS:]
+    gram_ref[0] = jnp.concatenate([gram[:16], gram[16:32]], axis=1)
+    gram_ref[1] = jnp.concatenate([gram[32:48], gram[48:]], axis=1)
 
 
 def two_parts(spatial):
@@ -44,21 +50,20 @@
     return pl.pallas_call(
         split_body,
         in_specs=[VMEM],
-        out_specs=VMEM,
-        out_shape=jax.ShapeDtypeStruct((2 * rows, channels), jnp.bfloat16),
+        out_specs=[VMEM, VMEM],
+        out_shape=[
+            jax.ShapeDtypeStruct((2 * rows, channels), jnp.bfloat16),
+            jax.ShapeDtypeStruct((2, 16, LANES), F32),
+        ],
         compiler_params=params(8),
         cost_estimate=cost(2**30, 2**17),
     )(spatial)
 
 
-def project_body(half_ref, parts_ref, signal_ref, away_ref, kept_ref):
+def project_body(half_ref, parts_ref, gram_ref, signal_ref, away_ref, kept_ref):
     first = half_ref[0] == 0
     parts = parts_ref[...]
-    gram = lax.dot_general(parts, parts, (((1,), (1,)), ((), ())), preferred_element_type=F32)
-    gram = gram[:ATOMS] + gram[ATOMS:]
-    gram = gram[:, :ATOMS] + gram[:, ATOMS:]
-    upper = jnp.concatenate([gram[:16], gram[16:32]], axis=1)
-    lower = jnp.concatenate([gram[32:48], gram[48:]], axis=1)
+    upper, lower = gram_ref[0], gram_ref[1]
     away_gram, kept_gram = jnp.where(first, lower, upper), jnp.where(first, upper, lower)
     for i in range(QUARTER):
         away_ref[i, BODY:] = away_gram
@@ -74,16 +79,16 @@
                 out_ref[i, t * ATOMS : (t + 1) * ATOMS] = product[:, t * LANES : (t + 1) * LANES]
 
 
-def project(half, parts, signal):
+def project(half, parts, gram, signal):
     channels, width = signal.shape
     return pl.pallas_call(
         project_body,
-        in_specs=[SMEM, VMEM, VMEM],
+        in_specs=[SMEM, VMEM, VMEM, VMEM],
         out_specs=[VMEM, VMEM],
         out_shape=[jax.ShapeDtypeStruct((QUARTER, ROWS, LANES), F32)] * 2,
         compiler_params=params(8),
         cost_estimate=cost(2 * channels * LANES * width, 2 * channels * width),
-    )(half, parts, signal)
+    )(half, parts, gram, signal)
 
 
 def to_segments(rows, segment, out_ref):
@@ -468,8 +473,8 @@
         place = lax.axis_index("y").astype(jnp.int32) * 2 + half
         time_block = lax.axis_index("tm").astype(jnp.int32)
         width = activations.shape[1]
-        parts = two_parts(spatial.T)
-        away, kept = project(half[None], parts, signal)
+        parts, gram_halves = two_parts(spatial.T)
+        away, kept = project(half[None], parts, gram_halves, signal)
         summed = kept + lax.ppermute(away, "c", swap)
 
         activations, summed = lax.optimization_barrier((activations, summed))

time: 77.3 us -> 77.2 us (level)
  no operation moved by 1% of the time
where the time goes in v10:
time: 77.2 us; the launch traced here: 76.9 us
  blocking collectives  28 us (36%)
  starting transfers between devices  27.6 us (36%)
  waiting for transfers between devices  9.16 us (12%)
  Pallas kernels  9.1 us (12%)
  local copies, waits for them, and re-layouts  1.34 us (2%)
  other arithmetic  0.93 us (1%)
  between operations  0.79 us (1%)
    all_gather x1, blocking collectives, per_device(): mine = jnp.sum(lax.all_gather(group_sum, 'zh', axis=0), axis=0)  16.9 us
    all_to_all x1, blocking collectives, per_device(): gathered = lax.all_to_all(update, 'y', 0, 0, tiled=True)  11.1 us
    ppermute x1, starting transfers between devices, per_device(): outer = lax.ppermute(outer, line, outside)  10.8 us
    all_to_all x1, waiting for transfers between devices, per_device(): pieces = lax.all_to_all(summed, 'y', 0, 0, tiled=True)  6.69 us
    ppermute x1, starting transfers between devices, per_device(): other = lax.ppermute(gathered, 'c', swap)  6.48 us
    pallas_call x1, Pallas kernels, steps(): pl.pallas_call(body, in_specs=[SMEM] * 3 + [VMEM] * 9, out_specs=VMEM, ou...  4.84 us
    all_to_all x1, starting transfers between devices, per_device(): pieces = lax.all_to_all(summed, 'y', 0, 0, tiled=True)  4.19 us
    ppermute x1, starting transfers between devices, per_device(): inner = lax.ppermute(inner, 'c', swap)  2.9 us
  transfers between devices with their start and end apart: 6, of which 4 were waited for; matrix products, arithmetic and copies ran while one was open for 0% of the time, Pallas kernels for 4%

profile of v10, /device:TPU:7, one launch (start us, length us, event | category | flops | bytes accessed | tf_op | source)
XLA Modules:
  0.0 76.9 jit_solution(339785437352126252)
XLA Ops:
  0.0 0.0 copy-start.1
  0.0 0.0 copy-start.4
  0.0 1.0 %copy-done.4 = f32[256,64]{0,1:T(8,128)S(1)} copy-done((f32[256,64]{0,1:T(8,128)S(1)}, f32[256,64]{0,1:T(8,128)}, u32[]{:S(2)}) %copy-start.4) | copy-done | bytes 65560
  1.0 0.3 shard_map.64
  1.3 0.3 copy-done.1
  1.6 0.0 copy-start
  1.6 0.0 copy-start.2
  1.6 0.5 shard_map.65
  2.1 2.6 %collective-permute-start = (f32[4,272,128]{2,1,0:T(8,128)S(1)}, f32[4,272,128]{2,1,0:T(8,128)S(1)}, u32[]{:S(2)}, u32[]{:S(2)}) collective-permute-start(f32[4,272,128]{2,1,0:T(8,128)S(1)} %get-tuple-element.22), channel_id=1, source_target_pairs={{0,32},{32,0},{1,33},{33,1},{2,34},{34,2},{3,35},{35,3},{4,36},{36... | collective-permute-start | bytes 1671176 | tf_op jit(solution)/shard_map/ppermute | solution.py:478
  4.7 1.6 %collective-permute-done = f32[4,272,128]{2,1,0:T(8,128)S(1)} collective-permute-done((f32[4,272,128]{2,1,0:T(8,128)S(1)}, f32[4,272,128]{2,1,0:T(8,128)S(1)}, u32[]{:S(2)}, u32[]{:S(2)}) %collective-permute-start) | collective-permute-done | bytes 557088 | tf_op jit(solution)/shard_map/ppermute | solution.py:478
  6.2 0.9 %add.11 = f32[4,272,128]{2,1,0:T(8,128)} add(f32[4,272,128]{2,1,0:T(8,128)S(1)} %get-tuple-element.21, f32[4,272,128]{2,1,0:T(8,128)S(1)} %collective-permute-done) | non-fusion elementwise | flops 139264 | bytes 1671168 | tf_op jit(solution)/shard_map/add | solution.py:478
  7.1 4.2 %all-to-all-start = ((f32[4,272,128]{2,1,0:T(8,128)}), f32[4,272,128]{2,1,0:T(8,128)S(1)}, u32[]{:S(2)}, u32[]{:S(2)}) async-start(f32[4,272,128]{2,1,0:T(8,128)} %add.11), calls=%async_computation | async-start | bytes 1114112 | tf_op jit(solution)/shard_map/all_to_all | solution.py:481
  11.3 0.0 copy-done
  11.3 0.0 copy-done.2
  11.3 1.9 %shard_map.66 = (f32[384,128]{1,0:T(8,128)S(1)}, f32[128,128]{1,0:T(8,128)S(1)}, f32[384,128]{1,0:T(8,128)S(1)}, f32[192,128]{1,0:T(8,128)S(1)}) custom-call(s32[1]{0:T(128)} %bitcast.2.place_ref.refs_1_, f32[64,128]{1,0:T(8,128)S(1)} %copy-done.2, f32[64,4096]{1,0:T(8,128)S(1)} %copy-done, f32[64,4096]{1,0:T(8,128)S(1)} %copy-done, f32[64,4096]{1,0:T(8,128)S(1)} %copy-done, ...), custom_call_target="tpu_custom_call" | custom-call | flops 14680064 | bytes 1048576 | tf_op jit(solution)/shard_map/pallas_call | solution.py:272
  13.2 0.0 copy-start.3
  13.2 0.7 collective-permute-start.3
  13.8 6.7 %all-to-all-done = f32[4,272,128]{2,1,0:T(8,128)S(1)} async-done(((f32[4,272,128]{2,1,0:T(8,128)}), f32[4,272,128]{2,1,0:T(8,128)S(1)}, u32[]{:S(2)}, u32[]{:S(2)}) %all-to-all-start) | async-done | bytes 557088 | tf_op jit(solution)/shard_map/all_to_all | solution.py:481
  20.6 16.9 %all-gather = f32[544,128]{1,0:T(8,128)S(1)} all-gather(f32[272,128]{1,0:T(8,128)S(1)} %reduce_sum.18), channel_id=2, replica_groups=mesh['zh'=2,'y'=4,'c'=2,'tm'=32] {'zh'}, dimensions={0}, use_global_device_ids=true | all-gather | bytes 417792 | tf_op jit(solution)/shard_map/all_gather | solution.py:486
  37.6 10.8 %collective-permute-start.2 = (f32[144,128]{1,0:T(8,128)S(1)}, f32[144,128]{1,0:T(8,128)S(1)}, u32[]{:S(2)}, u32[]{:S(2)}) collective-permute-start(f32[144,128]{1,0:T(8,128)S(1)} %get-tuple-element.35), channel_id=1, source_target_pairs={{32,64},{96,128},{160,192},{224,1},{33,65},{97,129},{161,193},{225... | collective-permute-start | bytes 221192 | tf_op jit(solution)/shard_map/ppermute | solution.py:491
  48.4 2.9 %collective-permute-start.1 = (f32[144,128]{1,0:T(8,128)S(1)}, f32[144,128]{1,0:T(8,128)S(1)}, u32[]{:S(2)}, u32[]{:S(2)}) collective-permute-start(f32[144,128]{1,0:T(8,128)S(1)} %get-tuple-element.36), channel_id=1, source_target_pairs={{0,32},{32,0},{1,33},{33,1},{2,34},{34,2},{3,35},{35,3},{4,36},{36... | collective-permute-start | bytes 221192 | tf_op jit(solution)/shard_map/ppermute | solution.py:493
  51.9 0.0 collective-permute-done.3.refs_6_
  51.9 0.0 collective-permute-done.2.refs_5_
  51.9 0.2 collective-permute-done.1.refs_4_
  52.2 0.0 copy-done.3
  52.2 4.8 %shard_map.67 = f32[4,64,512]{2,1,0:T(8,128)S(1)} custom-call(s32[1]{0:T(128)} %bitcast.1.refs_0_, s32[1]{0:T(128)} %bitcast.2.place_ref.refs_1_, f32[1]{0:T(128)S(6)} %copy.9.refs_2_, f32[272,128]{1,0:T(8,128)S(1)} %reduce_sum.19.refs_3_, f32[144,128]{1,0:T(8,128)S(1)} %collective-permute-done.1.refs_4_, f32[144,128]{1,0:T(8,128)S(1)} %collective-permute-done.2.refs_5_, ...), custom_call_target="tpu_custom_call" | custom-call | flops 37748736 | bytes 1048576 | tf_op jit(solution)/shard_map/pallas_call | solution.py:400
  57.0 11.1 %all_to_all.10.chunks_ref = f32[4,64,512]{2,1,0:T(8,128)S(1)} all-to-all(f32[4,64,512]{2,1,0:T(8,128)S(1)} %shard_map.67), channel_id=1, replica_groups=mesh['zh'=2,'y'=4,'c'=2,'tm'=32] {'y'}, dimensions={0} | all-to-all | bytes 1048576 | tf_op jit(solution)/shard_map/all_to_all | solution.py:500
  68.1 6.5 %collective-permute-start.4 = (f32[4,64,512]{2,1,0:T(8,128)S(1)}, f32[4,64,512]{2,1,0:T(8,128)S(1)}, u32[]{:S(2)}, u32[]{:S(2)}) collective-permute-start(f32[4,64,512]{2,1,0:T(8,128)S(1)} %all_to_all.10.chunks_ref), channel_id=1, source_target_pairs={{0,32},{32,0},{1,33},{33,1},{2,34},{34,2},{3,35},{35,3},{4,36},{36... | collective-permute-start | bytes 1572872 | tf_op jit(solution)/shard_map/ppermute | solution.py:501
  74.6 0.8 %shard_map.68.begun_ref = f32[64,4096]{1,0:T(8,128)} custom-call(s32[1]{0:T(128)} %bitcast.half_ref, f32[4,64,512]{2,1,0:T(8,128)S(1)} %all_to_all.10.chunks_ref), custom_call_target="tpu_custom_call" | custom-call | bytes 1048576 | tf_op jit(solution)/shard_map/pallas_call | solution.py:437
  75.4 0.7 collective-permute-done.4.chunks_ref
  76.1 0.8 %shard_map.69 = f32[64,4096]{1,0:T(8,128)} custom-call(s32[1]{0:T(128)} %bitcast.half_ref, f32[4,64,512]{2,1,0:T(8,128)S(1)} %collective-permute-done.4.chunks_ref, f32[64,4096]{1,0:T(8,128)} %shard_map.68.begun_ref), custom_call_target="tpu_custom_call", output_to_operand_aliasing={{}: (2, {})} | custom-call | bytes 1048576 | tf_op jit(solution)/shard_map/pallas_call | solution.py:437
  (5 shorter events, 0.1 us)
Async XLA Ops:
  0.0 1.6 %copy-start.1 = (bf16[256,4096]{1,0:T(8,128)(2,1)S(1)}, bf16[256,4096]{1,0:T(8,128)(2,1)}, u32[]{:S(2)}) copy-start(bf16[256,4096]{1,0:T(8,128)(2,1)} %signal_ref.1) | copy-start | bytes 6291460
  0.0 1.0 %copy-start.4 = (f32[256,64]{0,1:T(8,128)S(1)}, f32[256,64]{0,1:T(8,128)}, u32[]{:S(2)}) copy-start(f32[256,64]{0,1:T(8,128)} %param.7) | copy-start | bytes 196612
  1.6 9.7 %copy-start = (f32[64,4096]{1,0:T(8,128)S(1)}, f32[64,4096]{1,0:T(8,128)}, u32[]{:S(2)}) copy-start(f32[64,4096]{1,0:T(8,128)} %after_ref) | copy-start | bytes 3145732
  1.6 9.7 %copy-start.2 = (f32[64,128]{1,0:T(8,128)S(1)}, f32[64,128]{1,0:T(8,128)}, u32[]{:S(2)}) copy-start(f32[64,128]{1,0:T(8,128)} %refs_10_.1) | copy-start | bytes 98308
  2.1 4.1 %collective-permute-start = (f32[4,272,128]{2,1,0:T(8,128)S(1)}, f32[4,272,128]{2,1,0:T(8,128)S(1)}, u32[]{:S(2)}, u32[]{:S(2)}) collective-permute-start(f32[4,272,128]{2,1,0:T(8,128)S(1)} %get-tuple-element.22), channel_id=1, source_target_pairs={{0,32},{32,0},{1,33},{33,1},{2,34},{34,2},{3,35},{35,3},{4,36},{36... | collective-permute-start | bytes 1671176 | tf_op jit(solution)/shard_map/ppermute | solution.py:478
  7.1 13.4 %all-to-all-start = ((f32[4,272,128]{2,1,0:T(8,128)}), f32[4,272,128]{2,1,0:T(8,128)S(1)}, u32[]{:S(2)}, u32[]{:S(2)}) async-start(f32[4,272,128]{2,1,0:T(8,128)} %add.11), calls=%async_computation | async-start | bytes 1114112 | tf_op jit(solution)/shard_map/all_to_all | solution.py:481
  13.2 39.0 %copy-start.3 = (f32[64]{0:T(128)S(1)}, f32[64]{0:T(128)}, u32[]{:S(2)}) copy-start(f32[64]{0:T(128)} %param.10) | copy-start | bytes 772
  13.2 38.8 %collective-permute-start.3 = (f32[192,128]{1,0:T(8,128)S(1)}, f32[192,128]{1,0:T(8,128)S(1)}, u32[]{:S(2)}, u32[]{:S(2)}) collective-permute-start(f32[192,128]{1,0:T(8,128)S(1)} %get-tuple-element.29), channel_id=1, source_target_pairs={{224,1},{225,2},{226,3},{227,4},{228,5},{229,6},{230,7},{231,264},... | collective-permute-start | bytes 294920 | tf_op jit(solution)/shard_map/ppermute | solution.py:483
  37.6 14.4 %collective-permute-start.2 = (f32[144,128]{1,0:T(8,128)S(1)}, f32[144,128]{1,0:T(8,128)S(1)}, u32[]{:S(2)}, u32[]{:S(2)}) collective-permute-start(f32[144,128]{1,0:T(8,128)S(1)} %get-tuple-element.35), channel_id=1, source_target_pairs={{32,64},{96,128},{160,192},{224,1},{33,65},{97,129},{161,193},{225... | collective-permute-start | bytes 221192 | tf_op jit(solution)/shard_map/ppermute | solution.py:491
  48.4 3.8 %collective-permute-start.1 = (f32[144,128]{1,0:T(8,128)S(1)}, f32[144,128]{1,0:T(8,128)S(1)}, u32[]{:S(2)}, u32[]{:S(2)}) collective-permute-start(f32[144,128]{1,0:T(8,128)S(1)} %get-tuple-element.36), channel_id=1, source_target_pairs={{0,32},{32,0},{1,33},{33,1},{2,34},{34,2},{3,35},{35,3},{4,36},{36... | collective-permute-start | bytes 221192 | tf_op jit(solution)/shard_map/ppermute | solution.py:493
  68.1 8.0 %collective-permute-start.4 = (f32[4,64,512]{2,1,0:T(8,128)S(1)}, f32[4,64,512]{2,1,0:T(8,128)S(1)}, u32[]{:S(2)}, u32[]{:S(2)}) collective-permute-start(f32[4,64,512]{2,1,0:T(8,128)S(1)} %all_to_all.10.chunks_ref), channel_id=1, source_target_pairs={{0,32},{32,0},{1,33},{33,1},{2,34},{34,2},{3,35},{35,3},{4,36},{36... | collective-permute-start | bytes 1572872 | tf_op jit(solution)/shard_map/ppermute | solution.py:501

commit v11 on v10

--- a/solution.py
+++ b/solution.py
@@ -412,10 +412,14 @@
 
 def place_copies(half, chunks_ref, out_ref, sems):
     copies = []
-    for i in range(QUARTER):
-        column = pl.multiple_of((2 * i + half) * CHUNK, CHUNK)
+    rows = ATOMS // 2
+    for i in range(2 * QUARTER):
+        chunk, part = i // 2, pl.ds(i % 2 * rows, rows)
+        column = pl.multiple_of((2 * chunk + half) * CHUNK, CHUNK)
         copies.append(
-            pltpu.make_async_copy(chunks_ref.at[i], out_ref.at[:, pl.ds(column, CHUNK)], sems.at[i])
+            pltpu.make_async_copy(
+                chunks_ref.at[chunk, part], out_ref.at[part, pl.ds(column, CHUNK)], sems.at[i]
+            )
         )
     for copy in copies:
         copy.start()
@@ -439,7 +443,7 @@
         in_specs=[SMEM, ANY] + ([] if first else [ANY]),
         out_specs=ANY,
         out_shape=out_shape,
-        scratch_shapes=[pltpu.SemaphoreType.DMA((QUARTER,))],
+        scratch_shapes=[pltpu.SemaphoreType.DMA((2 * QUARTER,))],
         input_output_aliases={} if first else {2: 0},
         compiler_params=params(4),
         cost_estimate=cost(0, 2**20),

time: 77.2 us -> 77.3 us (level)
  no operation moved by 1% of the time
where the time goes in v11:
time: 77.3 us; the launch traced here: 76.9 us
  blocking collectives  28 us (36%)
  starting transfers between devices  27.6 us (36%)
  Pallas kernels  9.15 us (12%)
  waiting for transfers between devices  9.13 us (12%)
  local copies, waits for them, and re-layouts  1.34 us (2%)
  other arithmetic  0.93 us (1%)
  between operations  0.79 us (1%)
    all_gather x1, blocking collectives, per_device(): mine = jnp.sum(lax.all_gather(group_sum, 'zh', axis=0), axis=0)  16.9 us
    all_to_all x1, blocking collectives, per_device(): gathered = lax.all_to_all(update, 'y', 0, 0, tiled=True)  11.1 us
    ppermute x1, starting transfers between devices, per_device(): outer = lax.ppermute(outer, line, outside)  10.8 us
    all_to_all x1, waiting for transfers between devices, per_device(): pieces = lax.all_to_all(summed, 'y', 0, 0, tiled=True)  6.69 us
    ppermute x1, starting transfers between devices, per_device(): other = lax.ppermute(gathered, 'c', swap)  6.48 us
    pallas_call x1, Pallas kernels, steps(): pl.pallas_call(body, in_specs=[SMEM] * 3 + [VMEM] * 9, out_specs=VMEM, ou...  4.84 us
    all_to_all x1, starting transfers between devices, per_device(): pieces = lax.all_to_all(summed, 'y', 0, 0, tiled=True)  4.19 us
    ppermute x1, starting transfers between devices, per_device(): inner = lax.ppermute(inner, 'c', swap)  2.9 us
  transfers between devices with their start and end apart: 6, of which 4 were waited for; matrix products, arithmetic and copies ran while one was open for 0% of the time, Pallas kernels for 4%

profile of v11, /device:TPU:7, one launch (start us, length us, event | category | flops | bytes accessed | tf_op | source)
XLA Modules:
  0.0 76.9 jit_solution(9534426154118488370)
XLA Ops:
  0.0 0.0 copy-start.1
  0.0 0.0 copy-start.4
  0.0 1.0 %copy-done.4 = f32[256,64]{0,1:T(8,128)S(1)} copy-done((f32[256,64]{0,1:T(8,128)S(1)}, f32[256,64]{0,1:T(8,128)}, u32[]{:S(2)}) %copy-start.4) | copy-done | bytes 65560
  1.0 0.3 shard_map.64
  1.3 0.3 copy-done.1
  1.6 0.0 copy-start
  1.6 0.0 copy-start.2
  1.6 0.5 shard_map.65
  2.1 2.6 %collective-permute-start = (f32[4,272,128]{2,1,0:T(8,128)S(1)}, f32[4,272,128]{2,1,0:T(8,128)S(1)}, u32[]{:S(2)}, u32[]{:S(2)}) collective-permute-start(f32[4,272,128]{2,1,0:T(8,128)S(1)} %get-tuple-element.22), channel_id=1, source_target_pairs={{0,32},{32,0},{1,33},{33,1},{2,34},{34,2},{3,35},{35,3},{4,36},{36... | collective-permute-start | bytes 1671176 | tf_op jit(solution)/shard_map/ppermute | solution.py:482
  4.7 1.6 %collective-permute-done = f32[4,272,128]{2,1,0:T(8,128)S(1)} collective-permute-done((f32[4,272,128]{2,1,0:T(8,128)S(1)}, f32[4,272,128]{2,1,0:T(8,128)S(1)}, u32[]{:S(2)}, u32[]{:S(2)}) %collective-permute-start) | collective-permute-done | bytes 557088 | tf_op jit(solution)/shard_map/ppermute | solution.py:482
  6.2 0.9 %add.11 = f32[4,272,128]{2,1,0:T(8,128)} add(f32[4,272,128]{2,1,0:T(8,128)S(1)} %get-tuple-element.21, f32[4,272,128]{2,1,0:T(8,128)S(1)} %collective-permute-done) | non-fusion elementwise | flops 139264 | bytes 1671168 | tf_op jit(solution)/shard_map/add | solution.py:482
  7.1 4.2 %all-to-all-start = ((f32[4,272,128]{2,1,0:T(8,128)}), f32[4,272,128]{2,1,0:T(8,128)S(1)}, u32[]{:S(2)}, u32[]{:S(2)}) async-start(f32[4,272,128]{2,1,0:T(8,128)} %add.11), calls=%async_computation | async-start | bytes 1114112 | tf_op jit(solution)/shard_map/all_to_all | solution.py:485
  11.3 0.0 copy-done
  11.3 0.0 copy-done.2
  11.3 1.9 %shard_map.66 = (f32[384,128]{1,0:T(8,128)S(1)}, f32[128,128]{1,0:T(8,128)S(1)}, f32[384,128]{1,0:T(8,128)S(1)}, f32[192,128]{1,0:T(8,128)S(1)}) custom-call(s32[1]{0:T(128)} %bitcast.2.place_ref.refs_1_, f32[64,128]{1,0:T(8,128)S(1)} %copy-done.2, f32[64,4096]{1,0:T(8,128)S(1)} %copy-done, f32[64,4096]{1,0:T(8,128)S(1)} %copy-done, f32[64,4096]{1,0:T(8,128)S(1)} %copy-done, ...), custom_call_target="tpu_custom_call" | custom-call | flops 14680064 | bytes 1048576 | tf_op jit(solution)/shard_map/pallas_call | solution.py:272
  13.2 0.0 copy-start.3
  13.2 0.7 collective-permute-start.3
  13.8 6.7 %all-to-all-done = f32[4,272,128]{2,1,0:T(8,128)S(1)} async-done(((f32[4,272,128]{2,1,0:T(8,128)}), f32[4,272,128]{2,1,0:T(8,128)S(1)}, u32[]{:S(2)}, u32[]{:S(2)}) %all-to-all-start) | async-done | bytes 557088 | tf_op jit(solution)/shard_map/all_to_all | solution.py:485
  20.6 16.9 %all-gather = f32[544,128]{1,0:T(8,128)S(1)} all-gather(f32[272,128]{1,0:T(8,128)S(1)} %reduce_sum.18), channel_id=2, replica_groups=mesh['zh'=2,'y'=4,'c'=2,'tm'=32] {'zh'}, dimensions={0}, use_global_device_ids=true | all-gather | bytes 417792 | tf_op jit(solution)/shard_map/all_gather | solution.py:490
  37.6 10.8 %collective-permute-start.2 = (f32[144,128]{1,0:T(8,128)S(1)}, f32[144,128]{1,0:T(8,128)S(1)}, u32[]{:S(2)}, u32[]{:S(2)}) collective-permute-start(f32[144,128]{1,0:T(8,128)S(1)} %get-tuple-element.35), channel_id=1, source_target_pairs={{32,64},{96,128},{160,192},{224,1},{33,65},{97,129},{161,193},{225... | collective-permute-start | bytes 221192 | tf_op jit(solution)/shard_map/ppermute | solution.py:495
  48.4 2.9 %collective-permute-start.1 = (f32[144,128]{1,0:T(8,128)S(1)}, f32[144,128]{1,0:T(8,128)S(1)}, u32[]{:S(2)}, u32[]{:S(2)}) collective-permute-start(f32[144,128]{1,0:T(8,128)S(1)} %get-tuple-element.36), channel_id=1, source_target_pairs={{0,32},{32,0},{1,33},{33,1},{2,34},{34,2},{3,35},{35,3},{4,36},{36... | collective-permute-start | bytes 221192 | tf_op jit(solution)/shard_map/ppermute | solution.py:497
  51.9 0.0 collective-permute-done.3.refs_6_
  51.9 0.0 collective-permute-done.2.refs_5_
  51.9 0.2 collective-permute-done.1.refs_4_
  52.2 0.0 copy-done.3
  52.2 4.8 %shard_map.67 = f32[4,64,512]{2,1,0:T(8,128)S(1)} custom-call(s32[1]{0:T(128)} %bitcast.1.refs_0_, s32[1]{0:T(128)} %bitcast.2.place_ref.refs_1_, f32[1]{0:T(128)S(6)} %copy.9.refs_2_, f32[272,128]{1,0:T(8,128)S(1)} %reduce_sum.19.refs_3_, f32[144,128]{1,0:T(8,128)S(1)} %collective-permute-done.1.refs_4_, f32[144,128]{1,0:T(8,128)S(1)} %collective-permute-done.2.refs_5_, ...), custom_call_target="tpu_custom_call" | custom-call | flops 37748736 | bytes 1048576 | tf_op jit(solution)/shard_map/pallas_call | solution.py:400
  57.0 11.1 %all_to_all.10.chunks_ref = f32[4,64,512]{2,1,0:T(8,128)S(1)} all-to-all(f32[4,64,512]{2,1,0:T(8,128)S(1)} %shard_map.67), channel_id=1, replica_groups=mesh['zh'=2,'y'=4,'c'=2,'tm'=32] {'y'}, dimensions={0} | all-to-all | bytes 1048576 | tf_op jit(solution)/shard_map/all_to_all | solution.py:504
  68.1 6.5 %collective-permute-start.4 = (f32[4,64,512]{2,1,0:T(8,128)S(1)}, f32[4,64,512]{2,1,0:T(8,128)S(1)}, u32[]{:S(2)}, u32[]{:S(2)}) collective-permute-start(f32[4,64,512]{2,1,0:T(8,128)S(1)} %all_to_all.10.chunks_ref), channel_id=1, source_target_pairs={{0,32},{32,0},{1,33},{33,1},{2,34},{34,2},{3,35},{35,3},{4,36},{36... | collective-permute-start | bytes 1572872 | tf_op jit(solution)/shard_map/ppermute | solution.py:505
  74.6 0.9 %shard_map.68.begun_ref = f32[64,4096]{1,0:T(8,128)} custom-call(s32[1]{0:T(128)} %bitcast.half_ref, f32[4,64,512]{2,1,0:T(8,128)S(1)} %all_to_all.10.chunks_ref), custom_call_target="tpu_custom_call" | custom-call | bytes 1048576 | tf_op jit(solution)/shard_map/pallas_call | solution.py:441
  75.4 0.7 collective-permute-done.4.chunks_ref
  76.1 0.8 %shard_map.69 = f32[64,4096]{1,0:T(8,128)} custom-call(s32[1]{0:T(128)} %bitcast.half_ref, f32[4,64,512]{2,1,0:T(8,128)S(1)} %collective-permute-done.4.chunks_ref, f32[64,4096]{1,0:T(8,128)} %shard_map.68.begun_ref), custom_call_target="tpu_custom_call", output_to_operand_aliasing={{}: (2, {})} | custom-call | bytes 1048576 | tf_op jit(solution)/shard_map/pallas_call | solution.py:441
  (5 shorter events, 0.1 us)
Async XLA Ops:
  0.0 1.6 %copy-start.1 = (bf16[256,4096]{1,0:T(8,128)(2,1)S(1)}, bf16[256,4096]{1,0:T(8,128)(2,1)}, u32[]{:S(2)}) copy-start(bf16[256,4096]{1,0:T(8,128)(2,1)} %signal_ref.1) | copy-start | bytes 6291460
  0.0 1.0 %copy-start.4 = (f32[256,64]{0,1:T(8,128)S(1)}, f32[256,64]{0,1:T(8,128)}, u32[]{:S(2)}) copy-start(f32[256,64]{0,1:T(8,128)} %param.7) | copy-start | bytes 196612
  1.6 9.7 %copy-start = (f32[64,4096]{1,0:T(8,128)S(1)}, f32[64,4096]{1,0:T(8,128)}, u32[]{:S(2)}) copy-start(f32[64,4096]{1,0:T(8,128)} %after_ref) | copy-start | bytes 3145732
  1.6 9.7 %copy-start.2 = (f32[64,128]{1,0:T(8,128)S(1)}, f32[64,128]{1,0:T(8,128)}, u32[]{:S(2)}) copy-start(f32[64,128]{1,0:T(8,128)} %refs_10_.1) | copy-start | bytes 98308
  2.1 4.1 %collective-permute-start = (f32[4,272,128]{2,1,0:T(8,128)S(1)}, f32[4,272,128]{2,1,0:T(8,128)S(1)}, u32[]{:S(2)}, u32[]{:S(2)}) collective-permute-start(f32[4,272,128]{2,1,0:T(8,128)S(1)} %get-tuple-element.22), channel_id=1, source_target_pairs={{0,32},{32,0},{1,33},{33,1},{2,34},{34,2},{3,35},{35,3},{4,36},{36... | collective-permute-start | bytes 1671176 | tf_op jit(solution)/shard_map/ppermute | solution.py:482
  7.1 13.4 %all-to-all-start = ((f32[4,272,128]{2,1,0:T(8,128)}), f32[4,272,128]{2,1,0:T(8,128)S(1)}, u32[]{:S(2)}, u32[]{:S(2)}) async-start(f32[4,272,128]{2,1,0:T(8,128)} %add.11), calls=%async_computation | async-start | bytes 1114112 | tf_op jit(solution)/shard_map/all_to_all | solution.py:485
  13.2 39.0 %copy-start.3 = (f32[64]{0:T(128)S(1)}, f32[64]{0:T(128)}, u32[]{:S(2)}) copy-start(f32[64]{0:T(128)} %param.10) | copy-start | bytes 772
  13.2 38.8 %collective-permute-start.3 = (f32[192,128]{1,0:T(8,128)S(1)}, f32[192,128]{1,0:T(8,128)S(1)}, u32[]{:S(2)}, u32[]{:S(2)}) collective-permute-start(f32[192,128]{1,0:T(8,128)S(1)} %get-tuple-element.29), channel_id=1, source_target_pairs={{224,1},{225,2},{226,3},{227,4},{228,5},{229,6},{230,7},{231,264},... | collective-permute-start | bytes 294920 | tf_op jit(solution)/shard_map/ppermute | solution.py:487
  37.6 14.4 %collective-permute-start.2 = (f32[144,128]{1,0:T(8,128)S(1)}, f32[144,128]{1,0:T(8,128)S(1)}, u32[]{:S(2)}, u32[]{:S(2)}) collective-permute-start(f32[144,128]{1,0:T(8,128)S(1)} %get-tuple-element.35), channel_id=1, source_target_pairs={{32,64},{96,128},{160,192},{224,1},{33,65},{97,129},{161,193},{225... | collective-permute-start | bytes 221192 | tf_op jit(solution)/shard_map/ppermute | solution.py:495
  48.4 3.8 %collective-permute-start.1 = (f32[144,128]{1,0:T(8,128)S(1)}, f32[144,128]{1,0:T(8,128)S(1)}, u32[]{:S(2)}, u32[]{:S(2)}) collective-permute-start(f32[144,128]{1,0:T(8,128)S(1)} %get-tuple-element.36), channel_id=1, source_target_pairs={{0,32},{32,0},{1,33},{33,1},{2,34},{34,2},{3,35},{35,3},{4,36},{36... | collective-permute-start | bytes 221192 | tf_op jit(solution)/shard_map/ppermute | solution.py:497
  68.1 8.0 %collective-permute-start.4 = (f32[4,64,512]{2,1,0:T(8,128)S(1)}, f32[4,64,512]{2,1,0:T(8,128)S(1)}, u32[]{:S(2)}, u32[]{:S(2)}) collective-permute-start(f32[4,64,512]{2,1,0:T(8,128)S(1)} %all_to_all.10.chunks_ref), channel_id=1, source_target_pairs={{0,32},{32,0},{1,33},{33,1},{2,34},{34,2},{3,35},{35,3},{4,36},{36... | collective-permute-start | bytes 1572872 | tf_op jit(solution)/shard_map/ppermute | solution.py:505
